TPU v7x, 32 devices: a whole 2x2x4 slice. The times are simulated.
32 devices in a mesh: slab: 8 (over y, x, core), shots: 4 (over z).
Axes of the slice: x: 2, y: 2, z: 4, core: 2. Of those that a mesh axis runs over, the one named last changes fastest.
Arguments:
- src_prev: float32 [8, 64, 64, 128], P('shots', 'slab'), may hold values from -6 to 6
- src_cur: float32 [8, 64, 64, 128], P('shots', 'slab'), may hold values from -6 to 6
- rcv_prev: float32 [8, 64, 64, 128], P('shots', 'slab'), may hold values from -6 to 6
- rcv_cur: float32 [8, 64, 64, 128], P('shots', 'slab'), may hold values from -6 to 6
- velocity: float32 [64, 64, 128], P('slab'), may hold values from 0.05 to 0.18
- wavelet: float32 [2, 8], P(None, 'shots'), may hold values from -6 to 6
- residual_traces: float32 [2, 8, 256], P(None, 'shots'), may hold values from -6 to 6
- source_depth: int32 [8], P('shots'), may hold values from 0 to 63
- source_y: int32 [8], P('shots'), may hold values from 21 to 42
- source_x: int32 [8], P('shots'), may hold values from 42 to 85
- half_y: int32 [8], P('shots'), may hold values from 10 to 21
- half_x: int32 [8], P('shots'), may hold values from 21 to 42
- receiver_cell: int32 [8, 256], P('shots'), may hold values from 0 to 524287
Outputs:
- src_last: float32 [8, 64, 64, 128], P('shots', 'slab')
- rcv_last: float32 [8, 64, 64, 128], P('shots', 'slab')
- image: float32 [64, 64, 128], P('slab')
All inputs are finite; a program needn't handle non-finite values.
Results may differ from a plain program's by a relative error of at most 0.0003.
Values sent between devices are 32-bit elements; how exact they have to be, the bound alone decides.
No kernel may reach another device: no remote copies, remote signals or barrier semaphores. Data moves between devices by JAX's collectives and lax.ppermute only.
A program may use at most 64 MiB of HBM per device.

v0:
```python
import jax
import jax.numpy as jnp
from jax import lax
from jax.sharding import PartitionSpec as P

STEPS = 2


COEF = (-205.0 / 72.0, 8.0 / 5.0, -1.0 / 5.0, 8.0 / 315.0, -1.0 / 560.0)


def extended(block, sides, width):
    for axis, dim in sides:
        count = lax.axis_size(axis)
        forward = [(i, i + 1) for i in range(count - 1)]
        backward = [(target, source) for source, target in forward]
        low = lax.ppermute(
            lax.slice_in_dim(block, block.shape[dim] - width, None, axis=dim), axis, forward
        )
        high = lax.ppermute(lax.slice_in_dim(block, 0, width, axis=dim), axis, backward)
        block = jnp.concatenate([low, block, high], axis=dim)
    return block


def laplace(padded):
    axis_z = padded.ndim - 3
    length = padded.shape[axis_z] - 8
    center = lax.slice_in_dim(padded, 4, 4 + length, axis=axis_z)
    total = 3.0 * COEF[0] * center
    for shift_k in range(1, 5):
        upper = lax.slice_in_dim(padded, 4 + shift_k, 4 + shift_k + length, axis=axis_z)
        lower = lax.slice_in_dim(padded, 4 - shift_k, 4 - shift_k + length, axis=axis_z)
        total = total + COEF[shift_k] * (upper + lower)
    widths = [(0, 0)] * (center.ndim - 2) + [(4, 4), (4, 4)]
    plane = jnp.pad(center, widths)
    rows_y = center.shape[-2]
    cols_x = center.shape[-1]
    for shift_k in range(1, 5):
        side_y = (
            plane[..., 4 + shift_k : 4 + shift_k + rows_y, 4 : 4 + cols_x]
            + plane[..., 4 - shift_k : 4 - shift_k + rows_y, 4 : 4 + cols_x]
        )
        side_x = (
            plane[..., 4 : 4 + rows_y, 4 + shift_k : 4 + shift_k + cols_x]
            + plane[..., 4 : 4 + rows_y, 4 - shift_k : 4 - shift_k + cols_x]
        )
        total = total + COEF[shift_k] * (side_y + side_x)
    return total


def band_mask(source_y, source_x, half_y, half_x, rows_y, cols_x):
    grid_y = jnp.arange(rows_y, dtype=jnp.int32)
    grid_x = jnp.arange(cols_x, dtype=jnp.int32)
    inside_y = jnp.abs(grid_y[None, :, None] - source_y[:, None, None]) <= half_y[:, None, None]
    inside_x = jnp.abs(grid_x[None, None, :] - source_x[:, None, None]) <= half_x[:, None, None]
    return (inside_y & inside_x).astype(jnp.float32)


def inject(cells, values, begin, length, rows_y, cols_x):
    plane = rows_y * cols_x
    depth = cells // plane
    rest = cells - depth * plane
    local = depth - begin
    valid = (local >= 0) & (local < length)
    flat = jnp.where(valid, local * plane + rest, 0)
    amounts = jnp.where(valid, values, jnp.zeros_like(values))
    count = cells.shape[0]
    rows = jnp.broadcast_to(jnp.arange(count, dtype=jnp.int32)[:, None], flat.shape)
    field = jnp.zeros((count, length * plane), jnp.float32).at[rows, flat].add(amounts)
    return field.reshape(count, length, rows_y, cols_x)


def per_device(
    src_prev,
    src_cur,
    rcv_prev,
    rcv_cur,
    velocity,
    wavelet,
    residual_traces,
    source_depth,
    source_y,
    source_x,
    half_y,
    half_x,
    receiver_cell,
):
    shot_count, depth, rows_y, cols_x = src_cur.shape
    start = lax.axis_index("slab") * depth
    mask = band_mask(source_y, source_x, half_y, half_x, rows_y, cols_x)[:, None]
    scells = (source_depth * rows_y * cols_x + source_y * cols_x + source_x)[:, None]
    terms = []
    up, u, vp, v = (src_prev, src_cur, rcv_prev, rcv_cur)
    for step in range(STEPS):
        stacked = jnp.stack([u, v])
        padded = extended(stacked, (("slab", 2),), 4)
        lap = laplace(padded)
        sdelta = inject(scells, wavelet[step][:, None], start, depth, rows_y, cols_x)
        rdelta = inject(receiver_cell, residual_traces[step], start, depth, rows_y, cols_x)
        sdelta, rdelta = (sdelta, rdelta)
        unew = mask * (2.0 * u - up + velocity * lap[0] + sdelta)
        vnew = mask * (2.0 * v - vp + velocity * lap[1] + rdelta)
        terms.append(jnp.sum((unew - 2.0 * u + up) * vnew, axis=0))
        up, u, vp, v = (u, unew, v, vnew)
    src_last, rcv_last = (u, v)
    local_sum = terms[0]
    for extra in terms[1:]:
        local_sum = local_sum + extra
    image = lax.psum(local_sum, "shots")
    return (src_last, rcv_last, image)


def solution(mesh):
    return jax.shard_map(
        per_device,
        mesh=mesh,
        in_specs=(
            P("shots", "slab", None, None),
            P("shots", "slab", None, None),
            P("shots", "slab", None, None),
            P("shots", "slab", None, None),
            P("slab", None, None),
            P(None, "shots"),
            P(None, "shots", None),
            P("shots"),
            P("shots"),
            P("shots"),
            P("shots"),
            P("shots"),
            P("shots", None),
        ),
        out_specs=(
            P("shots", "slab", None, None),
            P("shots", "slab", None, None),
            P("slab", None, None),
        ),
        check_vma=False,
    )
```

profile of v0, /device:TPU:0, one launch (start us, length us, event | category | flops | bytes accessed | tf_op | source)
XLA Modules:
  0.0 131.4 jit_solution(1499858588321943835)
XLA Ops:
  7.2 0.0 copy-start.7
  7.2 0.0 copy-start.6
  7.2 0.0 copy-start.8
  7.2 0.0 copy-start.9
  7.2 0.0 copy-start.11
  7.2 0.0 copy-start.10
  7.2 0.0 all-reduce.4.cloned.1.call-start
  7.3 2.3 %fusion.58 = (f32[2,2,4,64,128]{4,3,2,1,0:T(8,128)}, f32[2,2,4,64,128]{4,3,2,1,0:T(8,128)}) fusion(f32[1,2,8,64,128]{4,3,2,1,0:T(8,128)} %bitcast.91, f32[1,2,8,64,128]{4,3,2,1,0:T(8,128)} %bitcast.94), kind=kLoop, calls=%fused_computation.116 | loop fusion | flops 262144 | bytes 2097152 | tf_op jit(solution)/shard_map/stack | solution.py:95
  9.5 1.3 collective-permute-start
  10.8 3.1 %collective-permute-start.1 = (f32[2,2,4,64,128]{4,3,2,1,0:T(8,128)}, f32[2,2,4,64,128]{4,3,2,1,0:T(8,128)S(1)}, u32[]{:S(2)}, u32[]{:S(2)}) collective-permute-start(f32[2,2,4,64,128]{4,3,2,1,0:T(8,128)} %get-tuple-element.21), channel_id=1, source_target_pairs={{0,4},{4,8},{8,12},{12,16},{16,20},{20,24},{24,28},{1,5},{5,9},{9,... | collective-permute-start | bytes 1572872 | tf_op jit(solution)/shard_map/ppermute | solution.py:17
  13.9 0.0 copy-done.7
  13.9 0.0 copy-done.6
  14.0 0.0 copy-done.8
  14.0 0.0 copy-done.9
  14.0 0.0 copy-done.11
  14.0 0.0 copy-done.10
  14.1 0.1 copy.17
  14.2 0.2 fusion.83
  14.4 0.1 broadcast.180.clone.1
  14.5 0.6 scatter_fusion
  15.2 0.1 broadcast.180.clone
  15.4 0.0 copy-start.12
  15.4 0.0 copy-start
  15.4 0.0 copy-start.1
  15.4 24.6 %scatter_fusion.1 = f32[2,65536]{1,0:T(2,128)S(1)} fusion(f32[2,65536]{1,0:T(2,128)S(1)} %broadcast.180.clone, s32[512]{0:T(512)S(1)} %bitcast.87, f32[512]{0:T(512)S(1)} %bitcast.111), kind=kCustom, calls=%fused_computation.1 | custom fusion | flops 512 | bytes 10240 | tf_op jit(solution)/shard_map/scatter-add | solution.py:69
  40.0 0.0 copy-start.13
  40.1 0.0 copy-done.12
  40.1 0.1 abs_compare_fusion
  40.2 0.0 copy-done
  40.2 0.0 copy-done.1
  40.2 0.1 pad_maximum_fusion.2
  40.3 0.4 copy-done.13
  40.7 0.1 abs_compare_fusion.1
  40.8 0.1 and_convert_fusion
  40.9 0.0 collective-permute-done
  40.9 0.0 collective-permute-done.1
  40.9 0.4 pad_maximum_fusion
  41.3 0.0 copy-start.2
  41.3 0.0 copy-start.4
  41.3 0.0 copy-start.5
  41.3 2.5 %fusion.6 = f32[2,2,8,64,128]{4,3,2,1,0:T(8,128)S(1)} fusion(f32[2,2,8,64,128]{4,3,2,1,0:T(8,128)S(1)} %pad_maximum_fusion.2, f32[2,2,12,64,128]{4,3,2,1,0:T(8,128)S(1)} %get-tuple-element.19, f32[2,2,12,64,128]{4,3,2,1,0:T(8,128)S(1)} %get-tuple-element.18), kind=kLoop, calls=%fused_computation.56 | loop fusion | flops 8650752 | bytes 10485760 | tf_op jit(solution)/shard_map/add | solution.py:47
  43.8 0.0 copy-done.2
  43.8 0.0 copy-done.4
  43.8 0.0 copy-done.5
  43.8 0.5 fusion.71
  44.3 1.0 fusion.56
  45.4 1.3 collective-permute-start.2
  46.6 5.9 %collective-permute-start.3 = (f32[2,2,4,64,128]{4,3,2,1,0:T(8,128)}, f32[2,2,4,64,128]{4,3,2,1,0:T(8,128)}, u32[]{:S(2)}, u32[]{:S(2)}) collective-permute-start(f32[2,2,4,64,128]{4,3,2,1,0:T(8,128)} %get-tuple-element.17), channel_id=1, source_target_pairs={{0,4},{4,8},{8,12},{12,16},{16,20},{20,24},{24,28},{1,5},{5,9},{9,... | collective-permute-start | bytes 1572872 | tf_op jit(solution)/shard_map/ppermute | solution.py:17
  52.6 0.1 broadcast.180.clone.3
  52.7 0.6 scatter_fusion.2
  53.4 0.1 broadcast.180.clone.2
  53.5 24.6 %scatter_fusion.3 = f32[2,65536]{1,0:T(2,128)S(1)} fusion(f32[2,65536]{1,0:T(2,128)S(1)} %broadcast.180.clone.2, s32[512]{0:T(512)S(1)} %bitcast.88, f32[512]{0:T(512)S(1)} %bitcast.110), kind=kCustom, calls=%fused_computation.3 | custom fusion | flops 512 | bytes 10240 | tf_op jit(solution)/shard_map/scatter-add | solution.py:69
  78.2 0.1 pad_maximum_fusion.3
  78.3 0.0 collective-permute-done.2
  78.3 0.0 collective-permute-done.3
  78.3 1.6 %pad_maximum_fusion.1 = (f32[2,2,12,64,128]{4,3,2,1,0:T(8,128)S(1)}, f32[2,2,12,64,128]{4,3,2,1,0:T(8,128)S(1)}) fusion(f32[2,2,4,64,128]{4,3,2,1,0:T(8,128)} %collective-permute-done.2, f32[1,2,8,64,128]{4,3,2,1,0:T(8,128)S(1)} %bitcast.99, f32[1,2,8,64,128]{4,3,2,1,0:T(8,128)S(1)} %bitcast.102, f32[2,2,4,64,128]{4,3,2,1,0:T(8,128)} %collective-permute-done.3), kind=kLoop, calls=%fused_computation.38 | loop fusion | flops 1572864 | bytes 5242880 | tf_op jit(solution)/shard_map/concatenate | solution.py:21
  80.0 0.0 copy-start.3
  80.0 2.5 %fusion.26 = f32[2,2,8,64,128]{4,3,2,1,0:T(8,128)S(1)} fusion(f32[2,2,8,64,128]{4,3,2,1,0:T(8,128)S(1)} %pad_maximum_fusion.3, f32[2,2,12,64,128]{4,3,2,1,0:T(8,128)S(1)} %get-tuple-element.15, f32[2,2,12,64,128]{4,3,2,1,0:T(8,128)S(1)} %get-tuple-element.14), kind=kLoop, calls=%fused_computation.76 | loop fusion | flops 8650752 | bytes 10485760 | tf_op jit(solution)/shard_map/add | solution.py:47
  82.4 0.0 copy-done.3
  82.4 1.6 %multiply_reduce_fusion = (f32[8,64,128]{2,1,0:T(8,128)S(1)}, f32[8,64,128]{2,1,0:T(8,128)S(1)}, f32[2,8,64,128]{3,2,1,0:T(8,128)}, f32[2,8,64,128]{3,2,1,0:T(8,128)}) fusion(f32[2,8,64,128]{3,2,1,0:T(8,128)S(1)} %copy-done, f32[2,8,64,128]{3,2,1,0:T(8,128)S(1)} %get-tuple-element.13, f32[2,8,64,128]{3,2,1,0:T(8,128)S(1)} %get-tuple-element.12, ...), kind=kLoop, calls=%fused_computation.138 | loop fusion | flops 2621440 | bytes 6619136 | tf_op jit(solution)/shard_map/reduce_sum | solution.py:103
  84.1 0.7 add.287
  84.8 0.0 all-reduce.4.cloned.1.call-update
  84.8 38.1 %all-reduce.4.cloned.1.call-done = f32[8,64,128]{2,1,0:T(8,128)} async-done(((f32[8,64,128]{2,1,0:T(8,128)}), f32[8,64,128]{2,1,0:T(8,128)}) %all-reduce.4.cloned.1.call-update) | async-done | bytes 262160 | tf_op jit(solution)/shard_map/psum | solution.py:109
  122.9 1.7 %copy.30 = f32[8,64,128]{2,1,0:T(8,128)} copy(f32[8,64,128]{2,1,0:T(8,128)} %all-reduce.4.cloned.1.call-done) | data formatting | bytes 524288
  (15 shorter events, 0.2 us)
Async XLA Ops:
  7.2 6.7 %copy-start.7 = (f32[2,2,256]{2,1,0:T(2,128)S(1)}, f32[2,2,256]{2,1,0:T(2,128)}, u32[]{:S(2)}) copy-start(f32[2,2,256]{2,1,0:T(2,128)} %param.19) | copy-start | bytes 12292
  7.2 6.7 %copy-start.6 = (s32[2,256]{1,0:T(2,128)S(1)}, s32[2,256]{1,0:T(2,128)}, u32[]{:S(2)}) copy-start(s32[2,256]{1,0:T(2,128)} %param.25) | copy-start | bytes 6148
  7.2 6.8 %copy-start.8 = (f32[2,2]{1,0:T(2,128)S(1)}, f32[2,2]{1,0:T(2,128)}, u32[]{:S(2)}) copy-start(f32[2,2]{1,0:T(2,128)} %param.18) | copy-start | bytes 52
  7.2 6.8 %copy-start.9 = (s32[2]{0:T(128)S(1)}, s32[2]{0:T(128)}, u32[]{:S(2)}) copy-start(s32[2]{0:T(128)} %param.20) | copy-start | bytes 28
  7.2 6.8 %copy-start.11 = (s32[2]{0:T(128)S(1)}, s32[2]{0:T(128)}, u32[]{:S(2)}) copy-start(s32[2]{0:T(128)} %param.21) | copy-start | bytes 28
  7.2 6.8 %copy-start.10 = (s32[2]{0:T(128)S(1)}, s32[2]{0:T(128)}, u32[]{:S(2)}) copy-start(s32[2]{0:T(128)} %param.22) | copy-start | bytes 28
  7.2 115.7 %all-reduce.4.cloned.1.call-start = ((), (), s32[]{:S(2)}) async-start(), calls=%async_computation | async-start | bytes 524288 | tf_op jit(solution)/shard_map/psum | solution.py:109
  9.5 31.3 %collective-permute-start = (f32[2,2,4,64,128]{4,3,2,1,0:T(8,128)}, f32[2,2,4,64,128]{4,3,2,1,0:T(8,128)S(1)}, u32[]{:S(2)}, u32[]{:S(2)}) collective-permute-start(f32[2,2,4,64,128]{4,3,2,1,0:T(8,128)} %get-tuple-element.20), channel_id=1, source_target_pairs={{4,0},{8,4},{12,8},{16,12},{20,16},{24,20},{28,24},{5,1},{9,5},{13... | collective-permute-start | bytes 1572872 | tf_op jit(solution)/shard_map/ppermute | solution.py:20
  10.8 30.1 %collective-permute-start.1 = (f32[2,2,4,64,128]{4,3,2,1,0:T(8,128)}, f32[2,2,4,64,128]{4,3,2,1,0:T(8,128)S(1)}, u32[]{:S(2)}, u32[]{:S(2)}) collective-permute-start(f32[2,2,4,64,128]{4,3,2,1,0:T(8,128)} %get-tuple-element.21), channel_id=1, source_target_pairs={{0,4},{4,8},{8,12},{12,16},{16,20},{20,24},{24,28},{1,5},{5,9},{9,... | collective-permute-start | bytes 1572872 | tf_op jit(solution)/shard_map/ppermute | solution.py:17
  15.4 24.7 %copy-start.12 = (s32[2]{0:T(128)S(1)}, s32[2]{0:T(128)}, u32[]{:S(2)}) copy-start(s32[2]{0:T(128)} %param.24) | copy-start | bytes 28
  15.4 24.8 %copy-start = (f32[2,8,64,128]{3,2,1,0:T(8,128)S(1)}, f32[2,8,64,128]{3,2,1,0:T(8,128)}, u32[]{:S(2)}) copy-start(f32[2,8,64,128]{3,2,1,0:T(8,128)} %param.14) | copy-start | bytes 1572868
  15.4 24.8 %copy-start.1 = (f32[2,8,64,128]{3,2,1,0:T(8,128)S(1)}, f32[2,8,64,128]{3,2,1,0:T(8,128)}, u32[]{:S(2)}) copy-start(f32[2,8,64,128]{3,2,1,0:T(8,128)} %param.16) | copy-start | bytes 1572868
  40.0 0.7 copy-start.13
  41.3 2.5 %copy-start.2 = (f32[2,8,64,128]{3,2,1,0:T(8,128)S(1)}, f32[2,8,64,128]{3,2,1,0:T(8,128)}, u32[]{:S(2)}) copy-start(f32[2,8,64,128]{3,2,1,0:T(8,128)} %param.13) | copy-start | bytes 1572868
  41.3 2.5 %copy-start.4 = (f32[8,64,128]{2,1,0:T(8,128)S(1)}, f32[8,64,128]{2,1,0:T(8,128)}, u32[]{:S(2)}) copy-start(f32[8,64,128]{2,1,0:T(8,128)} %param.17) | copy-start | bytes 786436
  41.3 2.5 %copy-start.5 = (f32[2,8,64,128]{3,2,1,0:T(8,128)S(1)}, f32[2,8,64,128]{3,2,1,0:T(8,128)}, u32[]{:S(2)}) copy-start(f32[2,8,64,128]{3,2,1,0:T(8,128)} %param.15) | copy-start | bytes 1572868
  45.4 33.0 %collective-permute-start.2 = (f32[2,2,4,64,128]{4,3,2,1,0:T(8,128)}, f32[2,2,4,64,128]{4,3,2,1,0:T(8,128)}, u32[]{:S(2)}, u32[]{:S(2)}) collective-permute-start(f32[2,2,4,64,128]{4,3,2,1,0:T(8,128)} %get-tuple-element.16), channel_id=1, source_target_pairs={{4,0},{8,4},{12,8},{16,12},{20,16},{24,20},{28,24},{5,1},{9,5},{13... | collective-permute-start | bytes 1572872 | tf_op jit(solution)/shard_map/ppermute | solution.py:20
  46.6 31.7 %collective-permute-start.3 = (f32[2,2,4,64,128]{4,3,2,1,0:T(8,128)}, f32[2,2,4,64,128]{4,3,2,1,0:T(8,128)}, u32[]{:S(2)}, u32[]{:S(2)}) collective-permute-start(f32[2,2,4,64,128]{4,3,2,1,0:T(8,128)} %get-tuple-element.17), channel_id=1, source_target_pairs={{0,4},{4,8},{8,12},{12,16},{16,20},{20,24},{24,28},{1,5},{5,9},{9,... | collective-permute-start | bytes 1572872 | tf_op jit(solution)/shard_map/ppermute | solution.py:17
  80.0 2.5 %copy-start.3 = (f32[2,8,64,128]{3,2,1,0:T(8,128)S(1)}, f32[2,8,64,128]{3,2,1,0:T(8,128)}, u32[]{:S(2)}) copy-start(f32[2,8,64,128]{3,2,1,0:T(8,128)} %param.13) | copy-start | bytes 1572868
Sparse Core Ops, SparseCore 0:
  84.9 37.9 all-reduce.3
where the time goes:
time: 132 us; the launch traced here: 131 us
  other arithmetic  64.3 us (49%)
  waiting for transfers between devices  38.1 us (29%)
  between operations  14.5 us (11%)
  starting transfers between devices  11.6 us (9%)
  local copies, waits for them, and re-layouts  2.97 us (2%)
    scatter-add x4, other arithmetic, inject(): jnp.zeros((count, length * plane), jnp.float32).at[rows, flat].add(amounts)  50.6 us
    psum x1, waiting for transfers between devices, per_device(): image = lax.psum(local_sum, 'shots')  38.1 us
    ppermute x2, starting transfers between devices, extended(): lax.ppermute(lax.slice_in_dim(block, block.shape[dim] - width, None, axis...  8.97 us
    add x2, other arithmetic, laplace(): total = total + COEF[shift_k] * (side_y + side_x)  4.91 us
    another operation x4, other arithmetic, per_device(): stacked = jnp.stack([u, v])  3.46 us
  transfers between devices with their start and end apart: 5, of which 1 were waited for; matrix products, arithmetic and copies ran while one was open for 40% of the time, Pallas kernels for 0%

commit v1 on v0

v1 whole, which is shorter than its diff:
```python
import functools

import jax
import jax.numpy as jnp
from jax import lax
from jax.experimental import pallas as pl
from jax.experimental.pallas import tpu as pltpu
from jax.sharding import PartitionSpec as P

STEPS = 2
COEF = (-205.0 / 72.0, 8.0 / 5.0, -1.0 / 5.0, 8.0 / 315.0, -1.0 / 560.0)
R = 4
HALF_Y, HALF_X = 21, 42
WIN_Y, WIN_X = 2 * HALF_Y + 1, 2 * HALF_X + 1
PACK = 32
UNPACK = 48
SCALE = 5040.0
MARGIN = 8

VMEM = pl.BlockSpec(memory_space=pltpu.VMEM)
ANY = pl.BlockSpec(memory_space=pl.ANY)
HBM = pl.BlockSpec(memory_space=pltpu.HBM)


def params(**more):
    return pltpu.CompilerParams(vmem_limit_bytes=24 * 1024 * 1024, **more)


def cost(flops, nbytes):
    return pl.CostEstimate(flops=flops, bytes_accessed=nbytes, transcendentals=0)


def parity():
    return lax.rem(lax.axis_index("slab"), 2)


def halves():
    par = parity()
    return par * R, R - par * R


def lanes(shape):
    return lax.broadcasted_iota(jnp.int32, shape, 1)


def sublanes(shape):
    return lax.broadcasted_iota(jnp.int32, shape, 0)


def band(scal, s, shape):
    sy, sx, hy, hx = (ref[s] for ref in scal)
    return (jnp.abs(sublanes(shape) - sy) <= hy) & (jnp.abs(lanes(shape) - sx) <= hx)


def pack(rows, col0):
    cols = rows.shape[1]
    main = pltpu.roll(rows[:PACK], cols - col0, 1)
    left = pltpu.roll(rows[PACK:], lax.rem(WIN_X - col0 + cols, cols), 1)
    right = pltpu.roll(rows[PACK:], lax.rem(HALF_X - col0 + cols, cols), 1)
    return jnp.where(lanes(main.shape) < WIN_X, main, jnp.concatenate([left, right], 0))


def unpack(packed, col0):
    cols = packed.shape[1]
    main = pltpu.roll(packed, col0, 1)
    left = pltpu.roll(packed[: PACK // 2], lax.rem(col0 + cols - WIN_X, cols), 1)
    right = pltpu.roll(packed[PACK // 2 :], lax.rem(col0 + cols - HALF_X, cols), 1)
    rest = jnp.where(lanes(left.shape) < col0 + (cols - WIN_X), left, right)
    return jnp.concatenate([main, rest], 0)


def pack_planes(planes, out, scal, par):
    for f in range(4):
        row0 = scal[0][f % 2] - HALF_Y
        col0 = scal[1][f % 2] - HALF_X
        for d in range(R):
            i = d + par * (R - 1 - 2 * d)
            out[f * R + d] = pack(planes[f, i, pl.ds(row0, UNPACK), :], col0)


def copies_of(pairs, sems):
    copies = [pltpu.make_async_copy(a, b, sems.at[n]) for n, (a, b) in enumerate(pairs)]
    for copy in copies:
        copy.start()
    return copies


def wait(copies):
    for copy in copies:
        copy.wait()


def pack_kernel(sy_in, sx_in, src, rcv, out, far_out, sy, sx, planes, sems):
    par = parity()
    near, far = halves()
    rows = src.shape[2]
    pairs = [(sy_in, sy), (sx_in, sx)]
    for f in range(4):
        ref = (src, rcv)[f // 2].at[f % 2]
        pairs.append((ref.at[pl.ds(near, R)], planes.at[f, :, pl.ds(0, rows), :]))
    for f in range(4):
        ref = (src, rcv)[f // 2].at[f % 2]
        pairs.append((ref.at[pl.ds(far, R)], far_out.at[f]))
    copies = copies_of(pairs, sems)
    planes[:, :, rows:, :] = jnp.zeros((4, R, MARGIN, planes.shape[3]), jnp.float32)
    wait(copies[:6])
    pack_planes(planes, out, (sy, sx), par)
    wait(copies[6:])


def band_matrix(out):
    cols = out.shape[1]
    apart = jnp.abs(sublanes((cols, cols)) - lanes((cols, cols)))
    weights = jnp.zeros((cols, cols), jnp.float32)
    for k in range(1, R + 1):
        weights = jnp.where(apart == k, round(COEF[k] * SCALE) * 1.0, weights)
    for n in range(3):
        out[pl.ds(n * cols, cols)] = weights.astype(jnp.bfloat16)


def x_part(cur, first, matrix, out):
    rows, cols = out.shape[2], out.shape[3]
    for f in range(4):
        rest = cur[f, pl.ds(first + R, R), pl.ds(MARGIN, rows), :].reshape(R * rows, cols)
        parts = []
        for _ in range(3):
            parts.append(rest.astype(jnp.bfloat16))
            rest = rest - parts[-1].astype(jnp.float32)
        total = lax.dot_general(
            jnp.concatenate(parts, 1),
            matrix[...],
            (((1,), (0,)), ((), ())),
            preferred_element_type=jnp.float32,
        )
        out[f] = total.reshape(R, rows, cols)


def laplace(cur, xs, f, i, slot, rows):
    at = lambda layer, row: cur[f, layer, pl.ds(MARGIN + row, rows), :]
    total = 3.0 * COEF[0] * at(slot, 0) + (1.0 / SCALE) * xs[f, i]
    for k in range(1, R + 1):
        side_z = at(slot - k, 0) + at(slot + k, 0)
        side_y = at(slot, -k) + at(slot, k)
        total = total + COEF[k] * (side_z + side_y)
    return total


def inject(cells, traces, step, out, first):
    shots, layers, rows, cols = out.shape
    count = cells.shape[1]
    for s in range(shots):
        flat = cells[pl.ds(s, 1), :]
        line = lax.div(flat, cols)
        col = flat - line * cols
        line = line - first * rows
        spot = sublanes((layers * rows, count)) == line
        spot = jnp.where(spot, 1.0, 0.0).astype(jnp.bfloat16)
        value = jnp.where(sublanes((cols, count)) == col, traces[step, pl.ds(s, 1), :], 0.0)
        total = None
        for _ in range(3):
            part = value.astype(jnp.bfloat16)
            value = value - part.astype(jnp.float32)
            term = lax.dot_general(
                spot, part, (((1,), (1,)), ((), ())), preferred_element_type=jnp.float32
            )
            total = term if total is None else total + term
        out[s] = total.reshape(layers, rows, cols)


def clear(ref, layers):
    fields, slots, tall, cols = ref.shape
    ref[:, :, :MARGIN, :] = jnp.zeros((fields, slots, MARGIN, cols), jnp.float32)
    ref[:, :, tall - MARGIN :, :] = jnp.zeros((fields, slots, MARGIN, cols), jnp.float32)
    if layers is not None:
        ref[:, pl.ds(layers, R), :, :] = jnp.zeros((fields, R, tall, cols), jnp.float32)


def step_half(first, refs, scal, wave, depth, step, base, write):
    cur, prev, vel, delta, matrix, xs = refs
    rows = vel.shape[1]
    x_part(cur, first, matrix, xs)
    for s in range(2):
        spot = (sublanes(vel.shape[1:]) == scal[0][s]) & (lanes(vel.shape[1:]) == scal[1][s])
        here = depth[s] - base

        def layer(i, _):
            p = first + i
            amount = jnp.where(here == p, wave[step, s], 0.0)
            out = []
            for f in (s, 2 + s):
                twice = 2.0 * cur[f, p + R, pl.ds(MARGIN, rows), :] - prev[f, i]
                new = twice + vel[i] * laplace(cur, xs, f, i, p + R, rows)
                if f < 2:
                    new = new + jnp.where(spot, amount, 0.0)
                else:
                    new = new + delta[s, i]
                out.append((twice, new))
            write(s, i, out)
            return 0

        lax.fori_loop(0, R, layer, 0)


def writer_far(scal, new_src, new_rcv, image, before):
    shape = image.shape[1:]

    def write(s, i, out):
        inside = band(scal, s, shape)
        new = [jnp.where(inside, n, 0.0) for _, n in out]
        new_src[s, i] = new[0]
        new_rcv[s, i] = new[1]
        term = (new[0] - out[0][0]) * new[1]
        if s == 0:
            image[i] = term if before is None else term + before[i]
        else:
            image[i] = image[i] + term

    return write


def writer_near(part, twice):
    def write(s, i, out):
        part[s, i] = out[0][1]
        part[2 + s, i] = out[1][1]
        twice[s, i] = out[0][0]

    return write


def first_kernel(
    sy_in, sx_in, hy_in, hx_in, depth_in, wave_in,
    src, rcv, src_prev, rcv_prev, halo, vel_in, cells, traces,
    src_out, rcv_out, far_image, near_part, near_twice, near_vel,
    sy, sx, hy, hx, depth, wave, cur, prev, vel, delta, matrix, xs, sems,
):
    scal = (sy, sx, hy, hx)
    par = parity()
    near, far = halves()
    layers, rows = vel_in.shape[0], vel_in.shape[1]
    base = lax.axis_index("slab") * layers
    pairs = list(zip((sy_in, sx_in, hy_in, hx_in, depth_in, wave_in), (sy, sx, hy, hx, depth, wave)))
    for f in range(4):
        now, before = (src, rcv)[f // 2].at[f % 2], (src_prev, rcv_prev)[f // 2].at[f % 2]
        pairs.append((now, cur.at[f, pl.ds(R, layers), pl.ds(MARGIN, rows), :]))
        pairs.append((before, prev.at[f]))
    pairs.append((halo, cur.at[:, pl.ds((layers + R) * (1 - par), R), pl.ds(MARGIN, rows), :]))
    pairs.append((vel_in, vel))
    copies = copies_of(pairs, sems)
    clear(cur, (layers + R) * par)
    band_matrix(matrix)
    inject(cells, traces, 0, delta, base)
    wait(copies)
    has = jnp.where((base == 0) | (lax.axis_index("slab") == lax.axis_size("slab") - 1), 0.0, 1.0)
    near_vel[...] = vel[pl.ds(near, R)] * has

    for first, write in (
        (far, writer_far(scal, src_out, rcv_out, far_image, None)),
        (near, writer_near(near_part, near_twice)),
    ):
        half = lambda ref: ref.at[:, pl.ds(first, R)]
        refs = (cur, half(prev), vel.at[pl.ds(first, R)], half(delta), matrix, xs)
        step_half(first, refs, scal, wave, depth, 0, base, write)


def finish_near(scal, part, twice, halo, vel, planes, write):
    par = parity()
    rows, cols = vel.shape[1], vel.shape[2]
    for f in range(4):
        row0 = scal[0][f % 2] - HALF_Y
        col0 = scal[1][f % 2] - HALF_X
        for e in range(R):
            planes[f, e, pl.ds(row0, UNPACK), :] = unpack(halo[f * R + e], col0)
    for s in range(2):
        inside = band(scal, s, (rows, cols))
        for d in range(R):
            i = d + par * (R - 1 - 2 * d)
            new = []
            for f in (s, 2 + s):
                side = COEF[d + 1] * planes[f, 0, pl.ds(0, rows), :]
                for k in range(d + 2, R + 1):
                    side = side + COEF[k] * planes[f, k - d - 1, pl.ds(0, rows), :]
                new.append(jnp.where(inside, part[f, i] + vel[i] * side, 0.0))
            write(s, i, new, (new[0] - twice[s, i]) * new[1])


def middle_kernel(
    sy_in, sx_in, hy_in, hx_in, part, twice, halo, vel,
    near_out, near_image, packed,
    sy, sx, hy, hx, planes, sems,
):
    scal = (sy, sx, hy, hx)
    wait(copies_of(zip((sy_in, sx_in, hy_in, hx_in), scal), sems))

    def write(s, i, new, term):
        near_out[s, i] = new[0]
        near_out[2 + s, i] = new[1]
        near_image[i] = term if s == 0 else near_image[i] + term

    finish_near(scal, part, twice, halo, vel, planes, write)
    rows = vel.shape[1]
    planes[:, :, pl.ds(0, rows), :] = near_out[...]
    planes[:, :, rows:, :] = jnp.zeros((4, R, MARGIN, planes.shape[3]), jnp.float32)
    pack_planes(planes, packed, scal, parity())


def second_far_kernel(
    sy_in, sx_in, hy_in, hx_in, depth_in, wave_in,
    src, rcv, near_cur, far_src, far_rcv, halo_src, halo_rcv, vel_in, cells, traces, before,
    src_last, rcv_last, image,
    sy, sx, hy, hx, depth, wave, cur, prev, vel, delta, matrix, xs, new_far, sems,
):
    scal = (sy, sx, hy, hx)
    par = parity()
    near, far = halves()
    layers, rows = vel_in.shape[0], vel_in.shape[1]
    base = lax.axis_index("slab") * layers
    pairs = list(zip((sy_in, sx_in, hy_in, hx_in, depth_in, wave_in), (sy, sx, hy, hx, depth, wave)))
    pairs += [
        (near_cur, cur.at[:, pl.ds(R + near, R), pl.ds(MARGIN, rows), :]),
        (far_src, cur.at[pl.ds(0, 2), pl.ds(R + far, R), pl.ds(MARGIN, rows), :]),
        (far_rcv, cur.at[pl.ds(2, 2), pl.ds(R + far, R), pl.ds(MARGIN, rows), :]),
        (halo_src, cur.at[pl.ds(0, 2), pl.ds((layers + R) * (1 - par), R), pl.ds(MARGIN, rows), :]),
        (halo_rcv, cur.at[pl.ds(2, 2), pl.ds((layers + R) * (1 - par), R), pl.ds(MARGIN, rows), :]),
        (src.at[:, pl.ds(far, R)], prev.at[pl.ds(0, 2)]),
        (rcv.at[:, pl.ds(far, R)], prev.at[pl.ds(2, 2)]),
        (vel_in.at[pl.ds(far, R)], vel),
    ]
    copies = copies_of(pairs, sems)
    clear(cur, None)
    band_matrix(matrix)
    inject(cells, traces, 1, delta, base + far)
    wait(copies)
    refs = (cur, prev, vel, delta, matrix, xs)
    step_half(far, refs, scal, wave, depth, 1, base, writer_far(scal, new_far.at[pl.ds(0, 2)], new_far.at[pl.ds(2, 2)], image, before))
    wait(copies_of([
        (new_far.at[pl.ds(2 * n, 2)], (src_last, rcv_last)[n].at[:, pl.ds(far, R)]) for n in range(2)
    ], sems))


def second_near_kernel(
    sy_in, sx_in, depth_in, wave_in,
    src, rcv, near_cur, far_src, far_rcv, vel_in, cells, traces,
    near_part, near_twice,
    sy, sx, depth, wave, cur, prev, vel, delta, matrix, xs, sems,
):
    scal = (sy, sx)
    par = parity()
    near, far = halves()
    layers, rows = vel_in.shape[0], vel_in.shape[1]
    base = lax.axis_index("slab") * layers
    pairs = list(zip((sy_in, sx_in, depth_in, wave_in), (sy, sx, depth, wave)))
    pairs += [
        (near_cur, cur.at[:, pl.ds(R + near, R), pl.ds(MARGIN, rows), :]),
        (far_src, cur.at[pl.ds(0, 2), pl.ds(R + far, R), pl.ds(MARGIN, rows), :]),
        (far_rcv, cur.at[pl.ds(2, 2), pl.ds(R + far, R), pl.ds(MARGIN, rows), :]),
        (src.at[:, pl.ds(near, R)], prev.at[pl.ds(0, 2)]),
        (rcv.at[:, pl.ds(near, R)], prev.at[pl.ds(2, 2)]),
        (vel_in.at[pl.ds(near, R)], vel),
    ]
    copies = copies_of(pairs, sems)
    clear(cur, (layers + R) * par)
    band_matrix(matrix)
    inject(cells, traces, 1, delta, base + near)
    wait(copies)
    refs = (cur, prev, vel, delta, matrix, xs)
    step_half(near, refs, scal, wave, depth, 1, base, writer_near(near_part, near_twice))


def last_kernel(
    sy_in, sx_in, hy_in, hx_in, part, twice, halo, vel, near_image, far_a, far_b, src_in, rcv_in,
    image, far_sum, src_last, rcv_last,
    sy, sx, hy, hx, planes, new_near, sems,
):
    del src_in, rcv_in
    scal = (sy, sx, hy, hx)
    near, _ = halves()
    copies = copies_of(zip((sy_in, sx_in, hy_in, hx_in), scal), sems)
    far_sum[...] = far_a[...] + far_b[...]
    wait(copies)

    def write(s, i, new, term):
        new_near[s, i] = new[0]
        new_near[2 + s, i] = new[1]
        image[i] = term + (near_image[i] if s == 0 else image[i])

    finish_near(scal, part, twice, halo, vel, planes, write)
    wait(copies_of([
        (new_near.at[pl.ds(2 * n, 2)], (src_last, rcv_last)[n].at[:, pl.ds(near, R)]) for n in range(2)
    ], sems))


def image_kernel(near_a, near_b, far_a, far_b, out):
    near, far = halves()
    out[pl.ds(near, R)] = near_a[...] + near_b[...]
    out[pl.ds(far, R)] = far_a[...] + far_b[...]


def swap_a(block):
    count = lax.axis_size("slab")
    return lax.ppermute(block, "slab", [(i, i ^ 1) for i in range(count)])


def swap_b(block):
    count = lax.axis_size("slab")
    return lax.ppermute(block, "slab", [(i, ((i + 1) ^ 1) - 1 if 0 < i < count - 1 else count - 1 - i) for i in range(count)])


def swap_shots(block, turn):
    flip = 2 ** (turn + 1) - 1
    count = lax.axis_size("shots")
    return lax.ppermute(block, "shots", [(i, i ^ flip) for i in range(count)])


def shot_rounds(block, turn):
    other = swap_shots(block, turn)
    while 2 ** (turn + 1) < lax.axis_size("shots"):
        turn += 1
        block = block + other
        other = swap_shots(block, turn)
    return block, other


def per_device(
    src_prev, src_cur, rcv_prev, rcv_cur, velocity, wavelet, residual_traces,
    source_depth, source_y, source_x, half_y, half_x, receiver_cell,
):
    layers, rows, cols = velocity.shape
    f32 = jnp.float32
    in_hbm = lambda x: pltpu.with_memory_space_constraint(x, pltpu.HBM)
    src_prev, src_cur, rcv_prev, rcv_cur, velocity, wavelet = (
        in_hbm(x) for x in (src_prev, src_cur, rcv_prev, rcv_cur, velocity, wavelet)
    )
    source_depth, source_y, source_x, half_y, half_x = (
        in_hbm(x) for x in (source_depth, source_y, source_x, half_y, half_x)
    )
    shape = jax.ShapeDtypeStruct
    half4 = shape((4, R, rows, cols), f32)
    half2 = shape((2, R, rows, cols), f32)
    half1 = shape((R, rows, cols), f32)
    packed = shape((4 * R, PACK, cols), f32)
    whole = shape(src_cur.shape, f32)
    dma = lambda n: pltpu.SemaphoreType.DMA((n,))
    planes = pltpu.VMEM((4, R, rows + MARGIN, cols), f32)
    two = pltpu.SMEM(source_y.shape, jnp.int32)
    waves = pltpu.SMEM(wavelet.shape, f32)
    state = lambda deep: [
        pltpu.VMEM((4, layers + 2 * R, rows + 2 * MARGIN, cols), f32),
        pltpu.VMEM((4, deep, rows, cols), f32),
        pltpu.VMEM((deep, rows, cols), f32),
        pltpu.VMEM((2, deep, rows, cols), f32),
        pltpu.VMEM((3 * cols, cols), jnp.bfloat16),
        pltpu.VMEM((4, R, rows, cols), f32),
    ]
    new_half = pltpu.VMEM((4, R, rows, cols), f32)
    scal = (source_y, source_x, half_y, half_x)

    to_b, far_raw = pl.pallas_call(
        pack_kernel,
        out_shape=(packed, half4),
        in_specs=[HBM] * 4,
        out_specs=(VMEM, ANY),
        scratch_shapes=[two, two, planes, dma(10)],
        compiler_params=params(),
        cost_estimate=cost(1 << 20, 1 << 20),
        name="pack_halo",
    )(source_y, source_x, src_cur, rcv_cur)
    from_b = swap_b(to_b)
    halo_a = swap_a(far_raw)

    far_src, far_rcv, far_image, near_part, near_twice, near_vel = pl.pallas_call(
        first_kernel,
        out_shape=(half2, half2, half1, half4, half2, half1),
        in_specs=[HBM] * 10 + [ANY, HBM, VMEM, VMEM],
        out_specs=(VMEM,) * 6,
        scratch_shapes=[two] * 5 + [waves] + state(layers) + [dma(16)],
        compiler_params=params(),
        cost_estimate=cost(1 << 24, 1 << 25),
        name="first_step",
    )(*scal, source_depth, wavelet, src_cur, rcv_cur, src_prev, rcv_prev, halo_a, velocity, receiver_cell, residual_traces)
    halo_src, halo_rcv = swap_a(far_src), swap_a(far_rcv)

    near_cur, near_image, to_b = pl.pallas_call(
        middle_kernel,
        out_shape=(half4, half1, packed),
        in_specs=[HBM] * 4 + [VMEM] * 4,
        out_specs=(VMEM,) * 3,
        scratch_shapes=[two] * 4 + [planes, dma(4)],
        compiler_params=params(),
        cost_estimate=cost(1 << 21, 1 << 26),
        name="first_step_near",
    )(*scal, near_part, near_twice, from_b, near_vel)
    from_b = swap_b(to_b)

    src_last, rcv_last, far_image = pl.pallas_call(
        second_far_kernel,
        out_shape=(whole, whole, half1),
        in_specs=[HBM] * 8 + [ANY] * 5 + [HBM] + [VMEM] * 3,
        out_specs=(HBM, HBM, VMEM),
        scratch_shapes=[two] * 5 + [waves] + state(R) + [new_half, dma(14)],
        compiler_params=params(),
        cost_estimate=cost(1 << 23, 1 << 24),
        name="second_step_far",
    )(*scal, source_depth, wavelet, src_cur, rcv_cur, near_cur, far_src, far_rcv, halo_src, halo_rcv, velocity, receiver_cell, residual_traces, far_image)
    far_other = swap_shots(far_image, 0)

    near_part, near_twice = pl.pallas_call(
        second_near_kernel,
        out_shape=(half4, half2),
        in_specs=[HBM] * 6 + [ANY] * 3 + [HBM] + [VMEM] * 2,
        out_specs=(VMEM, VMEM),
        scratch_shapes=[two] * 3 + [waves] + state(R) + [dma(10)],
        compiler_params=params(),
        cost_estimate=cost(1 << 23, 1 << 24),
        name="second_step_part",
    )(source_y, source_x, source_depth, wavelet, src_cur, rcv_cur, near_cur, far_src, far_rcv, velocity, receiver_cell, residual_traces)

    near_image, far_sum, src_last, rcv_last = pl.pallas_call(
        last_kernel,
        out_shape=(half1, half1, whole, whole),
        in_specs=[HBM] * 4 + [VMEM] * 7 + [HBM] * 2,
        out_specs=(VMEM, VMEM, HBM, HBM),
        scratch_shapes=[two] * 4 + [planes, new_half, dma(4)],
        input_output_aliases={11: 2, 12: 3},
        compiler_params=params(),
        cost_estimate=cost(1 << 21, 1 << 21),
        name="second_step_near",
    )(*scal, near_part, near_twice, from_b, near_vel, near_image, far_image, far_other, src_last, rcv_last)
    near_a, near_b = shot_rounds(near_image, 0)
    far_a, far_b = shot_rounds(far_sum, 1)

    image = pl.pallas_call(
        image_kernel,
        out_shape=shape((layers, rows, cols), f32),
        in_specs=[VMEM] * 4,
        out_specs=VMEM,
        compiler_params=params(),
        cost_estimate=cost(1 << 17, 1 << 20),
        name="image_sum",
    )(near_a, near_b, far_a, far_b)
    return src_last, rcv_last, image


def solution(mesh):
    return jax.shard_map(
        per_device,
        mesh=mesh,
        in_specs=(
            P("shots", "slab", None, None),
            P("shots", "slab", None, None),
            P("shots", "slab", None, None),
            P("shots", "slab", None, None),
            P("slab", None, None),
            P(None, "shots"),
            P(None, "shots", None),
            P("shots"),
            P("shots"),
            P("shots"),
            P("shots"),
            P("shots"),
            P("shots", None),
        ),
        out_specs=(
            P("shots", "slab", None, None),
            P("shots", "slab", None, None),
            P("slab", None, None),
        ),
        check_vma=False,
    )
```

time: 132 us -> 41.3 us (0.31)
  the two profiles are of different devices: /device:TPU:0 before, /device:TPU:28 now
where the time goes in v1:
time: 41.3 us; the launch traced here: 41.1 us
  waiting for transfers between devices  19.3 us (47%)
  Pallas kernels  15.1 us (37%)
  starting transfers between devices  5.96 us (14%)
  between operations  0.73 us (2%)
    ppermute x4, waiting for transfers between devices, swap_shots(): return lax.ppermute(block, 'shots', [(i, i ^ flip) for i in range(count)])  15.1 us
    pallas_call x1, Pallas kernels, per_device(): pl.pallas_call(first_kernel, out_shape=(half2, half2, half1, half4, half2...  3.89 us
    ppermute x2, waiting for transfers between devices, swap_b(): lax.ppermute(block, 'slab', [(i, (i + 1 ^ 1) - 1 if 0 < i < count - 1 els...  3.84 us
    pallas_call x1, Pallas kernels, per_device(): pl.pallas_call(second_far_kernel, out_shape=(whole, whole, half1), in_spe...  3.34 us
    ppermute x2, starting transfers between devices, swap_b(): lax.ppermute(block, 'slab', [(i, (i + 1 ^ 1) - 1 if 0 < i < count - 1 els...  2.86 us
    ppermute x4, starting transfers between devices, swap_shots(): return lax.ppermute(block, 'shots', [(i, i ^ flip) for i in range(count)])  2.45 us
    pallas_call x1, Pallas kernels, per_device(): pl.pallas_call(second_near_kernel, out_shape=(half4, half2), in_specs=[HB...  2.42 us
    pallas_call x1, Pallas kernels, per_device(): pl.pallas_call(last_kernel, out_shape=(half1, half1, whole, whole), in_sp...  1.89 us
  transfers between devices with their start and end apart: 9, of which 6 were waited for; matrix products, arithmetic and copies ran while one was open for 0% of the time, Pallas kernels for 27%

profile of v1, /device:TPU:28, one launch (start us, length us, event | category | flops | bytes accessed | tf_op | source)
XLA Modules:
  0.0 41.1 jit_solution(1284708896877186064)
XLA Ops:
  0.6 0.0 copy-start
  0.6 1.4 %pack_halo.1 = (f32[16,32,128]{2,1,0:T(8,128)S(1)}, f32[4,4,64,128]{3,2,1,0:T(8,128)S(1)}) custom-call(s32[2]{0:T(128)} %sy_in.11, s32[2]{0:T(128)} %sx_in.11, f32[2,8,64,128]{3,2,1,0:T(8,128)} %src.7, f32[2,8,64,128]{3,2,1,0:T(8,128)} %rcv.7), custom_call_target="tpu_custom_call" | custom-call | flops 1048576 | bytes 1048576 | tf_op jit(solution)/shard_map/pack_halo/pallas_call | solution.py:457
  2.1 0.0 copy-start.1
  2.1 0.1 collective-permute-start
  2.2 1.5 %collective-permute-start.1 = (f32[16,32,128]{2,1,0:T(8,128)S(1)}, f32[16,32,128]{2,1,0:T(8,128)S(1)}, u32[]{:S(2)}, u32[]{:S(2)}) collective-permute-start(f32[16,32,128]{2,1,0:T(8,128)S(1)} %get-tuple-element.26), channel_id=1, source_target_pairs={{0,28},{4,8},{8,4},{12,16},{16,12},{20,24},{24,20},{28,0},{1,29},{... | collective-permute-start | bytes 786440 | tf_op jit(solution)/shard_map/ppermute | solution.py:405
  3.7 0.4 collective-permute-done.halo
  4.0 0.0 copy-done
  4.1 0.0 copy-done.1
  4.1 3.9 %first_step.1 = (f32[2,4,64,128]{3,2,1,0:T(8,128)S(1)}, f32[2,4,64,128]{3,2,1,0:T(8,128)S(1)}, f32[4,64,128]{2,1,0:T(8,128)S(1)}, f32[4,4,64,128]{3,2,1,0:T(8,12...) custom-call(s32[2]{0:T(128)} %sy_in.11, s32[2]{0:T(128)} %sx_in.11, s32[2]{0:T(128)} %hy_in.7, s32[2]{0:T(128)} %hx_in.7, ...), custom_call_target="tpu_custom_call" | custom-call | flops 16777216 | bytes 33554432 | tf_op jit(solution)/shard_map/first_step/pallas_call | solution.py:470
  7.9 0.2 collective-permute-start.3
  8.2 0.4 collective-permute-start.4
  8.5 2.9 %collective-permute-done.1.halo = f32[16,32,128]{2,1,0:T(8,128)S(1)} collective-permute-done((f32[16,32,128]{2,1,0:T(8,128)S(1)}, f32[16,32,128]{2,1,0:T(8,128)S(1)}, u32[]{:S(2)}, u32[]{:S(2)}) %collective-permute-start.1) | collective-permute-done | bytes 262176 | tf_op jit(solution)/shard_map/ppermute | solution.py:405
  11.4 1.4 %first_step_near.1 = (f32[4,4,64,128]{3,2,1,0:T(8,128)S(1)}, f32[4,64,128]{2,1,0:T(8,128)S(1)}, f32[16,32,128]{2,1,0:T(8,128)S(1)}) custom-call(s32[2]{0:T(128)} %sy_in.11, s32[2]{0:T(128)} %sx_in.11, s32[2]{0:T(128)} %hy_in.7, s32[2]{0:T(128)} %hx_in.7, f32[4,4,64,128]{3,2,1,0:T(8,128)S(1)} %get-tuple-element.24.part, ...), custom_call_target="tpu_custom_call" | custom-call | flops 2097152 | bytes 67108864 | tf_op jit(solution)/shard_map/first_step_near/pallas_call | solution.py:482
  12.8 1.3 %collective-permute-start.2 = (f32[16,32,128]{2,1,0:T(8,128)S(1)}, f32[16,32,128]{2,1,0:T(8,128)S(1)}, u32[]{:S(2)}, u32[]{:S(2)}) collective-permute-start(f32[16,32,128]{2,1,0:T(8,128)S(1)} %get-tuple-element.33), channel_id=1, source_target_pairs={{0,28},{4,8},{8,4},{12,16},{16,12},{20,24},{24,20},{28,0},{1,29},{... | collective-permute-start | bytes 786440 | tf_op jit(solution)/shard_map/ppermute | solution.py:405
  14.1 0.0 collective-permute-done.3.halo_src
  14.1 0.0 collective-permute-done.4.halo_rcv
  14.1 3.3 %second_step_far.1 = (f32[2,8,64,128]{3,2,1,0:T(8,128)}, f32[2,8,64,128]{3,2,1,0:T(8,128)}, f32[4,64,128]{2,1,0:T(8,128)S(1)}) custom-call(s32[2]{0:T(128)} %sy_in.11, s32[2]{0:T(128)} %sx_in.11, s32[2]{0:T(128)} %hy_in.7, s32[2]{0:T(128)} %hx_in.7, s32[2]{0:T(128)} %depth_in.5, f32[2,2]{1,0:T(2,128)} %wave_in.5, f32[2,8,64,128]{3,2,1,0:T(8,128)} %src.7, ...), custom_call_target="tpu_custom_call" | custom-call | flops 8388608 | bytes 16777216 | tf_op jit(solution)/shard_map/second_step_far/pallas_call | solution.py:494
  17.4 0.5 %collective-permute-start.5 = (f32[4,64,128]{2,1,0:T(8,128)S(1)}, f32[4,64,128]{2,1,0:T(8,128)S(1)}, u32[]{:S(2)}, u32[]{:S(2)}) collective-permute-start(f32[4,64,128]{2,1,0:T(8,128)S(1)} %get-tuple-element.36.far_a), channel_id=1, source_target_pairs={{0,1},{1,0},{2,3},{3,2},{4,5},{5,4},{6,7},{7,6},{8,9},{9,8},{10,11... | collective-permute-start | bytes 393224 | tf_op jit(solution)/shard_map/ppermute | solution.py:411
  18.0 2.4 %second_step_part.1 = (f32[4,4,64,128]{3,2,1,0:T(8,128)S(1)}, f32[2,4,64,128]{3,2,1,0:T(8,128)S(1)}) custom-call(s32[2]{0:T(128)} %sy_in.11, s32[2]{0:T(128)} %sx_in.11, s32[2]{0:T(128)} %depth_in.5, f32[2,2]{1,0:T(2,128)} %wave_in.5, f32[2,8,64,128]{3,2,1,0:T(8,128)} %src.7, f32[2,8,64,128]{3,2,1,0:T(8,128)} %rcv.7, ...), custom_call_target="tpu_custom_call" | custom-call | flops 8388608 | bytes 16777216 | tf_op jit(solution)/shard_map/second_step_part/pallas_call | solution.py:506
  20.4 1.0 %collective-permute-done.2.halo = f32[16,32,128]{2,1,0:T(8,128)S(1)} collective-permute-done((f32[16,32,128]{2,1,0:T(8,128)S(1)}, f32[16,32,128]{2,1,0:T(8,128)S(1)}, u32[]{:S(2)}, u32[]{:S(2)}) %collective-permute-start.2) | collective-permute-done | bytes 262176 | tf_op jit(solution)/shard_map/ppermute | solution.py:405
  21.4 1.1 %collective-permute-done.5.far_b = f32[4,64,128]{2,1,0:T(8,128)S(1)} collective-permute-done((f32[4,64,128]{2,1,0:T(8,128)S(1)}, f32[4,64,128]{2,1,0:T(8,128)S(1)}, u32[]{:S(2)}, u32[]{:S(2)}) %collective-permute-start.5) | collective-permute-done | bytes 131104 | tf_op jit(solution)/shard_map/ppermute | solution.py:411
  22.5 1.9 %second_step_near.1 = (f32[4,64,128]{2,1,0:T(8,128)S(1)}, f32[4,64,128]{2,1,0:T(8,128)S(1)}, f32[2,8,64,128]{3,2,1,0:T(8,128)}, f32[2,8,64,128]{3,2,1,0:T(8,128)}) custom-call(s32[2]{0:T(128)} %sy_in.11, s32[2]{0:T(128)} %sx_in.11, s32[2]{0:T(128)} %hy_in.7, s32[2]{0:T(128)} %hx_in.7, ...), custom_call_target="tpu_custom_call", output_to_operand_aliasing={{2}: (11, {}), {3}: (12, {})} | custom-call | flops 2097152 | bytes 2097152 | tf_op jit(solution)/shard_map/second_step_near/pallas_call | solution.py:517
  24.4 0.5 %collective-permute-start.6 = (f32[4,64,128]{2,1,0:T(8,128)S(1)}, f32[4,64,128]{2,1,0:T(8,128)S(1)}, u32[]{:S(2)}, u32[]{:S(2)}) collective-permute-start(f32[4,64,128]{2,1,0:T(8,128)S(1)} %get-tuple-element.41), channel_id=1, source_target_pairs={{0,1},{1,0},{2,3},{3,2},{4,5},{5,4},{6,7},{7,6},{8,9},{9,8},{10,11... | collective-permute-start | bytes 393224 | tf_op jit(solution)/shard_map/ppermute | solution.py:411
  24.9 1.3 %collective-permute-start.8 = (f32[4,64,128]{2,1,0:T(8,128)S(1)}, f32[4,64,128]{2,1,0:T(8,128)S(1)}, u32[]{:S(2)}, u32[]{:S(2)}) collective-permute-start(f32[4,64,128]{2,1,0:T(8,128)S(1)} %get-tuple-element.42.far_a), channel_id=1, source_target_pairs={{0,3},{1,2},{2,1},{3,0},{4,7},{5,6},{6,5},{7,4},{8,11},{9,10},{10,... | collective-permute-start | bytes 393224 | tf_op jit(solution)/shard_map/ppermute | solution.py:411
  26.2 7.2 %collective-permute-done.6 = f32[4,64,128]{2,1,0:T(8,128)S(1)} collective-permute-done((f32[4,64,128]{2,1,0:T(8,128)S(1)}, f32[4,64,128]{2,1,0:T(8,128)S(1)}, u32[]{:S(2)}, u32[]{:S(2)}) %collective-permute-start.6) | collective-permute-done | bytes 131104 | tf_op jit(solution)/shard_map/ppermute | solution.py:411
  33.5 0.1 collective-permute-start.7
  33.6 0.0 collective-permute-done.8.far_b
  33.6 6.7 %collective-permute-done.7.near_b = f32[4,64,128]{2,1,0:T(8,128)S(1)} collective-permute-done((f32[4,64,128]{2,1,0:T(8,128)S(1)}, f32[4,64,128]{2,1,0:T(8,128)S(1)}, u32[]{:S(2)}, u32[]{:S(2)}) %collective-permute-start.7) | collective-permute-done | bytes 131104 | tf_op jit(solution)/shard_map/ppermute | solution.py:411
  40.3 0.7 %image_sum.1 = f32[8,64,128]{2,1,0:T(8,128)} custom-call(f32[4,64,128]{2,1,0:T(8,128)S(1)} %add.3.near_a, f32[4,64,128]{2,1,0:T(8,128)S(1)} %collective-permute-done.7.near_b, f32[4,64,128]{2,1,0:T(8,128)S(1)} %get-tuple-element.42.far_a, f32[4,64,128]{2,1,0:T(8,128)S(1)} %collective-permute-done.8.far_b), custom_call_target="tpu_custom_call" | custom-call | flops 131072 | bytes 1048576 | tf_op jit(solution)/shard_map/image_sum/pallas_call | solution.py:531
  (1 shorter events, 0.0 us)
Async XLA Ops:
  0.6 3.4 %copy-start = (f32[2,2,256]{2,1,0:T(2,128)S(1)}, f32[2,2,256]{2,1,0:T(2,128)}, u32[]{:S(2)}) copy-start(f32[2,2,256]{2,1,0:T(2,128)} %traces.5) | copy-start | bytes 12292
  2.1 2.0 %copy-start.1 = (s32[2,256]{1,0:T(2,128)S(1)}, s32[2,256]{1,0:T(2,128)}, u32[]{:S(2)}) copy-start(s32[2,256]{1,0:T(2,128)} %cells.5) | copy-start | bytes 6148
  2.1 2.0 %collective-permute-start = (f32[4,4,64,128]{3,2,1,0:T(8,128)S(1)}, f32[4,4,64,128]{3,2,1,0:T(8,128)S(1)}, u32[]{:S(2)}, u32[]{:S(2)}) collective-permute-start(f32[4,4,64,128]{3,2,1,0:T(8,128)S(1)} %get-tuple-element.23), channel_id=1, source_target_pairs={{0,4},{4,0},{8,12},{12,8},{16,20},{20,16},{24,28},{28,24},{1,5},{5... | collective-permute-start | bytes 1572872 | tf_op jit(solution)/shard_map/ppermute | solution.py:400
  2.2 9.2 %collective-permute-start.1 = (f32[16,32,128]{2,1,0:T(8,128)S(1)}, f32[16,32,128]{2,1,0:T(8,128)S(1)}, u32[]{:S(2)}, u32[]{:S(2)}) collective-permute-start(f32[16,32,128]{2,1,0:T(8,128)S(1)} %get-tuple-element.26), channel_id=1, source_target_pairs={{0,28},{4,8},{8,4},{12,16},{16,12},{20,24},{24,20},{28,0},{1,29},{... | collective-permute-start | bytes 786440 | tf_op jit(solution)/shard_map/ppermute | solution.py:405
  7.9 6.1 %collective-permute-start.3 = (f32[2,4,64,128]{3,2,1,0:T(8,128)S(1)}, f32[2,4,64,128]{3,2,1,0:T(8,128)S(1)}, u32[]{:S(2)}, u32[]{:S(2)}) collective-permute-start(f32[2,4,64,128]{3,2,1,0:T(8,128)S(1)} %get-tuple-element.29.far_src), channel_id=1, source_target_pairs={{0,4},{4,0},{8,12},{12,8},{16,20},{20,16},{24,28},{28,24},{1,5},{5... | collective-permute-start | bytes 786440 | tf_op jit(solution)/shard_map/ppermute | solution.py:400
  8.2 5.9 %collective-permute-start.4 = (f32[2,4,64,128]{3,2,1,0:T(8,128)S(1)}, f32[2,4,64,128]{3,2,1,0:T(8,128)S(1)}, u32[]{:S(2)}, u32[]{:S(2)}) collective-permute-start(f32[2,4,64,128]{3,2,1,0:T(8,128)S(1)} %get-tuple-element.30.far_rcv), channel_id=1, source_target_pairs={{0,4},{4,0},{8,12},{12,8},{16,20},{20,16},{24,28},{28,24},{1,5},{5... | collective-permute-start | bytes 786440 | tf_op jit(solution)/shard_map/ppermute | solution.py:400
  12.8 8.6 %collective-permute-start.2 = (f32[16,32,128]{2,1,0:T(8,128)S(1)}, f32[16,32,128]{2,1,0:T(8,128)S(1)}, u32[]{:S(2)}, u32[]{:S(2)}) collective-permute-start(f32[16,32,128]{2,1,0:T(8,128)S(1)} %get-tuple-element.33), channel_id=1, source_target_pairs={{0,28},{4,8},{8,4},{12,16},{16,12},{20,24},{24,20},{28,0},{1,29},{... | collective-permute-start | bytes 786440 | tf_op jit(solution)/shard_map/ppermute | solution.py:405
  17.4 5.0 %collective-permute-start.5 = (f32[4,64,128]{2,1,0:T(8,128)S(1)}, f32[4,64,128]{2,1,0:T(8,128)S(1)}, u32[]{:S(2)}, u32[]{:S(2)}) collective-permute-start(f32[4,64,128]{2,1,0:T(8,128)S(1)} %get-tuple-element.36.far_a), channel_id=1, source_target_pairs={{0,1},{1,0},{2,3},{3,2},{4,5},{5,4},{6,7},{7,6},{8,9},{9,8},{10,11... | collective-permute-start | bytes 393224 | tf_op jit(solution)/shard_map/ppermute | solution.py:411
  24.4 9.1 %collective-permute-start.6 = (f32[4,64,128]{2,1,0:T(8,128)S(1)}, f32[4,64,128]{2,1,0:T(8,128)S(1)}, u32[]{:S(2)}, u32[]{:S(2)}) collective-permute-start(f32[4,64,128]{2,1,0:T(8,128)S(1)} %get-tuple-element.41), channel_id=1, source_target_pairs={{0,1},{1,0},{2,3},{3,2},{4,5},{5,4},{6,7},{7,6},{8,9},{9,8},{10,11... | collective-permute-start | bytes 393224 | tf_op jit(solution)/shard_map/ppermute | solution.py:411
  24.9 8.7 %collective-permute-start.8 = (f32[4,64,128]{2,1,0:T(8,128)S(1)}, f32[4,64,128]{2,1,0:T(8,128)S(1)}, u32[]{:S(2)}, u32[]{:S(2)}) collective-permute-start(f32[4,64,128]{2,1,0:T(8,128)S(1)} %get-tuple-element.42.far_a), channel_id=1, source_target_pairs={{0,3},{1,2},{2,1},{3,0},{4,7},{5,6},{6,5},{7,4},{8,11},{9,10},{10,... | collective-permute-start | bytes 393224 | tf_op jit(solution)/shard_map/ppermute | solution.py:411
  33.5 6.8 %collective-permute-start.7 = (f32[4,64,128]{2,1,0:T(8,128)S(1)}, f32[4,64,128]{2,1,0:T(8,128)S(1)}, u32[]{:S(2)}, u32[]{:S(2)}) collective-permute-start(f32[4,64,128]{2,1,0:T(8,128)S(1)} %add.3.near_a), channel_id=1, source_target_pairs={{0,3},{1,2},{2,1},{3,0},{4,7},{5,6},{6,5},{7,4},{8,11},{9,10},{10,... | collective-permute-start | bytes 393224 | tf_op jit(solution)/shard_map/ppermute | solution.py:411

commit v2 on v1

v2 whole, which is shorter than its diff:
```python
import functools

import jax
import jax.numpy as jnp
from jax import lax
from jax.experimental import pallas as pl
from jax.experimental.pallas import tpu as pltpu
from jax.sharding import PartitionSpec as P

STEPS = 2
COEF = (-205.0 / 72.0, 8.0 / 5.0, -1.0 / 5.0, 8.0 / 315.0, -1.0 / 560.0)
R = 4
HALF_Y, HALF_X = 21, 42
WIN_Y, WIN_X = 2 * HALF_Y + 1, 2 * HALF_X + 1
PACK = 29
REST = WIN_Y - PACK
SCALE = 5040.0
MARGIN = 8

VMEM = pl.BlockSpec(memory_space=pltpu.VMEM)
ANY = pl.BlockSpec(memory_space=pl.ANY)
HBM = pl.BlockSpec(memory_space=pltpu.HBM)


def params(**more):
    return pltpu.CompilerParams(vmem_limit_bytes=24 * 1024 * 1024, **more)


def cost(flops, nbytes):
    return pl.CostEstimate(flops=flops, bytes_accessed=nbytes, transcendentals=0)


def parity():
    return lax.rem(lax.axis_index("slab"), 2)


def halves():
    par = parity()
    return par * R, R - par * R


def lanes(shape):
    return lax.broadcasted_iota(jnp.int32, shape, 1)


def sublanes(shape):
    return lax.broadcasted_iota(jnp.int32, shape, 0)


def band(scal, s, shape):
    sy, sx, hy, hx = (ref[s] for ref in scal)
    return (jnp.abs(sublanes(shape) - sy) <= hy) & (jnp.abs(lanes(shape) - sx) <= hx)


def pack(planes, f, i, row0, col0):
    cols = planes.shape[3]
    main = pltpu.roll(planes[f, i, pl.ds(row0, 32), :], cols - col0, 1)
    left = pltpu.roll(planes[f, i, pl.ds(row0 + PACK, 16), :], lax.rem(WIN_X - col0 + cols, cols), 1)
    right = pltpu.roll(planes[f, i, pl.ds(row0 + PACK - REST + 8, 24), :], lax.rem(HALF_X - col0 + cols, cols), 1)
    left = jnp.concatenate([left, right[8:]], 0)
    right = jnp.concatenate([right[:8], right], 0)
    spare = jnp.where(sublanes(main.shape) < REST, left, right)
    return jnp.where(lanes(main.shape) < WIN_X, main, spare)


def pack_field(planes, f, out, scal, par):
    row0 = scal[0][f % 2] - HALF_Y
    col0 = scal[1][f % 2] - HALF_X
    for d in range(R):
        i = d + par * (R - 1 - 2 * d)
        out[pl.ds((f * R + d) * PACK, PACK), :] = pack(planes, f, i, row0, col0)[:PACK]


def unpack_planes(packed, planes, scal):
    cols = packed.shape[1]
    for f in range(4):
        row0 = scal[0][f % 2] - HALF_Y
        col0 = scal[1][f % 2] - HALF_X
        for e in range(R):
            n = (f * R + e) * PACK
            planes[f, e, pl.ds(row0, PACK), :] = pltpu.roll(packed[pl.ds(n, PACK), :], col0, 1)
            left = pltpu.roll(packed[pl.ds(n, REST), :], lax.rem(col0 + cols - WIN_X, cols), 1)
            right = pltpu.roll(packed[pl.ds(n + REST, REST), :], lax.rem(col0 + cols - HALF_X, cols), 1)
            rest = jnp.where(lanes(left.shape) < col0 + (cols - WIN_X), left, right)
            planes[f, e, pl.ds(row0 + PACK, REST), :] = rest


def copies_of(pairs, sems):
    copies = [pltpu.make_async_copy(a, b, sems.at[n]) for n, (a, b) in enumerate(pairs)]
    for copy in copies:
        copy.start()
    return copies


def wait(copies):
    for copy in copies:
        copy.wait()


def pack_kernel(*refs):
    scal_in, (src, rcv, out), scal, (planes, far_src, far_rcv, sems) = refs[:6], refs[6:9], refs[9:15], refs[15:]
    near, far = halves()
    rows = src.shape[2]
    pairs = list(zip(scal_in, scal))
    for f in range(4):
        ref = (src, rcv)[f // 2].at[f % 2]
        pairs.append((ref.at[pl.ds(near, R)], planes.at[f, :, pl.ds(0, rows), :]))
    for ref, far_ref in ((src, far_src), (rcv, far_rcv)):
        pairs.append((ref.at[:, pl.ds(far, R)], far_ref))
    copies = copies_of(pairs, sems)
    planes[:, :, rows:, :] = jnp.zeros((4, R, MARGIN, planes.shape[3]), jnp.float32)
    wait(copies[:6])
    for f in range(4):
        wait(copies[6 + f : 7 + f])
        pack_field(planes, f, out, scal, parity())
    wait(copies[10:])


def band_matrix(out):
    cols = out.shape[1]
    apart = jnp.abs(sublanes((cols, cols)) - lanes((cols, cols)))
    weights = jnp.zeros((cols, cols), jnp.float32)
    for k in range(1, R + 1):
        weights = jnp.where(apart == k, round(COEF[k] * SCALE) * 1.0, weights)
    for n in range(3):
        out[pl.ds(n * cols, cols)] = weights.astype(jnp.bfloat16)


def x_part(cur, first, matrix, out):
    rows, cols = out.shape[2], out.shape[3]
    for f in range(4):
        rest = cur[f, pl.ds(first + R, R), pl.ds(MARGIN, rows), :].reshape(R * rows, cols)
        parts = []
        for _ in range(3):
            parts.append(rest.astype(jnp.bfloat16))
            rest = rest - parts[-1].astype(jnp.float32)
        total = lax.dot_general(
            jnp.concatenate(parts, 1),
            matrix[...],
            (((1,), (0,)), ((), ())),
            preferred_element_type=jnp.float32,
        )
        out[f] = total.reshape(R, rows, cols)


def laplace(cur, xs, f, i, slot, rows):
    at = lambda layer, row: cur[f, layer, pl.ds(MARGIN + row, rows), :]
    total = 3.0 * COEF[0] * at(slot, 0) + (1.0 / SCALE) * xs[f, i]
    for k in range(1, R + 1):
        side_z = at(slot - k, 0) + at(slot + k, 0)
        side_y = at(slot, -k) + at(slot, k)
        total = total + COEF[k] * (side_z + side_y)
    return total


def inject(cells, traces, first, outs):
    shots, layers, rows, cols = outs[0].shape
    count = cells.shape[1]
    for s in range(shots):
        flat = cells[pl.ds(s, 1), :]
        line = lax.div(flat, cols)
        col = flat - line * cols
        line = line - first * rows
        spot = sublanes((layers * rows, count)) == line
        spot = jnp.where(spot, 1.0, 0.0).astype(jnp.bfloat16)
        here = sublanes((cols, count)) == col
        value = jnp.concatenate(
            [jnp.where(here, traces[step, pl.ds(s, 1), :], 0.0) for step in range(STEPS)], 0
        )
        total = None
        for _ in range(3):
            part = value.astype(jnp.bfloat16)
            value = value - part.astype(jnp.float32)
            term = lax.dot_general(
                spot, part, (((1,), (1,)), ((), ())), preferred_element_type=jnp.float32
            )
            total = term if total is None else total + term
        for step, out in enumerate(outs):
            out[s] = total[:, step * cols : (step + 1) * cols].reshape(layers, rows, cols)


def clear(ref, layers):
    fields, slots, tall, cols = ref.shape
    ref[:, :, :MARGIN, :] = jnp.zeros((fields, slots, MARGIN, cols), jnp.float32)
    ref[:, :, tall - MARGIN :, :] = jnp.zeros((fields, slots, MARGIN, cols), jnp.float32)
    if layers is not None:
        ref[:, pl.ds(layers, R), :, :] = jnp.zeros((fields, R, tall, cols), jnp.float32)


def step_half(first, refs, scal, wave, depth, step, base, write):
    cur, prev, vel, delta, xs = refs
    rows = vel.shape[1]
    for s in range(2):
        spot = (sublanes(vel.shape[1:]) == scal[0][s]) & (lanes(vel.shape[1:]) == scal[1][s])
        here = depth[s] - base

        def layer(i, _):
            p = first + i
            amount = jnp.where(here == p, wave[step, s], 0.0)
            out = []
            for f in (s, 2 + s):
                twice = 2.0 * cur[f, p + R, pl.ds(MARGIN, rows), :] - prev[f, i]
                new = twice + vel[i] * laplace(cur, xs, f, i, p + R, rows)
                if f < 2:
                    new = new + jnp.where(spot, amount, 0.0)
                else:
                    new = new + delta[s, i]
                out.append((twice, new))
            write(s, i, out)
            return 0

        lax.fori_loop(0, R, layer, 0, unroll=True)


def writer_far(scal, new_src, new_rcv, image, before):
    shape = image.shape[1:]

    def write(s, i, out):
        inside = band(scal, s, shape)
        new = [jnp.where(inside, n, 0.0) for _, n in out]
        new_src[s, i] = new[0]
        new_rcv[s, i] = new[1]
        term = (new[0] - out[0][0]) * new[1]
        if s == 0:
            image[i] = term if before is None else term + before[i]
        else:
            image[i] = image[i] + term

    return write


def writer_near(part, twice):
    def write(s, i, out):
        part[s, i] = out[0][1]
        part[2 + s, i] = out[1][1]
        twice[s, i] = out[0][0]

    return write


def first_kernel(
    sy, sx, hy, hx, depth, wave, planes,
    far_src, far_rcv, halo_src, halo_rcv, src_prev, rcv_prev, vel_in, cells, traces,
    src_out, rcv_out, far_image, near_part, near_twice, near_vel, before, vel, later,
    cur, prev, delta, matrix, xs_near, xs_far, sems,
):
    scal = (sy, sx, hy, hx)
    par = parity()
    near, far = halves()
    layers, rows = vel_in.shape[0], vel_in.shape[1]
    base = lax.axis_index("slab") * layers
    inner = pl.ds(MARGIN, rows)
    near_raw = planes.at[:, :, pl.ds(0, rows), :]
    halo = (layers + R) * (1 - par)
    fields = (pl.ds(0, 2), pl.ds(2, 2))
    pairs = [
        (near_raw, cur.at[:, pl.ds(R + near, R), inner, :]),
        (near_raw, before.at[:, pl.ds(near, R)]),
    ]
    for own, other, n in ((far_src, halo_src, 0), (far_rcv, halo_rcv, 1)):
        pairs += [
            (own, cur.at[fields[n], pl.ds(R + far, R), inner, :]),
            (own, before.at[fields[n], pl.ds(far, R)]),
            (other, cur.at[fields[n], pl.ds(halo, R), inner, :]),
        ]
    pairs.append((vel_in, vel))
    for first in (near, far):
        for ref, n in ((src_prev, 0), (rcv_prev, 1)):
            pairs.append((ref.at[:, pl.ds(first, R)], prev.at[fields[n], pl.ds(first, R)]))
    copies = copies_of(pairs, sems)
    clear(cur, (layers + R) * par)
    band_matrix(matrix)
    inject(cells, traces, base, (delta, later))
    wait(copies[:8])
    x_part(cur, near, matrix, xs_near)
    x_part(cur, far, matrix, xs_far)
    wait(copies[8:11])
    has = jnp.where((base == 0) | (lax.axis_index("slab") == lax.axis_size("slab") - 1), 0.0, 1.0)
    near_vel[...] = vel[pl.ds(near, R)] * has

    def half_step(first, xs, write):
        refs = (cur, prev.at[:, pl.ds(first, R)], vel.at[pl.ds(first, R)], delta.at[:, pl.ds(first, R)], xs)
        step_half(first, refs, scal, wave, depth, 0, base, write)

    half_step(near, xs_near, writer_near(near_part, near_twice))
    wait(copies[11:])
    half_step(far, xs_far, writer_far(scal, src_out, rcv_out, far_image, None))


def finish_near(scal, part, twice, halo, vel, planes, write):
    par = parity()
    rows, cols = vel.shape[1], vel.shape[2]
    unpack_planes(halo, planes, scal)
    for s in range(2):
        inside = band(scal, s, (rows, cols))
        for d in range(R):
            i = d + par * (R - 1 - 2 * d)
            new = []
            for f in (s, 2 + s):
                side = COEF[d + 1] * planes[f, 0, pl.ds(0, rows), :]
                for k in range(d + 2, R + 1):
                    side = side + COEF[k] * planes[f, k - d - 1, pl.ds(0, rows), :]
                new.append(jnp.where(inside, part[f, i] + vel[i] * side, 0.0))
            write(s, i, new, (new[0] - twice[s, i]) * new[1])


def middle_kernel(
    sy, sx, hy, hx, part, twice, halo, vel,
    near_out, near_image, packed,
    planes,
):
    scal = (sy, sx, hy, hx)

    def write(s, i, new, term):
        near_out[s, i] = new[0]
        near_out[2 + s, i] = new[1]
        near_image[i] = term if s == 0 else near_image[i] + term

    finish_near(scal, part, twice, halo, vel, planes, write)
    rows = vel.shape[1]
    planes[:, :, pl.ds(0, rows), :] = near_out[...]
    planes[:, :, rows:, :] = jnp.zeros((4, R, MARGIN, planes.shape[3]), jnp.float32)
    for f in range(4):
        pack_field(planes, f, packed, scal, parity())


def second_far_kernel(
    sy, sx, hy, hx, depth, wave,
    before, near_cur, far_src, far_rcv, halo_src, halo_rcv, vel, delta, image_before,
    new_far, image,
    cur, matrix, xs, sems,
):
    scal = (sy, sx, hy, hx)
    par = parity()
    near, far = halves()
    layers, rows = vel.shape[0], vel.shape[1]
    base = lax.axis_index("slab") * layers
    src, rcv = pl.ds(0, 2), pl.ds(2, 2)
    own, halo = pl.ds(R + far, R), pl.ds((layers + R) * (1 - par), R)
    inner = pl.ds(MARGIN, rows)
    copies = copies_of([
        (far_src, cur.at[src, own, inner, :]),
        (far_rcv, cur.at[rcv, own, inner, :]),
        (near_cur, cur.at[:, pl.ds(R + near, R), inner, :]),
        (halo_src, cur.at[src, halo, inner, :]),
        (halo_rcv, cur.at[rcv, halo, inner, :]),
    ], sems)
    clear(cur, None)
    band_matrix(matrix)
    wait(copies)
    x_part(cur, far, matrix, xs)
    refs = (cur, before.at[:, pl.ds(far, R)], vel.at[pl.ds(far, R)], delta.at[:, pl.ds(far, R)], xs)
    write = writer_far(scal, new_far.at[src], new_far.at[rcv], image, image_before)
    step_half(far, refs, scal, wave, depth, 1, base, write)


def second_near_kernel(
    sy, sx, depth, wave,
    before, near_cur, far_src, far_rcv, vel, delta,
    near_part, near_twice,
    cur, matrix, xs, sems,
):
    scal = (sy, sx)
    par = parity()
    near, far = halves()
    layers, rows = vel.shape[0], vel.shape[1]
    base = lax.axis_index("slab") * layers
    inner = pl.ds(MARGIN, rows)
    copies = copies_of([
        (near_cur, cur.at[:, pl.ds(R + near, R), inner, :]),
        (far_src, cur.at[pl.ds(0, 2), pl.ds(R + far, R), inner, :]),
        (far_rcv, cur.at[pl.ds(2, 2), pl.ds(R + far, R), inner, :]),
    ], sems)
    clear(cur, (layers + R) * par)
    band_matrix(matrix)
    wait(copies)
    x_part(cur, near, matrix, xs)
    refs = (cur, before.at[:, pl.ds(near, R)], vel.at[pl.ds(near, R)], delta.at[:, pl.ds(near, R)], xs)
    step_half(near, refs, scal, wave, depth, 1, base, writer_near(near_part, near_twice))


def last_kernel(
    sy, sx, hy, hx, part, twice, halo, vel, near_image, far_a, far_b,
    image, far_sum, new_near,
    planes,
):
    scal = (sy, sx, hy, hx)
    far_sum[...] = far_a[...] + far_b[...]

    def write(s, i, new, term):
        new_near[s, i] = new[0]
        new_near[2 + s, i] = new[1]
        image[i] = term + (near_image[i] if s == 0 else image[i])

    finish_near(scal, part, twice, halo, vel, planes, write)


def write_kernel(new_near, new_far, src_last, rcv_last, sems):
    near, far = halves()
    wait(copies_of([
        (new.at[pl.ds(2 * n, 2)], (src_last, rcv_last)[n].at[:, pl.ds(first, R)])
        for new, first in ((new_near, near), (new_far, far))
        for n in range(2)
    ], sems))


def image_kernel(near_a, near_b, far_a, far_b, out):
    near, far = halves()
    out[pl.ds(near, R)] = near_a[...] + near_b[...]
    out[pl.ds(far, R)] = far_a[...] + far_b[...]


def swap_a(block):
    count = lax.axis_size("slab")
    return lax.ppermute(block, "slab", [(i, i ^ 1) for i in range(count)])


def swap_b(block):
    count = lax.axis_size("slab")
    return lax.ppermute(block, "slab", [(i, ((i + 1) ^ 1) - 1 if 0 < i < count - 1 else count - 1 - i) for i in range(count)])


def swap_shots(block, turn):
    flip = 2 ** (turn + 1) - 1
    count = lax.axis_size("shots")
    return lax.ppermute(block, "shots", [(i, i ^ flip) for i in range(count)])


def shot_rounds(block, turn):
    other = swap_shots(block, turn)
    while 2 ** (turn + 1) < lax.axis_size("shots"):
        turn += 1
        block = block + other
        other = swap_shots(block, turn)
    return block, other


def per_device(
    src_prev, src_cur, rcv_prev, rcv_cur, velocity, wavelet, residual_traces,
    source_depth, source_y, source_x, half_y, half_x, receiver_cell,
):
    layers, rows, cols = velocity.shape
    f32 = jnp.float32
    in_hbm = lambda x: pltpu.with_memory_space_constraint(x, pltpu.HBM)
    src_prev, src_cur, rcv_prev, rcv_cur, velocity = (
        in_hbm(x) for x in (src_prev, src_cur, rcv_prev, rcv_cur, velocity)
    )
    scal_hbm = [
        in_hbm(x) for x in (source_y, source_x, half_y, half_x, source_depth, wavelet)
    ]
    shape = jax.ShapeDtypeStruct
    half4 = shape((4, R, rows, cols), f32)
    half2 = shape((2, R, rows, cols), f32)
    half1 = shape((R, rows, cols), f32)
    packed = shape((4 * R * PACK, cols), f32)
    dma = lambda n: pltpu.SemaphoreType.DMA((n,))
    planes = (4, R, rows + MARGIN, cols)
    state = pltpu.VMEM((4, layers + 2 * R, rows + 2 * MARGIN, cols), f32)
    matrix = pltpu.VMEM((3 * cols, cols), jnp.bfloat16)
    xs = pltpu.VMEM((4, R, rows, cols), f32)

    to_b, *scal, near_raw, far_src, far_rcv = pl.pallas_call(
        pack_kernel,
        out_shape=(packed, *(shape(x.shape, x.dtype) for x in scal_hbm), shape(planes, f32), half2, half2),
        in_specs=[HBM] * 8,
        out_specs=(VMEM,) * 10,
        scratch_shapes=[dma(12)],
        compiler_params=params(),
        cost_estimate=cost(1 << 20, 1 << 20),
        name="pack_halo",
    )(*scal_hbm, src_cur, rcv_cur)
    from_b = swap_b(to_b)
    halo_src, halo_rcv = swap_a(far_src), swap_a(far_rcv)

    far_src, far_rcv, far_image, near_part, near_twice, near_vel, before, vel, later = pl.pallas_call(
        first_kernel,
        out_shape=(half2, half2, half1, half4, half2, half1, shape((4, layers, rows, cols), f32), shape(velocity.shape, f32), shape((2, layers, rows, cols), f32)),
        in_specs=[VMEM] * 9 + [ANY] * 2 + [HBM] * 3 + [VMEM, VMEM],
        out_specs=(VMEM,) * 9,
        scratch_shapes=[state, pltpu.VMEM((4, layers, rows, cols), f32), pltpu.VMEM((2, layers, rows, cols), f32), matrix, xs, xs, dma(13)],
        compiler_params=params(),
        cost_estimate=cost(1 << 24, 1 << 25),
        name="first_step",
    )(*scal, near_raw, far_src, far_rcv, halo_src, halo_rcv, src_prev, rcv_prev, velocity, receiver_cell, residual_traces)
    halo_src, halo_rcv = swap_a(far_src), swap_a(far_rcv)

    near_cur, near_image, to_b = pl.pallas_call(
        middle_kernel,
        out_shape=(half4, half1, packed),
        in_specs=[VMEM] * 8,
        out_specs=(VMEM,) * 3,
        scratch_shapes=[pltpu.VMEM(planes, f32)],
        compiler_params=params(),
        cost_estimate=cost(1 << 21, 1 << 26),
        name="first_step_near",
    )(*scal[:4], near_part, near_twice, from_b, near_vel)
    from_b = swap_b(to_b)

    new_far, far_image = pl.pallas_call(
        second_far_kernel,
        out_shape=(half4, half1),
        in_specs=[VMEM] * 7 + [ANY] * 5 + [VMEM] * 3,
        out_specs=(VMEM, VMEM),
        scratch_shapes=[state, matrix, xs, dma(5)],
        compiler_params=params(),
        cost_estimate=cost(1 << 23, 1 << 24),
        name="second_step_far",
    )(*scal, before, near_cur, far_src, far_rcv, halo_src, halo_rcv, vel, later, far_image)
    far_other = swap_shots(far_image, 0)


    near_part, near_twice = pl.pallas_call(
        second_near_kernel,
        out_shape=(half4, half2),
        in_specs=[VMEM] * 5 + [ANY] * 3 + [VMEM] * 2,
        out_specs=(VMEM, VMEM),
        scratch_shapes=[state, matrix, xs, dma(3)],
        compiler_params=params(),
        cost_estimate=cost(1 << 23, 1 << 24),
        name="second_step_part",
    )(scal[0], scal[1], scal[4], scal[5], before, near_cur, far_src, far_rcv, vel, later)

    near_image, far_image, new_near = pl.pallas_call(
        last_kernel,
        out_shape=(half1, half1, half4),
        in_specs=[VMEM] * 11,
        out_specs=(VMEM,) * 3,
        scratch_shapes=[pltpu.VMEM(planes, f32)],
        compiler_params=params(),
        cost_estimate=cost(1 << 21, 1 << 21),
        name="second_step_near",
    )(*scal[:4], near_part, near_twice, from_b, near_vel, near_image, far_image, far_other)
    near_a, near_b = shot_rounds(near_image, 0)
    far_a, far_b = shot_rounds(far_image, 1)

    src_last, rcv_last = pl.pallas_call(
        write_kernel,
        out_shape=(shape(src_cur.shape, f32),) * 2,
        in_specs=[VMEM, VMEM],
        out_specs=(HBM, HBM),
        scratch_shapes=[dma(4)],
        compiler_params=params(),
        cost_estimate=cost(1 << 10, 1 << 22),
        name="write_fields",
    )(new_near, new_far)

    image = pl.pallas_call(
        image_kernel,
        out_shape=shape((layers, rows, cols), f32),
        in_specs=[VMEM] * 4,
        out_specs=VMEM,
        compiler_params=params(),
        cost_estimate=cost(1 << 17, 1 << 20),
        name="image_sum",
    )(near_a, near_b, far_a, far_b)
    return src_last, rcv_last, image


def solution(mesh):
    return jax.shard_map(
        per_device,
        mesh=mesh,
        in_specs=(
            P("shots", "slab", None, None),
            P("shots", "slab", None, None),
            P("shots", "slab", None, None),
            P("shots", "slab", None, None),
            P("slab", None, None),
            P(None, "shots"),
            P(None, "shots", None),
            P("shots"),
            P("shots"),
            P("shots"),
            P("shots"),
            P("shots"),
            P("shots", None),
        ),
        out_specs=(
            P("shots", "slab", None, None),
            P("shots", "slab", None, None),
            P("slab", None, None),
        ),
        check_vma=False,
    )
```

time: 41.3 us -> 37.3 us (0.903)
  the two profiles are of different devices: /device:TPU:28 before, /device:TPU:0 now
where the time goes in v2:
time: 37.3 us; the launch traced here: 37 us
  starting transfers between devices  16.5 us (44%)
  Pallas kernels  10.4 us (28%)
  waiting for transfers between devices  8.74 us (23%)
  between operations  0.72 us (2%)
  local copies, waits for them, and re-layouts  0.69 us (2%)
    ppermute x4, starting transfers between devices, swap_shots(): return lax.ppermute(block, 'shots', [(i, i ^ flip) for i in range(count)])  9.5 us
    ppermute x2, starting transfers between devices, swap_b(): lax.ppermute(block, 'slab', [(i, (i + 1 ^ 1) - 1 if 0 < i < count - 1 els...  5.85 us
    ppermute x4, waiting for transfers between devices, swap_shots(): return lax.ppermute(block, 'shots', [(i, i ^ flip) for i in range(count)])  5.14 us
    ppermute x2, waiting for transfers between devices, swap_b(): lax.ppermute(block, 'slab', [(i, (i + 1 ^ 1) - 1 if 0 < i < count - 1 els...  3.59 us
    pallas_call x1, Pallas kernels, per_device(): pl.pallas_call(first_kernel, out_shape=(half2, half2, half1, half4, half2...  3.02 us
    pallas_call x1, Pallas kernels, per_device(): pl.pallas_call(pack_kernel, out_shape=(packed, *(shape(x.shape, x.dtype)...  1.82 us
    pallas_call x1, Pallas kernels, per_device(): pl.pallas_call(second_far_kernel, out_shape=(half4, half1), in_specs=[VME...  1.38 us
    ppermute x4, starting transfers between devices, swap_a(): return lax.ppermute(block, 'slab', [(i, i ^ 1) for i in range(count)])  1.16 us
  transfers between devices with their start and end apart: 10, of which 5 were waited for; matrix products, arithmetic and copies ran while one was open for 0% of the time, Pallas kernels for 20%

profile of v2, /device:TPU:0, one launch (start us, length us, event | category | flops | bytes accessed | tf_op | source)
XLA Modules:
  0.0 37.0 jit_solution(16211932890847378261)
XLA Ops:
  0.6 1.8 %pack_halo.1 = (f32[464,128]{1,0:T(8,128)S(1)}, s32[2]{0:T(128)S(1)}, s32[2]{0:T(128)S(1)}, s32[2]{0:T(128)S(1)}, s32[2]{0:T(128)S(1)}, /*index=5*/s32[2]{0:T(12...) custom-call(s32[2]{0:T(128)} %refs_0_.1, ...), custom_call_target="tpu_custom_call" | custom-call | flops 1048576 | bytes 1048576 | tf_op jit(solution)/shard_map/pack_halo/pallas_call | solution.py:462
  2.5 0.5 %collective-permute-start = (f32[2,4,64,128]{3,2,1,0:T(8,128)S(1)}, f32[2,4,64,128]{3,2,1,0:T(8,128)S(1)}, u32[]{:S(2)}, u32[]{:S(2)}) collective-permute-start(f32[2,4,64,128]{3,2,1,0:T(8,128)S(1)} %get-tuple-element.41.far_src), channel_id=1, source_target_pairs={{0,4},{4,0},{8,12},{12,8},{16,20},{20,16},{24,28},{28,24},{1,5},{5... | collective-permute-start | bytes 786440 | tf_op jit(solution)/shard_map/ppermute | solution.py:415
  3.0 0.1 collective-permute-start.1
  3.1 3.6 %collective-permute-start.2 = (f32[464,128]{1,0:T(8,128)S(1)}, f32[464,128]{1,0:T(8,128)S(1)}, u32[]{:S(2)}, u32[]{:S(2)}) collective-permute-start(f32[464,128]{1,0:T(8,128)S(1)} %get-tuple-element.46), channel_id=1, source_target_pairs={{0,28},{4,8},{8,4},{12,16},{16,12},{20,24},{24,20},{28,0},{1,29},{... | collective-permute-start | bytes 712712 | tf_op jit(solution)/shard_map/ppermute | solution.py:420
  6.6 0.0 collective-permute-done.halo_src
  6.6 0.0 collective-permute-done.1.halo_rcv
  6.6 0.0 copy-start
  6.6 0.0 copy-start.1
  6.6 0.7 %copy-done = f32[2,2,256]{2,1,0:T(2,128)S(1)} copy-done((f32[2,2,256]{2,1,0:T(2,128)S(1)}, f32[2,2,256]{2,1,0:T(2,128)}, u32[]{:S(2)}) %copy-start) | copy-done | bytes 4120
  7.3 0.0 copy-done.1
  7.3 3.0 %first_step.1 = (f32[2,4,64,128]{3,2,1,0:T(8,128)S(1)}, f32[2,4,64,128]{3,2,1,0:T(8,128)S(1)}, f32[4,64,128]{2,1,0:T(8,128)S(1)}, f32[4,4,64,128]{3,2,1,0:T(8,12...) custom-call(s32[2]{0:T(128)S(1)} %get-tuple-element.34.sy, ...), custom_call_target="tpu_custom_call" | custom-call | flops 16777216 | bytes 33554432 | tf_op jit(solution)/shard_map/first_step/pallas_call | solution.py:475
  10.4 0.1 collective-permute-start.4
  10.4 0.5 %collective-permute-start.5 = (f32[2,4,64,128]{3,2,1,0:T(8,128)S(1)}, f32[2,4,64,128]{3,2,1,0:T(8,128)S(1)}, u32[]{:S(2)}, u32[]{:S(2)}) collective-permute-start(f32[2,4,64,128]{3,2,1,0:T(8,128)S(1)} %get-tuple-element.50.far_rcv), channel_id=1, source_target_pairs={{0,4},{4,0},{8,12},{12,8},{16,20},{20,16},{24,28},{28,24},{1,5},{5... | collective-permute-start | bytes 786440 | tf_op jit(solution)/shard_map/ppermute | solution.py:415
  10.9 1.2 %collective-permute-done.2.halo = f32[464,128]{1,0:T(8,128)S(1)} collective-permute-done((f32[464,128]{1,0:T(8,128)S(1)}, f32[464,128]{1,0:T(8,128)S(1)}, u32[]{:S(2)}, u32[]{:S(2)}) %collective-permute-start.2) | collective-permute-done | bytes 237600 | tf_op jit(solution)/shard_map/ppermute | solution.py:420
  12.2 0.9 %first_step_near.1 = (f32[4,4,64,128]{3,2,1,0:T(8,128)S(1)}, f32[4,64,128]{2,1,0:T(8,128)S(1)}, f32[464,128]{1,0:T(8,128)S(1)}) custom-call(s32[2]{0:T(128)S(1)} %get-tuple-element.34.sy, s32[2]{0:T(128)S(1)} %get-tuple-element.35.sx, s32[2]{0:T(128)S(1)} %get-tuple-element.36.hy, s32[2]{0:T(128)S(1)} %get-tuple-element.37.hx, ...), custom_call_target="tpu_custom_call" | custom-call | flops 2097152 | bytes 67108864 | tf_op jit(solution)/shard_map/first_step_near/pallas_call | solution.py:487
  13.1 2.3 %collective-permute-start.3 = (f32[464,128]{1,0:T(8,128)S(1)}, f32[464,128]{1,0:T(8,128)S(1)}, u32[]{:S(2)}, u32[]{:S(2)}) collective-permute-start(f32[464,128]{1,0:T(8,128)S(1)} %get-tuple-element.55), channel_id=1, source_target_pairs={{0,28},{4,8},{8,4},{12,16},{16,12},{20,24},{24,20},{28,0},{1,29},{... | collective-permute-start | bytes 712712 | tf_op jit(solution)/shard_map/ppermute | solution.py:420
  15.4 0.0 collective-permute-done.4.halo_src
  15.4 0.0 collective-permute-done.5.halo_rcv
  15.4 1.4 %second_step_far.1 = (f32[4,4,64,128]{3,2,1,0:T(8,128)S(1)}, f32[4,64,128]{2,1,0:T(8,128)S(1)}) custom-call(s32[2]{0:T(128)S(1)} %get-tuple-element.34.sy, s32[2]{0:T(128)S(1)} %get-tuple-element.35.sx, s32[2]{0:T(128)S(1)} %get-tuple-element.36.hy, s32[2]{0:T(128)S(1)} %get-tuple-element.37.hx, s32[2]{0:T(128)S(1)} %get-tuple-element.38.depth, ...), custom_call_target="tpu_custom_call" | custom-call | flops 8388608 | bytes 16777216 | tf_op jit(solution)/shard_map/second_step_far/pallas_call | solution.py:499
  16.8 1.6 %collective-permute-start.6 = (f32[4,64,128]{2,1,0:T(8,128)S(1)}, f32[4,64,128]{2,1,0:T(8,128)S(1)}, u32[]{:S(2)}, u32[]{:S(2)}) collective-permute-start(f32[4,64,128]{2,1,0:T(8,128)S(1)} %get-tuple-element.58.far_a), channel_id=1, source_target_pairs={{0,1},{1,0},{2,3},{3,2},{4,5},{5,4},{6,7},{7,6},{8,9},{9,8},{10,11... | collective-permute-start | bytes 393224 | tf_op jit(solution)/shard_map/ppermute | solution.py:426
  18.4 1.0 %second_step_part.1 = (f32[4,4,64,128]{3,2,1,0:T(8,128)S(1)}, f32[2,4,64,128]{3,2,1,0:T(8,128)S(1)}) custom-call(s32[2]{0:T(128)S(1)} %get-tuple-element.34.sy, s32[2]{0:T(128)S(1)} %get-tuple-element.35.sx, s32[2]{0:T(128)S(1)} %get-tuple-element.38.depth, f32[2,2]{1,0:T(2,128)S(1)} %get-tuple-element.39.wave, ...), custom_call_target="tpu_custom_call" | custom-call | flops 8388608 | bytes 16777216 | tf_op jit(solution)/shard_map/second_step_part/pallas_call | solution.py:512
  19.5 2.4 %collective-permute-done.3.halo = f32[464,128]{1,0:T(8,128)S(1)} collective-permute-done((f32[464,128]{1,0:T(8,128)S(1)}, f32[464,128]{1,0:T(8,128)S(1)}, u32[]{:S(2)}, u32[]{:S(2)}) %collective-permute-start.3) | collective-permute-done | bytes 237600 | tf_op jit(solution)/shard_map/ppermute | solution.py:420
  21.8 0.0 collective-permute-done.6.far_b
  21.8 0.5 %second_step_near.1 = (f32[4,64,128]{2,1,0:T(8,128)S(1)}, f32[4,64,128]{2,1,0:T(8,128)S(1)}, f32[4,4,64,128]{3,2,1,0:T(8,128)S(1)}) custom-call(s32[2]{0:T(128)S(1)} %get-tuple-element.34.sy, s32[2]{0:T(128)S(1)} %get-tuple-element.35.sx, s32[2]{0:T(128)S(1)} %get-tuple-element.36.hy, s32[2]{0:T(128)S(1)} %get-tuple-element.37.hx, ...), custom_call_target="tpu_custom_call" | custom-call | flops 2097152 | bytes 2097152 | tf_op jit(solution)/shard_map/second_step_near/pallas_call | solution.py:523
  22.3 2.7 %collective-permute-start.7 = (f32[4,64,128]{2,1,0:T(8,128)S(1)}, f32[4,64,128]{2,1,0:T(8,128)S(1)}, u32[]{:S(2)}, u32[]{:S(2)}) collective-permute-start(f32[4,64,128]{2,1,0:T(8,128)S(1)} %get-tuple-element.63), channel_id=1, source_target_pairs={{0,1},{1,0},{2,3},{3,2},{4,5},{5,4},{6,7},{7,6},{8,9},{9,8},{10,11... | collective-permute-start | bytes 393224 | tf_op jit(solution)/shard_map/ppermute | solution.py:426
  25.0 2.5 %collective-permute-start.9 = (f32[4,64,128]{2,1,0:T(8,128)S(1)}, f32[4,64,128]{2,1,0:T(8,128)S(1)}, u32[]{:S(2)}, u32[]{:S(2)}) collective-permute-start(f32[4,64,128]{2,1,0:T(8,128)S(1)} %get-tuple-element.64.far_a), channel_id=1, source_target_pairs={{0,3},{1,2},{2,1},{3,0},{4,7},{5,6},{6,5},{7,4},{8,11},{9,10},{10,... | collective-permute-start | bytes 393224 | tf_op jit(solution)/shard_map/ppermute | solution.py:426
  27.4 1.9 %collective-permute-done.7 = f32[4,64,128]{2,1,0:T(8,128)S(1)} collective-permute-done((f32[4,64,128]{2,1,0:T(8,128)S(1)}, f32[4,64,128]{2,1,0:T(8,128)S(1)}, u32[]{:S(2)}, u32[]{:S(2)}) %collective-permute-start.7) | collective-permute-done | bytes 131104 | tf_op jit(solution)/shard_map/ppermute | solution.py:426
  29.4 2.7 %collective-permute-start.8 = (f32[4,64,128]{2,1,0:T(8,128)S(1)}, f32[4,64,128]{2,1,0:T(8,128)S(1)}, u32[]{:S(2)}, u32[]{:S(2)}) collective-permute-start(f32[4,64,128]{2,1,0:T(8,128)S(1)} %add.3.near_a), channel_id=1, source_target_pairs={{0,3},{1,2},{2,1},{3,0},{4,7},{5,6},{6,5},{7,4},{8,11},{9,10},{10,... | collective-permute-start | bytes 393224 | tf_op jit(solution)/shard_map/ppermute | solution.py:426
  32.1 1.0 %write_fields.1 = (f32[2,8,64,128]{3,2,1,0:T(8,128)}, f32[2,8,64,128]{3,2,1,0:T(8,128)}) custom-call(f32[4,4,64,128]{3,2,1,0:T(8,128)S(1)} %get-tuple-element.59.new_near, f32[4,4,64,128]{3,2,1,0:T(8,128)S(1)} %get-tuple-element.60.new_far), custom_call_target="tpu_custom_call" | custom-call | flops 1024 | bytes 4194304 | tf_op jit(solution)/shard_map/write_fields/pallas_call | solution.py:536
  33.1 0.2 collective-permute-done.9.far_b
  33.3 3.0 %collective-permute-done.8.near_b = f32[4,64,128]{2,1,0:T(8,128)S(1)} collective-permute-done((f32[4,64,128]{2,1,0:T(8,128)S(1)}, f32[4,64,128]{2,1,0:T(8,128)S(1)}, u32[]{:S(2)}, u32[]{:S(2)}) %collective-permute-start.8) | collective-permute-done | bytes 131104 | tf_op jit(solution)/shard_map/ppermute | solution.py:426
  36.3 0.7 %image_sum.1 = f32[8,64,128]{2,1,0:T(8,128)} custom-call(f32[4,64,128]{2,1,0:T(8,128)S(1)} %add.3.near_a, f32[4,64,128]{2,1,0:T(8,128)S(1)} %collective-permute-done.8.near_b, f32[4,64,128]{2,1,0:T(8,128)S(1)} %get-tuple-element.64.far_a, f32[4,64,128]{2,1,0:T(8,128)S(1)} %collective-permute-done.9.far_b), custom_call_target="tpu_custom_call" | custom-call | flops 131072 | bytes 1048576 | tf_op jit(solution)/shard_map/image_sum/pallas_call | solution.py:547
  (1 shorter events, 0.0 us)
Async XLA Ops:
  2.5 4.2 %collective-permute-start = (f32[2,4,64,128]{3,2,1,0:T(8,128)S(1)}, f32[2,4,64,128]{3,2,1,0:T(8,128)S(1)}, u32[]{:S(2)}, u32[]{:S(2)}) collective-permute-start(f32[2,4,64,128]{3,2,1,0:T(8,128)S(1)} %get-tuple-element.41.far_src), channel_id=1, source_target_pairs={{0,4},{4,0},{8,12},{12,8},{16,20},{20,16},{24,28},{28,24},{1,5},{5... | collective-permute-start | bytes 786440 | tf_op jit(solution)/shard_map/ppermute | solution.py:415
  3.0 3.6 %collective-permute-start.1 = (f32[2,4,64,128]{3,2,1,0:T(8,128)S(1)}, f32[2,4,64,128]{3,2,1,0:T(8,128)S(1)}, u32[]{:S(2)}, u32[]{:S(2)}) collective-permute-start(f32[2,4,64,128]{3,2,1,0:T(8,128)S(1)} %get-tuple-element.42.far_rcv), channel_id=1, source_target_pairs={{0,4},{4,0},{8,12},{12,8},{16,20},{20,16},{24,28},{28,24},{1,5},{5... | collective-permute-start | bytes 786440 | tf_op jit(solution)/shard_map/ppermute | solution.py:415
  3.1 9.1 %collective-permute-start.2 = (f32[464,128]{1,0:T(8,128)S(1)}, f32[464,128]{1,0:T(8,128)S(1)}, u32[]{:S(2)}, u32[]{:S(2)}) collective-permute-start(f32[464,128]{1,0:T(8,128)S(1)} %get-tuple-element.46), channel_id=1, source_target_pairs={{0,28},{4,8},{8,4},{12,16},{16,12},{20,24},{24,20},{28,0},{1,29},{... | collective-permute-start | bytes 712712 | tf_op jit(solution)/shard_map/ppermute | solution.py:420
  6.6 0.7 %copy-start = (f32[2,2,256]{2,1,0:T(2,128)S(1)}, f32[2,2,256]{2,1,0:T(2,128)}, u32[]{:S(2)}) copy-start(f32[2,2,256]{2,1,0:T(2,128)} %traces.1) | copy-start | bytes 12292
  6.6 0.7 %copy-start.1 = (s32[2,256]{1,0:T(2,128)S(1)}, s32[2,256]{1,0:T(2,128)}, u32[]{:S(2)}) copy-start(s32[2,256]{1,0:T(2,128)} %cells.1) | copy-start | bytes 6148
  10.4 5.0 %collective-permute-start.4 = (f32[2,4,64,128]{3,2,1,0:T(8,128)S(1)}, f32[2,4,64,128]{3,2,1,0:T(8,128)S(1)}, u32[]{:S(2)}, u32[]{:S(2)}) collective-permute-start(f32[2,4,64,128]{3,2,1,0:T(8,128)S(1)} %get-tuple-element.49.far_src), channel_id=1, source_target_pairs={{0,4},{4,0},{8,12},{12,8},{16,20},{20,16},{24,28},{28,24},{1,5},{5... | collective-permute-start | bytes 786440 | tf_op jit(solution)/shard_map/ppermute | solution.py:415
  10.4 5.0 %collective-permute-start.5 = (f32[2,4,64,128]{3,2,1,0:T(8,128)S(1)}, f32[2,4,64,128]{3,2,1,0:T(8,128)S(1)}, u32[]{:S(2)}, u32[]{:S(2)}) collective-permute-start(f32[2,4,64,128]{3,2,1,0:T(8,128)S(1)} %get-tuple-element.50.far_rcv), channel_id=1, source_target_pairs={{0,4},{4,0},{8,12},{12,8},{16,20},{20,16},{24,28},{28,24},{1,5},{5... | collective-permute-start | bytes 786440 | tf_op jit(solution)/shard_map/ppermute | solution.py:415
  13.1 8.7 %collective-permute-start.3 = (f32[464,128]{1,0:T(8,128)S(1)}, f32[464,128]{1,0:T(8,128)S(1)}, u32[]{:S(2)}, u32[]{:S(2)}) collective-permute-start(f32[464,128]{1,0:T(8,128)S(1)} %get-tuple-element.55), channel_id=1, source_target_pairs={{0,28},{4,8},{8,4},{12,16},{16,12},{20,24},{24,20},{28,0},{1,29},{... | collective-permute-start | bytes 712712 | tf_op jit(solution)/shard_map/ppermute | solution.py:420
  16.8 5.0 %collective-permute-start.6 = (f32[4,64,128]{2,1,0:T(8,128)S(1)}, f32[4,64,128]{2,1,0:T(8,128)S(1)}, u32[]{:S(2)}, u32[]{:S(2)}) collective-permute-start(f32[4,64,128]{2,1,0:T(8,128)S(1)} %get-tuple-element.58.far_a), channel_id=1, source_target_pairs={{0,1},{1,0},{2,3},{3,2},{4,5},{5,4},{6,7},{7,6},{8,9},{9,8},{10,11... | collective-permute-start | bytes 393224 | tf_op jit(solution)/shard_map/ppermute | solution.py:426
  22.3 7.1 %collective-permute-start.7 = (f32[4,64,128]{2,1,0:T(8,128)S(1)}, f32[4,64,128]{2,1,0:T(8,128)S(1)}, u32[]{:S(2)}, u32[]{:S(2)}) collective-permute-start(f32[4,64,128]{2,1,0:T(8,128)S(1)} %get-tuple-element.63), channel_id=1, source_target_pairs={{0,1},{1,0},{2,3},{3,2},{4,5},{5,4},{6,7},{7,6},{8,9},{9,8},{10,11... | collective-permute-start | bytes 393224 | tf_op jit(solution)/shard_map/ppermute | solution.py:426
  25.0 8.3 %collective-permute-start.9 = (f32[4,64,128]{2,1,0:T(8,128)S(1)}, f32[4,64,128]{2,1,0:T(8,128)S(1)}, u32[]{:S(2)}, u32[]{:S(2)}) collective-permute-start(f32[4,64,128]{2,1,0:T(8,128)S(1)} %get-tuple-element.64.far_a), channel_id=1, source_target_pairs={{0,3},{1,2},{2,1},{3,0},{4,7},{5,6},{6,5},{7,4},{8,11},{9,10},{10,... | collective-permute-start | bytes 393224 | tf_op jit(solution)/shard_map/ppermute | solution.py:426
  29.4 6.9 %collective-permute-start.8 = (f32[4,64,128]{2,1,0:T(8,128)S(1)}, f32[4,64,128]{2,1,0:T(8,128)S(1)}, u32[]{:S(2)}, u32[]{:S(2)}) collective-permute-start(f32[4,64,128]{2,1,0:T(8,128)S(1)} %add.3.near_a), channel_id=1, source_target_pairs={{0,3},{1,2},{2,1},{3,0},{4,7},{5,6},{6,5},{7,4},{8,11},{9,10},{10,... | collective-permute-start | bytes 393224 | tf_op jit(solution)/shard_map/ppermute | solution.py:426

commit v3 on v2

--- a/solution.py
+++ b/solution.py
@@ -17,6 +17,7 @@
 SCALE = 5040.0
 MARGIN = 8
 
+SPARE = 16
 VMEM = pl.BlockSpec(memory_space=pltpu.VMEM)
 ANY = pl.BlockSpec(memory_space=pl.ANY)
 HBM = pl.BlockSpec(memory_space=pltpu.HBM)
@@ -52,15 +53,19 @@
     return (jnp.abs(sublanes(shape) - sy) <= hy) & (jnp.abs(lanes(shape) - sx) <= hx)
 
 
+def inside_columns(col0, shape):
+    lane = lanes(shape)
+    return (lane >= col0) & (lane < col0 + WIN_X)
+
+
 def pack(planes, f, i, row0, col0):
-    cols = planes.shape[3]
-    main = pltpu.roll(planes[f, i, pl.ds(row0, 32), :], cols - col0, 1)
-    left = pltpu.roll(planes[f, i, pl.ds(row0 + PACK, 16), :], lax.rem(WIN_X - col0 + cols, cols), 1)
-    right = pltpu.roll(planes[f, i, pl.ds(row0 + PACK - REST + 8, 24), :], lax.rem(HALF_X - col0 + cols, cols), 1)
+    main = planes[f, i, pl.ds(row0, 32), :]
+    left = pltpu.roll(planes[f, i, pl.ds(row0 + PACK, 16), :], WIN_X, 1)
+    right = pltpu.roll(planes[f, i, pl.ds(row0 + PACK - REST + 8, 24), :], HALF_X, 1)
     left = jnp.concatenate([left, right[8:]], 0)
     right = jnp.concatenate([right[:8], right], 0)
     spare = jnp.where(sublanes(main.shape) < REST, left, right)
-    return jnp.where(lanes(main.shape) < WIN_X, main, spare)
+    return jnp.where(inside_columns(col0, main.shape), main, spare)
 
 
 def pack_field(planes, f, out, scal, par):
@@ -78,9 +83,9 @@
         col0 = scal[1][f % 2] - HALF_X
         for e in range(R):
             n = (f * R + e) * PACK
-            planes[f, e, pl.ds(row0, PACK), :] = pltpu.roll(packed[pl.ds(n, PACK), :], col0, 1)
-            left = pltpu.roll(packed[pl.ds(n, REST), :], lax.rem(col0 + cols - WIN_X, cols), 1)
-            right = pltpu.roll(packed[pl.ds(n + REST, REST), :], lax.rem(col0 + cols - HALF_X, cols), 1)
+            planes[f, e, pl.ds(row0, PACK), :] = packed[pl.ds(n, PACK), :]
+            left = pltpu.roll(packed[pl.ds(n, REST), :], cols - WIN_X, 1)
+            right = pltpu.roll(packed[pl.ds(n + REST, REST), :], cols - HALF_X, 1)
             rest = jnp.where(lanes(left.shape) < col0 + (cols - WIN_X), left, right)
             planes[f, e, pl.ds(row0 + PACK, REST), :] = rest
 
@@ -98,22 +103,22 @@
 
 
 def pack_kernel(*refs):
-    scal_in, (src, rcv, out), scal, (planes, far_src, far_rcv, sems) = refs[:6], refs[6:9], refs[9:15], refs[15:]
+    small_in, (src, rcv, out), small, (planes, far_raw, sems) = refs[:8], refs[8:11], refs[11:19], refs[19:]
     near, far = halves()
     rows = src.shape[2]
-    pairs = list(zip(scal_in, scal))
+    pairs = []
     for f in range(4):
         ref = (src, rcv)[f // 2].at[f % 2]
         pairs.append((ref.at[pl.ds(near, R)], planes.at[f, :, pl.ds(0, rows), :]))
-    for ref, far_ref in ((src, far_src), (rcv, far_rcv)):
-        pairs.append((ref.at[:, pl.ds(far, R)], far_ref))
+    pairs += list(zip(small_in, small))
+    for n, ref in enumerate((src, rcv)):
+        pairs.append((ref.at[:, pl.ds(far, R)], far_raw.at[pl.ds(2 * n, 2)]))
     copies = copies_of(pairs, sems)
     planes[:, :, rows:, :] = jnp.zeros((4, R, MARGIN, planes.shape[3]), jnp.float32)
     wait(copies[:6])
     for f in range(4):
-        wait(copies[6 + f : 7 + f])
-        pack_field(planes, f, out, scal, parity())
-    wait(copies[10:])
+        pack_field(planes, f, out, small[:2], parity())
+    wait(copies[6:])
 
 
 def band_matrix(out):
@@ -239,8 +244,8 @@
 
 
 def first_kernel(
-    sy, sx, hy, hx, depth, wave, planes,
-    far_src, far_rcv, halo_src, halo_rcv, src_prev, rcv_prev, vel_in, cells, traces,
+    sy, sx, hy, hx, depth, wave, cells, traces, planes, far_raw, halo_raw,
+    src_prev, rcv_prev, vel_in,
     src_out, rcv_out, far_image, near_part, near_twice, near_vel, before, vel, later,
     cur, prev, delta, matrix, xs_near, xs_far, sems,
 ):
@@ -257,12 +262,11 @@
         (near_raw, cur.at[:, pl.ds(R + near, R), inner, :]),
         (near_raw, before.at[:, pl.ds(near, R)]),
     ]
-    for own, other, n in ((far_src, halo_src, 0), (far_rcv, halo_rcv, 1)):
-        pairs += [
-            (own, cur.at[fields[n], pl.ds(R + far, R), inner, :]),
-            (own, before.at[fields[n], pl.ds(far, R)]),
-            (other, cur.at[fields[n], pl.ds(halo, R), inner, :]),
-        ]
+    pairs += [
+        (far_raw, cur.at[:, pl.ds(R + far, R), inner, :]),
+        (far_raw, before.at[:, pl.ds(far, R)]),
+        (halo_raw, cur.at[:, pl.ds(halo, R), inner, :]),
+    ]
     pairs.append((vel_in, vel))
     for first in (near, far):
         for ref, n in ((src_prev, 0), (rcv_prev, 1)):
@@ -271,10 +275,10 @@
     clear(cur, (layers + R) * par)
     band_matrix(matrix)
     inject(cells, traces, base, (delta, later))
-    wait(copies[:8])
+    wait(copies[:5])
     x_part(cur, near, matrix, xs_near)
     x_part(cur, far, matrix, xs_far)
-    wait(copies[8:11])
+    wait(copies[5:8])
     has = jnp.where((base == 0) | (lax.axis_index("slab") == lax.axis_size("slab") - 1), 0.0, 1.0)
     near_vel[...] = vel[pl.ds(near, R)] * has
 
@@ -283,7 +287,7 @@
         step_half(first, refs, scal, wave, depth, 0, base, write)
 
     half_step(near, xs_near, writer_near(near_part, near_twice))
-    wait(copies[11:])
+    wait(copies[8:])
     half_step(far, xs_far, writer_far(scal, src_out, rcv_out, far_image, None))
 
 
@@ -310,25 +314,24 @@
     planes,
 ):
     scal = (sy, sx, hy, hx)
+    rows = vel.shape[1]
+    near_out[:, :, rows:, :] = jnp.zeros((4, R, MARGIN, planes.shape[3]), jnp.float32)
 
     def write(s, i, new, term):
-        near_out[s, i] = new[0]
-        near_out[2 + s, i] = new[1]
+        near_out[s, i, pl.ds(0, rows), :] = new[0]
+        near_out[2 + s, i, pl.ds(0, rows), :] = new[1]
         near_image[i] = term if s == 0 else near_image[i] + term
 
     finish_near(scal, part, twice, halo, vel, planes, write)
-    rows = vel.shape[1]
-    planes[:, :, pl.ds(0, rows), :] = near_out[...]
-    planes[:, :, rows:, :] = jnp.zeros((4, R, MARGIN, planes.shape[3]), jnp.float32)
     for f in range(4):
-        pack_field(planes, f, packed, scal, parity())
+        pack_field(near_out, f, packed, scal, parity())
 
 
 def second_far_kernel(
     sy, sx, hy, hx, depth, wave,
     before, near_cur, far_src, far_rcv, halo_src, halo_rcv, vel, delta, image_before,
-    new_far, image,
-    cur, matrix, xs, sems,
+    new_far, image_out,
+    image, cur, matrix, xs, sems,
 ):
     scal = (sy, sx, hy, hx)
     par = parity()
@@ -341,7 +344,7 @@
     copies = copies_of([
         (far_src, cur.at[src, own, inner, :]),
         (far_rcv, cur.at[rcv, own, inner, :]),
-        (near_cur, cur.at[:, pl.ds(R + near, R), inner, :]),
+        (near_cur.at[:, :, pl.ds(0, rows), :], cur.at[:, pl.ds(R + near, R), inner, :]),
         (halo_src, cur.at[src, halo, inner, :]),
         (halo_rcv, cur.at[rcv, halo, inner, :]),
     ], sems)
@@ -352,6 +355,10 @@
     refs = (cur, before.at[:, pl.ds(far, R)], vel.at[pl.ds(far, R)], delta.at[:, pl.ds(far, R)], xs)
     write = writer_far(scal, new_far.at[src], new_far.at[rcv], image, image_before)
     step_half(far, refs, scal, wave, depth, 1, base, write)
+    used = R * rows
+    image_out[:used] = image[...].reshape(used, image.shape[2])
+    if image_out.shape[0] > used:
+        image_out[used:] = jnp.zeros((image_out.shape[0] - used, image.shape[2]), jnp.float32)
 
 
 def second_near_kernel(
@@ -367,7 +374,7 @@
     base = lax.axis_index("slab") * layers
     inner = pl.ds(MARGIN, rows)
     copies = copies_of([
-        (near_cur, cur.at[:, pl.ds(R + near, R), inner, :]),
+        (near_cur.at[:, :, pl.ds(0, rows), :], cur.at[:, pl.ds(R + near, R), inner, :]),
         (far_src, cur.at[pl.ds(0, 2), pl.ds(R + far, R), inner, :]),
         (far_rcv, cur.at[pl.ds(2, 2), pl.ds(R + far, R), inner, :]),
     ], sems)
@@ -380,12 +387,11 @@
 
 
 def last_kernel(
-    sy, sx, hy, hx, part, twice, halo, vel, near_image, far_a, far_b,
-    image, far_sum, new_near,
+    sy, sx, hy, hx, part, twice, halo, vel, near_image,
+    image, new_near,
     planes,
 ):
     scal = (sy, sx, hy, hx)
-    far_sum[...] = far_a[...] + far_b[...]
 
     def write(s, i, new, term):
         new_near[s, i] = new[0]
@@ -407,7 +413,8 @@
 def image_kernel(near_a, near_b, far_a, far_b, out):
     near, far = halves()
     out[pl.ds(near, R)] = near_a[...] + near_b[...]
-    out[pl.ds(far, R)] = far_a[...] + far_b[...]
+    used = R * out.shape[1]
+    out[pl.ds(far, R)] = (far_a[:used] + far_b[:used]).reshape(R, *out.shape[1:])
 
 
 def swap_a(block):
@@ -426,12 +433,13 @@
     return lax.ppermute(block, "shots", [(i, i ^ flip) for i in range(count)])
 
 
-def shot_rounds(block, turn):
-    other = swap_shots(block, turn)
-    while 2 ** (turn + 1) < lax.axis_size("shots"):
-        turn += 1
+def shot_rounds(block, turns):
+    other = swap_shots(block, turns[0])
+    turn = turns[1]
+    while 2**turn < lax.axis_size("shots"):
         block = block + other
         other = swap_shots(block, turn)
+        turn += 1
     return block, other
 
 
@@ -445,13 +453,15 @@
     src_prev, src_cur, rcv_prev, rcv_cur, velocity = (
         in_hbm(x) for x in (src_prev, src_cur, rcv_prev, rcv_cur, velocity)
     )
-    scal_hbm = [
-        in_hbm(x) for x in (source_y, source_x, half_y, half_x, source_depth, wavelet)
+    small_hbm = [
+        in_hbm(x)
+        for x in (source_y, source_x, half_y, half_x, source_depth, wavelet, receiver_cell, residual_traces)
     ]
     shape = jax.ShapeDtypeStruct
     half4 = shape((4, R, rows, cols), f32)
     half2 = shape((2, R, rows, cols), f32)
     half1 = shape((R, rows, cols), f32)
+    far_block = shape((R * rows + SPARE, cols), f32)
     packed = shape((4 * R * PACK, cols), f32)
     dma = lambda n: pltpu.SemaphoreType.DMA((n,))
     planes = (4, R, rows + MARGIN, cols)
@@ -459,34 +469,35 @@
     matrix = pltpu.VMEM((3 * cols, cols), jnp.bfloat16)
     xs = pltpu.VMEM((4, R, rows, cols), f32)
 
-    to_b, *scal, near_raw, far_src, far_rcv = pl.pallas_call(
+    to_b, *small, near_raw, far_raw = pl.pallas_call(
         pack_kernel,
-        out_shape=(packed, *(shape(x.shape, x.dtype) for x in scal_hbm), shape(planes, f32), half2, half2),
-        in_specs=[HBM] * 8,
-        out_specs=(VMEM,) * 10,
-        scratch_shapes=[dma(12)],
+        out_shape=(packed, *(shape(x.shape, x.dtype) for x in small_hbm), shape(planes, f32), half4),
+        in_specs=[HBM] * 10,
+        out_specs=(VMEM,) * 11,
+        scratch_shapes=[dma(14)],
         compiler_params=params(),
         cost_estimate=cost(1 << 20, 1 << 20),
         name="pack_halo",
-    )(*scal_hbm, src_cur, rcv_cur)
+    )(*small_hbm, src_cur, rcv_cur)
     from_b = swap_b(to_b)
-    halo_src, halo_rcv = swap_a(far_src), swap_a(far_rcv)
+    halo_raw = swap_a(far_raw)
+    scal = small[:6]
 
     far_src, far_rcv, far_image, near_part, near_twice, near_vel, before, vel, later = pl.pallas_call(
         first_kernel,
         out_shape=(half2, half2, half1, half4, half2, half1, shape((4, layers, rows, cols), f32), shape(velocity.shape, f32), shape((2, layers, rows, cols), f32)),
-        in_specs=[VMEM] * 9 + [ANY] * 2 + [HBM] * 3 + [VMEM, VMEM],
+        in_specs=[VMEM] * 10 + [ANY] + [HBM] * 3,
         out_specs=(VMEM,) * 9,
         scratch_shapes=[state, pltpu.VMEM((4, layers, rows, cols), f32), pltpu.VMEM((2, layers, rows, cols), f32), matrix, xs, xs, dma(13)],
         compiler_params=params(),
         cost_estimate=cost(1 << 24, 1 << 25),
         name="first_step",
-    )(*scal, near_raw, far_src, far_rcv, halo_src, halo_rcv, src_prev, rcv_prev, velocity, receiver_cell, residual_traces)
+    )(*small, near_raw, far_raw, halo_raw, src_prev, rcv_prev, velocity)
     halo_src, halo_rcv = swap_a(far_src), swap_a(far_rcv)
 
     near_cur, near_image, to_b = pl.pallas_call(
         middle_kernel,
-        out_shape=(half4, half1, packed),
+        out_shape=(shape(planes, f32), half1, packed),
         in_specs=[VMEM] * 8,
         out_specs=(VMEM,) * 3,
         scratch_shapes=[pltpu.VMEM(planes, f32)],
@@ -498,15 +509,15 @@
 
     new_far, far_image = pl.pallas_call(
         second_far_kernel,
-        out_shape=(half4, half1),
+        out_shape=(half4, far_block),
         in_specs=[VMEM] * 7 + [ANY] * 5 + [VMEM] * 3,
         out_specs=(VMEM, VMEM),
-        scratch_shapes=[state, matrix, xs, dma(5)],
+        scratch_shapes=[pltpu.VMEM((R, rows, cols), f32), state, matrix, xs, dma(5)],
         compiler_params=params(),
         cost_estimate=cost(1 << 23, 1 << 24),
         name="second_step_far",
     )(*scal, before, near_cur, far_src, far_rcv, halo_src, halo_rcv, vel, later, far_image)
-    far_other = swap_shots(far_image, 0)
+    far_other = swap_shots(far_image, 1)
 
 
     near_part, near_twice = pl.pallas_call(
@@ -520,18 +531,21 @@
         name="second_step_part",
     )(scal[0], scal[1], scal[4], scal[5], before, near_cur, far_src, far_rcv, vel, later)
 
-    near_image, far_image, new_near = pl.pallas_call(
+    near_image, new_near = pl.pallas_call(
         last_kernel,
-        out_shape=(half1, half1, half4),
-        in_specs=[VMEM] * 11,
-        out_specs=(VMEM,) * 3,
+        out_shape=(half1, half4),
+        in_specs=[VMEM] * 9,
+        out_specs=(VMEM,) * 2,
         scratch_shapes=[pltpu.VMEM(planes, f32)],
         compiler_params=params(),
         cost_estimate=cost(1 << 21, 1 << 21),
         name="second_step_near",
-    )(*scal[:4], near_part, near_twice, from_b, near_vel, near_image, far_image, far_other)
-    near_a, near_b = shot_rounds(near_image, 0)
-    far_a, far_b = shot_rounds(far_image, 1)
+    )(*scal[:4], near_part, near_twice, from_b, near_vel, near_image)
+    near_other = swap_shots(near_image, 0)
+    near_image = near_image + near_other
+    far_image = far_image + far_other
+    near_a, near_b = shot_rounds(near_image, (1, 2))
+    far_a, far_b = shot_rounds(far_image, (0, 2))
 
     src_last, rcv_last = pl.pallas_call(
         write_kernel,

time: 37.3 us -> 35.4 us (0.949)
  Pallas kernels: 10.4 us -> 9.45 us
  local copies, waits for them, and re-layouts: 0.69 us -> 0 us
  waiting for transfers between devices: 8.74 us -> 8.07 us
  starting transfers between devices: 16.5 us -> 16.9 us
    ppermute x4, starting transfers between devices: 9.5 us -> 10.4 us  [swap_shots(): return lax.ppermute(block, 'shots', [(i, i ^ flip) for i in range(count)])]
    ppermute x2, waiting for transfers between devices: 3.59 us -> 2.81 us  [swap_b(): lax.ppermute(block, 'slab', [(i, (i + 1 ^ 1) - 1 if 0 < i < count - 1 els...]
    unnamed x4 -> x0, local copies, waits for them, and re-layouts: 0.69 us -> none
    pallas_call x3, Pallas kernels: 2.77 us -> 2.21 us  [the longest x1 1.36 us: per_device(): pl.pallas_call(second_far_kernel, out_shape=(half4, far_block), in_specs=...]
    ppermute x4 -> x3, starting transfers between devices: 1.16 us -> 1.09 us  [swap_a(): return lax.ppermute(block, 'slab', [(i, i ^ 1) for i in range(count)])]
  transfers between devices with their start and end apart: 10 -> 9, of which waited for: 5 -> 4; matrix products, arithmetic and copies ran while one was open for 0% -> 0% of each run, Pallas kernels for 20% -> 20%
where the time goes in v3:
time: 35.4 us; the launch traced here: 35.2 us
  starting transfers between devices  16.9 us (48%)
  Pallas kernels  9.45 us (27%)
  waiting for transfers between devices  8.07 us (23%)
  between operations  0.71 us (2%)
    ppermute x4, starting transfers between devices, swap_shots(): return lax.ppermute(block, 'shots', [(i, i ^ flip) for i in range(count)])  10.4 us
    ppermute x2, starting transfers between devices, swap_b(): lax.ppermute(block, 'slab', [(i, (i + 1 ^ 1) - 1 if 0 < i < count - 1 els...  5.5 us
    ppermute x4, waiting for transfers between devices, swap_shots(): return lax.ppermute(block, 'shots', [(i, i ^ flip) for i in range(count)])  5.25 us
    pallas_call x1, Pallas kernels, per_device(): pl.pallas_call(first_kernel, out_shape=(half2, half2, half1, half4, half2...  3.02 us
    ppermute x2, waiting for transfers between devices, swap_b(): lax.ppermute(block, 'slab', [(i, (i + 1 ^ 1) - 1 if 0 < i < count - 1 els...  2.81 us
    pallas_call x1, Pallas kernels, per_device(): pl.pallas_call(pack_kernel, out_shape=(packed, *(shape(x.shape, x.dtype)...  1.52 us
    pallas_call x1, Pallas kernels, per_device(): pl.pallas_call(second_far_kernel, out_shape=(half4, far_block), in_specs=...  1.36 us
    ppermute x3, starting transfers between devices, swap_a(): return lax.ppermute(block, 'slab', [(i, i ^ 1) for i in range(count)])  1.09 us
  transfers between devices with their start and end apart: 9, of which 4 were waited for; matrix products, arithmetic and copies ran while one was open for 0% of the time, Pallas kernels for 20%

profile of v3, /device:TPU:0, one launch (start us, length us, event | category | flops | bytes accessed | tf_op | source)
XLA Modules:
  0.0 35.2 jit_solution(14635839214069915062)
XLA Ops:
  0.6 1.5 %pack_halo.1 = (f32[464,128]{1,0:T(8,128)S(1)}, s32[2]{0:T(128)S(1)}, s32[2]{0:T(128)S(1)}, s32[2]{0:T(128)S(1)}, s32[2]{0:T(128)S(1)}, /*index=5*/s32[2]{0:T(12...) custom-call(s32[2]{0:T(128)} %refs_0_.1, ...), custom_call_target="tpu_custom_call" | custom-call | flops 1048576 | bytes 1048576 | tf_op jit(solution)/shard_map/pack_halo/pallas_call | solution.py:472
  2.2 0.5 %collective-permute-start = (f32[4,4,64,128]{3,2,1,0:T(8,128)S(1)}, f32[4,4,64,128]{3,2,1,0:T(8,128)S(1)}, u32[]{:S(2)}, u32[]{:S(2)}) collective-permute-start(f32[4,4,64,128]{3,2,1,0:T(8,128)S(1)} %get-tuple-element.43.far_raw), channel_id=1, source_target_pairs={{0,4},{4,0},{8,12},{12,8},{16,20},{20,16},{24,28},{28,24},{1,5},{5... | collective-permute-start | bytes 1572872 | tf_op jit(solution)/shard_map/ppermute | solution.py:422
  2.7 3.6 %collective-permute-start.1 = (f32[464,128]{1,0:T(8,128)S(1)}, f32[464,128]{1,0:T(8,128)S(1)}, u32[]{:S(2)}, u32[]{:S(2)}) collective-permute-start(f32[464,128]{1,0:T(8,128)S(1)} %get-tuple-element.47), channel_id=1, source_target_pairs={{0,28},{4,8},{8,4},{12,16},{16,12},{20,24},{24,20},{28,0},{1,29},{... | collective-permute-start | bytes 712712 | tf_op jit(solution)/shard_map/ppermute | solution.py:427
  6.2 0.0 collective-permute-done.halo_raw
  6.2 3.0 %first_step.1 = (f32[2,4,64,128]{3,2,1,0:T(8,128)S(1)}, f32[2,4,64,128]{3,2,1,0:T(8,128)S(1)}, f32[4,64,128]{2,1,0:T(8,128)S(1)}, f32[4,4,64,128]{3,2,1,0:T(8,12...) custom-call(s32[2]{0:T(128)S(1)} %get-tuple-element.34.sy, ...), custom_call_target="tpu_custom_call" | custom-call | flops 16777216 | bytes 33554432 | tf_op jit(solution)/shard_map/first_step/pallas_call | solution.py:486
  9.3 0.1 collective-permute-start.3
  9.3 0.5 %collective-permute-start.4 = (f32[2,4,64,128]{3,2,1,0:T(8,128)S(1)}, f32[2,4,64,128]{3,2,1,0:T(8,128)S(1)}, u32[]{:S(2)}, u32[]{:S(2)}) collective-permute-start(f32[2,4,64,128]{3,2,1,0:T(8,128)S(1)} %get-tuple-element.51.far_rcv), channel_id=1, source_target_pairs={{0,4},{4,0},{8,12},{12,8},{16,20},{20,16},{24,28},{28,24},{1,5},{5... | collective-permute-start | bytes 786440 | tf_op jit(solution)/shard_map/ppermute | solution.py:422
  9.8 1.9 %collective-permute-done.1.halo = f32[464,128]{1,0:T(8,128)S(1)} collective-permute-done((f32[464,128]{1,0:T(8,128)S(1)}, f32[464,128]{1,0:T(8,128)S(1)}, u32[]{:S(2)}, u32[]{:S(2)}) %collective-permute-start.1) | collective-permute-done | bytes 237600 | tf_op jit(solution)/shard_map/ppermute | solution.py:427
  11.8 0.5 %first_step_near.1 = (f32[4,4,72,128]{3,2,1,0:T(8,128)S(1)}, f32[4,64,128]{2,1,0:T(8,128)S(1)}, f32[464,128]{1,0:T(8,128)S(1)}) custom-call(s32[2]{0:T(128)S(1)} %get-tuple-element.34.sy, s32[2]{0:T(128)S(1)} %get-tuple-element.35.sx, s32[2]{0:T(128)S(1)} %get-tuple-element.36.hy, s32[2]{0:T(128)S(1)} %get-tuple-element.37.hx, ...), custom_call_target="tpu_custom_call" | custom-call | flops 2097152 | bytes 67108864 | tf_op jit(solution)/shard_map/first_step_near/pallas_call | solution.py:498
  12.3 1.9 %collective-permute-start.2 = (f32[464,128]{1,0:T(8,128)S(1)}, f32[464,128]{1,0:T(8,128)S(1)}, u32[]{:S(2)}, u32[]{:S(2)}) collective-permute-start(f32[464,128]{1,0:T(8,128)S(1)} %get-tuple-element.56), channel_id=1, source_target_pairs={{0,28},{4,8},{8,4},{12,16},{16,12},{20,24},{24,20},{28,0},{1,29},{... | collective-permute-start | bytes 712712 | tf_op jit(solution)/shard_map/ppermute | solution.py:427
  14.2 0.0 collective-permute-done.3.halo_src
  14.2 0.0 collective-permute-done.4.halo_rcv
  14.2 1.4 %second_step_far.1 = (f32[4,4,64,128]{3,2,1,0:T(8,128)S(1)}, f32[272,128]{1,0:T(8,128)S(1)}) custom-call(s32[2]{0:T(128)S(1)} %get-tuple-element.34.sy, s32[2]{0:T(128)S(1)} %get-tuple-element.35.sx, s32[2]{0:T(128)S(1)} %get-tuple-element.36.hy, s32[2]{0:T(128)S(1)} %get-tuple-element.37.hx, s32[2]{0:T(128)S(1)} %get-tuple-element.38.depth, ...), custom_call_target="tpu_custom_call" | custom-call | flops 8388608 | bytes 16777216 | tf_op jit(solution)/shard_map/second_step_far/pallas_call | solution.py:510
  15.6 3.7 %collective-permute-start.7 = (f32[272,128]{1,0:T(8,128)S(1)}, f32[272,128]{1,0:T(8,128)S(1)}, u32[]{:S(2)}, u32[]{:S(2)}) collective-permute-start(f32[272,128]{1,0:T(8,128)S(1)} %get-tuple-element.64), channel_id=1, source_target_pairs={{0,3},{1,2},{2,1},{3,0},{4,7},{5,6},{6,5},{7,4},{8,11},{9,10},{10,... | collective-permute-start | bytes 417800 | tf_op jit(solution)/shard_map/ppermute | solution.py:433
  19.3 1.0 %second_step_part.1 = (f32[4,4,64,128]{3,2,1,0:T(8,128)S(1)}, f32[2,4,64,128]{3,2,1,0:T(8,128)S(1)}) custom-call(s32[2]{0:T(128)S(1)} %get-tuple-element.34.sy, s32[2]{0:T(128)S(1)} %get-tuple-element.35.sx, s32[2]{0:T(128)S(1)} %get-tuple-element.38.depth, f32[2,2]{1,0:T(2,128)S(1)} %get-tuple-element.39.wave, ...), custom_call_target="tpu_custom_call" | custom-call | flops 8388608 | bytes 16777216 | tf_op jit(solution)/shard_map/second_step_part/pallas_call | solution.py:523
  20.3 0.9 %collective-permute-done.2.halo = f32[464,128]{1,0:T(8,128)S(1)} collective-permute-done((f32[464,128]{1,0:T(8,128)S(1)}, f32[464,128]{1,0:T(8,128)S(1)}, u32[]{:S(2)}, u32[]{:S(2)}) %collective-permute-start.2) | collective-permute-done | bytes 237600 | tf_op jit(solution)/shard_map/ppermute | solution.py:427
  21.1 0.3 second_step_near.1
  21.5 2.2 %collective-permute-start.5 = (f32[4,64,128]{2,1,0:T(8,128)S(1)}, f32[4,64,128]{2,1,0:T(8,128)S(1)}, u32[]{:S(2)}, u32[]{:S(2)}) collective-permute-start(f32[4,64,128]{2,1,0:T(8,128)S(1)} %get-tuple-element.63), channel_id=1, source_target_pairs={{0,1},{1,0},{2,3},{3,2},{4,5},{5,4},{6,7},{7,6},{8,9},{9,8},{10,11... | collective-permute-start | bytes 393224 | tf_op jit(solution)/shard_map/ppermute | solution.py:433
  23.6 0.0 collective-permute-done.7
  23.7 0.8 %collective-permute-start.8 = (f32[272,128]{1,0:T(8,128)S(1)}, f32[272,128]{1,0:T(8,128)S(1)}, u32[]{:S(2)}, u32[]{:S(2)}) collective-permute-start(f32[272,128]{1,0:T(8,128)S(1)} %add.7.far_a), channel_id=1, source_target_pairs={{0,1},{1,0},{2,3},{3,2},{4,5},{5,4},{6,7},{7,6},{8,9},{9,8},{10,11... | collective-permute-start | bytes 417800 | tf_op jit(solution)/shard_map/ppermute | solution.py:433
  24.5 3.0 %collective-permute-done.5 = f32[4,64,128]{2,1,0:T(8,128)S(1)} collective-permute-done((f32[4,64,128]{2,1,0:T(8,128)S(1)}, f32[4,64,128]{2,1,0:T(8,128)S(1)}, u32[]{:S(2)}, u32[]{:S(2)}) %collective-permute-start.5) | collective-permute-done | bytes 131104 | tf_op jit(solution)/shard_map/ppermute | solution.py:433
  27.5 3.7 %collective-permute-start.6 = (f32[4,64,128]{2,1,0:T(8,128)S(1)}, f32[4,64,128]{2,1,0:T(8,128)S(1)}, u32[]{:S(2)}, u32[]{:S(2)}) collective-permute-start(f32[4,64,128]{2,1,0:T(8,128)S(1)} %add.6.near_a), channel_id=1, source_target_pairs={{0,3},{1,2},{2,1},{3,0},{4,7},{5,6},{6,5},{7,4},{8,11},{9,10},{10,... | collective-permute-start | bytes 393224 | tf_op jit(solution)/shard_map/ppermute | solution.py:433
  31.2 1.0 %write_fields.1 = (f32[2,8,64,128]{3,2,1,0:T(8,128)}, f32[2,8,64,128]{3,2,1,0:T(8,128)}) custom-call(f32[4,4,64,128]{3,2,1,0:T(8,128)S(1)} %get-tuple-element.58.new_near, f32[4,4,64,128]{3,2,1,0:T(8,128)S(1)} %get-tuple-element.60.new_far), custom_call_target="tpu_custom_call" | custom-call | flops 1024 | bytes 4194304 | tf_op jit(solution)/shard_map/write_fields/pallas_call | solution.py:550
  32.2 2.2 %collective-permute-done.6.near_b = f32[4,64,128]{2,1,0:T(8,128)S(1)} collective-permute-done((f32[4,64,128]{2,1,0:T(8,128)S(1)}, f32[4,64,128]{2,1,0:T(8,128)S(1)}, u32[]{:S(2)}, u32[]{:S(2)}) %collective-permute-start.6) | collective-permute-done | bytes 131104 | tf_op jit(solution)/shard_map/ppermute | solution.py:433
  34.5 0.0 collective-permute-done.8.far_b
  34.5 0.7 %image_sum.1 = f32[8,64,128]{2,1,0:T(8,128)} custom-call(f32[4,64,128]{2,1,0:T(8,128)S(1)} %add.6.near_a, f32[4,64,128]{2,1,0:T(8,128)S(1)} %collective-permute-done.6.near_b, f32[272,128]{1,0:T(8,128)S(1)} %add.7.far_a, f32[272,128]{1,0:T(8,128)S(1)} %collective-permute-done.8.far_b), custom_call_target="tpu_custom_call" | custom-call | flops 131072 | bytes 1048576 | tf_op jit(solution)/shard_map/image_sum/pallas_call | solution.py:561
  (2 shorter events, 0.0 us)
Async XLA Ops:
  2.2 4.1 %collective-permute-start = (f32[4,4,64,128]{3,2,1,0:T(8,128)S(1)}, f32[4,4,64,128]{3,2,1,0:T(8,128)S(1)}, u32[]{:S(2)}, u32[]{:S(2)}) collective-permute-start(f32[4,4,64,128]{3,2,1,0:T(8,128)S(1)} %get-tuple-element.43.far_raw), channel_id=1, source_target_pairs={{0,4},{4,0},{8,12},{12,8},{16,20},{20,16},{24,28},{28,24},{1,5},{5... | collective-permute-start | bytes 1572872 | tf_op jit(solution)/shard_map/ppermute | solution.py:422
  2.7 9.1 %collective-permute-start.1 = (f32[464,128]{1,0:T(8,128)S(1)}, f32[464,128]{1,0:T(8,128)S(1)}, u32[]{:S(2)}, u32[]{:S(2)}) collective-permute-start(f32[464,128]{1,0:T(8,128)S(1)} %get-tuple-element.47), channel_id=1, source_target_pairs={{0,28},{4,8},{8,4},{12,16},{16,12},{20,24},{24,20},{28,0},{1,29},{... | collective-permute-start | bytes 712712 | tf_op jit(solution)/shard_map/ppermute | solution.py:427
  9.3 5.0 %collective-permute-start.3 = (f32[2,4,64,128]{3,2,1,0:T(8,128)S(1)}, f32[2,4,64,128]{3,2,1,0:T(8,128)S(1)}, u32[]{:S(2)}, u32[]{:S(2)}) collective-permute-start(f32[2,4,64,128]{3,2,1,0:T(8,128)S(1)} %get-tuple-element.50.far_src), channel_id=1, source_target_pairs={{0,4},{4,0},{8,12},{12,8},{16,20},{20,16},{24,28},{28,24},{1,5},{5... | collective-permute-start | bytes 786440 | tf_op jit(solution)/shard_map/ppermute | solution.py:422
  9.3 4.9 %collective-permute-start.4 = (f32[2,4,64,128]{3,2,1,0:T(8,128)S(1)}, f32[2,4,64,128]{3,2,1,0:T(8,128)S(1)}, u32[]{:S(2)}, u32[]{:S(2)}) collective-permute-start(f32[2,4,64,128]{3,2,1,0:T(8,128)S(1)} %get-tuple-element.51.far_rcv), channel_id=1, source_target_pairs={{0,4},{4,0},{8,12},{12,8},{16,20},{20,16},{24,28},{28,24},{1,5},{5... | collective-permute-start | bytes 786440 | tf_op jit(solution)/shard_map/ppermute | solution.py:422
  12.3 8.8 %collective-permute-start.2 = (f32[464,128]{1,0:T(8,128)S(1)}, f32[464,128]{1,0:T(8,128)S(1)}, u32[]{:S(2)}, u32[]{:S(2)}) collective-permute-start(f32[464,128]{1,0:T(8,128)S(1)} %get-tuple-element.56), channel_id=1, source_target_pairs={{0,28},{4,8},{8,4},{12,16},{16,12},{20,24},{24,20},{28,0},{1,29},{... | collective-permute-start | bytes 712712 | tf_op jit(solution)/shard_map/ppermute | solution.py:427
  15.6 8.0 %collective-permute-start.7 = (f32[272,128]{1,0:T(8,128)S(1)}, f32[272,128]{1,0:T(8,128)S(1)}, u32[]{:S(2)}, u32[]{:S(2)}) collective-permute-start(f32[272,128]{1,0:T(8,128)S(1)} %get-tuple-element.64), channel_id=1, source_target_pairs={{0,3},{1,2},{2,1},{3,0},{4,7},{5,6},{6,5},{7,4},{8,11},{9,10},{10,... | collective-permute-start | bytes 417800 | tf_op jit(solution)/shard_map/ppermute | solution.py:433
  21.5 6.0 %collective-permute-start.5 = (f32[4,64,128]{2,1,0:T(8,128)S(1)}, f32[4,64,128]{2,1,0:T(8,128)S(1)}, u32[]{:S(2)}, u32[]{:S(2)}) collective-permute-start(f32[4,64,128]{2,1,0:T(8,128)S(1)} %get-tuple-element.63), channel_id=1, source_target_pairs={{0,1},{1,0},{2,3},{3,2},{4,5},{5,4},{6,7},{7,6},{8,9},{9,8},{10,11... | collective-permute-start | bytes 393224 | tf_op jit(solution)/shard_map/ppermute | solution.py:433
  23.7 10.8 %collective-permute-start.8 = (f32[272,128]{1,0:T(8,128)S(1)}, f32[272,128]{1,0:T(8,128)S(1)}, u32[]{:S(2)}, u32[]{:S(2)}) collective-permute-start(f32[272,128]{1,0:T(8,128)S(1)} %add.7.far_a), channel_id=1, source_target_pairs={{0,1},{1,0},{2,3},{3,2},{4,5},{5,4},{6,7},{7,6},{8,9},{9,8},{10,11... | collective-permute-start | bytes 417800 | tf_op jit(solution)/shard_map/ppermute | solution.py:433
  27.5 6.9 %collective-permute-start.6 = (f32[4,64,128]{2,1,0:T(8,128)S(1)}, f32[4,64,128]{2,1,0:T(8,128)S(1)}, u32[]{:S(2)}, u32[]{:S(2)}) collective-permute-start(f32[4,64,128]{2,1,0:T(8,128)S(1)} %add.6.near_a), channel_id=1, source_target_pairs={{0,3},{1,2},{2,1},{3,0},{4,7},{5,6},{6,5},{7,4},{8,11},{9,10},{10,... | collective-permute-start | bytes 393224 | tf_op jit(solution)/shard_map/ppermute | solution.py:433

commit v4 on v3

--- a/solution.py
+++ b/solution.py
@@ -423,8 +423,13 @@
 
 
 def swap_b(block):
-    count = lax.axis_size("slab")
-    return lax.ppermute(block, "slab", [(i, ((i + 1) ^ 1) - 1 if 0 < i < count - 1 else count - 1 - i) for i in range(count)])
+    count, groups = lax.axis_size("slab"), lax.axis_size("shots")
+    pairs = []
+    for i in range(count):
+        for g in range(groups):
+            to = (i, g ^ 1) if i in (0, count - 1) else (((i + 1) ^ 1) - 1, g)
+            pairs.append((i * groups + g, to[0] * groups + to[1]))
+    return lax.ppermute(block, ("slab", "shots"), pairs)
 
 
 def swap_shots(block, turn):

time: 35.4 us -> 33.8 us (0.955)
  starting transfers between devices: 16.9 us -> 14.6 us
  waiting for transfers between devices: 8.07 us -> 8.84 us
    ppermute x4, waiting for transfers between devices: 5.25 us -> 8.34 us  [swap_shots(): return lax.ppermute(block, 'shots', [(i, i ^ flip) for i in range(count)])]
    ppermute x2, waiting for transfers between devices: 2.81 us -> 0.49 us  [swap_b(): return lax.ppermute(block, ('slab', 'shots'), pairs)]
    ppermute x4, starting transfers between devices: 10.4 us -> 8.79 us  [swap_shots(): return lax.ppermute(block, 'shots', [(i, i ^ flip) for i in range(count)])]
    ppermute x2, starting transfers between devices: 5.5 us -> 4.73 us  [swap_b(): return lax.ppermute(block, ('slab', 'shots'), pairs)]
  transfers between devices with their start and end apart: 9 -> 9, of which waited for: 4 -> 3; matrix products, arithmetic and copies ran while one was open for 0% -> 0% of each run, Pallas kernels for 20% -> 21%
where the time goes in v4:
time: 33.8 us; the launch traced here: 33.7 us
  starting transfers between devices  14.6 us (43%)
  Pallas kernels  9.46 us (28%)
  waiting for transfers between devices  8.84 us (26%)
  between operations  0.71 us (2%)
    ppermute x4, starting transfers between devices, swap_shots(): return lax.ppermute(block, 'shots', [(i, i ^ flip) for i in range(count)])  8.79 us
    ppermute x4, waiting for transfers between devices, swap_shots(): return lax.ppermute(block, 'shots', [(i, i ^ flip) for i in range(count)])  8.34 us
    ppermute x2, starting transfers between devices, swap_b(): return lax.ppermute(block, ('slab', 'shots'), pairs)  4.73 us
    pallas_call x1, Pallas kernels, per_device(): pl.pallas_call(first_kernel, out_shape=(half2, half2, half1, half4, half2...  3.02 us
    pallas_call x1, Pallas kernels, per_device(): pl.pallas_call(pack_kernel, out_shape=(packed, *(shape(x.shape, x.dtype)...  1.52 us
    pallas_call x1, Pallas kernels, per_device(): pl.pallas_call(second_far_kernel, out_shape=(half4, far_block), in_specs=...  1.36 us
    ppermute x3, starting transfers between devices, swap_a(): return lax.ppermute(block, 'slab', [(i, i ^ 1) for i in range(count)])  1.09 us
    pallas_call x1, Pallas kernels, per_device(): pl.pallas_call(write_kernel, out_shape=(shape(src_cur.shape, f32),) * 2,...  0.99 us
  transfers between devices with their start and end apart: 9, of which 3 were waited for; matrix products, arithmetic and copies ran while one was open for 0% of the time, Pallas kernels for 21%

profile of v4, /device:TPU:0, one launch (start us, length us, event | category | flops | bytes accessed | tf_op | source)
XLA Modules:
  0.0 33.7 jit_solution(6681422051761115167)
XLA Ops:
  0.6 1.5 %pack_halo.1 = (f32[464,128]{1,0:T(8,128)S(1)}, s32[2]{0:T(128)S(1)}, s32[2]{0:T(128)S(1)}, s32[2]{0:T(128)S(1)}, s32[2]{0:T(128)S(1)}, /*index=5*/s32[2]{0:T(12...) custom-call(s32[2]{0:T(128)} %refs_0_.1, ...), custom_call_target="tpu_custom_call" | custom-call | flops 1048576 | bytes 1048576 | tf_op jit(solution)/shard_map/pack_halo/pallas_call | solution.py:477
  2.2 0.5 %collective-permute-start = (f32[4,4,64,128]{3,2,1,0:T(8,128)S(1)}, f32[4,4,64,128]{3,2,1,0:T(8,128)S(1)}, u32[]{:S(2)}, u32[]{:S(2)}) collective-permute-start(f32[4,4,64,128]{3,2,1,0:T(8,128)S(1)} %get-tuple-element.43.far_raw), channel_id=1, source_target_pairs={{0,4},{4,0},{8,12},{12,8},{16,20},{20,16},{24,28},{28,24},{1,5},{5... | collective-permute-start | bytes 1572872 | tf_op jit(solution)/shard_map/ppermute | solution.py:422
  2.7 2.6 %collective-permute-start.1 = (f32[464,128]{1,0:T(8,128)S(1)}, f32[464,128]{1,0:T(8,128)S(1)}, u32[]{:S(2)}, u32[]{:S(2)}) collective-permute-start(f32[464,128]{1,0:T(8,128)S(1)} %get-tuple-element.47), channel_id=1, source_target_pairs={{0,1},{1,0},{2,3},{3,2},{4,8},{5,9},{6,10},{7,11},{8,4},{9,5},{10,... | collective-permute-start | bytes 712712 | tf_op jit(solution)/shard_map/ppermute | solution.py:432
  5.3 0.0 collective-permute-done.halo_raw
  5.3 3.0 %first_step.1 = (f32[2,4,64,128]{3,2,1,0:T(8,128)S(1)}, f32[2,4,64,128]{3,2,1,0:T(8,128)S(1)}, f32[4,64,128]{2,1,0:T(8,128)S(1)}, f32[4,4,64,128]{3,2,1,0:T(8,12...) custom-call(s32[2]{0:T(128)S(1)} %get-tuple-element.34.sy, ...), custom_call_target="tpu_custom_call" | custom-call | flops 16777216 | bytes 33554432 | tf_op jit(solution)/shard_map/first_step/pallas_call | solution.py:491
  8.4 0.1 collective-permute-start.3
  8.5 0.5 %collective-permute-start.4 = (f32[2,4,64,128]{3,2,1,0:T(8,128)S(1)}, f32[2,4,64,128]{3,2,1,0:T(8,128)S(1)}, u32[]{:S(2)}, u32[]{:S(2)}) collective-permute-start(f32[2,4,64,128]{3,2,1,0:T(8,128)S(1)} %get-tuple-element.51.far_rcv), channel_id=1, source_target_pairs={{0,4},{4,0},{8,12},{12,8},{16,20},{20,16},{24,28},{28,24},{1,5},{5... | collective-permute-start | bytes 786440 | tf_op jit(solution)/shard_map/ppermute | solution.py:422
  8.9 0.5 %collective-permute-done.1.halo = f32[464,128]{1,0:T(8,128)S(1)} collective-permute-done((f32[464,128]{1,0:T(8,128)S(1)}, f32[464,128]{1,0:T(8,128)S(1)}, u32[]{:S(2)}, u32[]{:S(2)}) %collective-permute-start.1) | collective-permute-done | bytes 237600 | tf_op jit(solution)/shard_map/ppermute | solution.py:432
  9.4 0.5 %first_step_near.1 = (f32[4,4,72,128]{3,2,1,0:T(8,128)S(1)}, f32[4,64,128]{2,1,0:T(8,128)S(1)}, f32[464,128]{1,0:T(8,128)S(1)}) custom-call(s32[2]{0:T(128)S(1)} %get-tuple-element.34.sy, s32[2]{0:T(128)S(1)} %get-tuple-element.35.sx, s32[2]{0:T(128)S(1)} %get-tuple-element.36.hy, s32[2]{0:T(128)S(1)} %get-tuple-element.37.hx, ...), custom_call_target="tpu_custom_call" | custom-call | flops 2097152 | bytes 67108864 | tf_op jit(solution)/shard_map/first_step_near/pallas_call | solution.py:503
  9.9 2.1 %collective-permute-start.2 = (f32[464,128]{1,0:T(8,128)S(1)}, f32[464,128]{1,0:T(8,128)S(1)}, u32[]{:S(2)}, u32[]{:S(2)}) collective-permute-start(f32[464,128]{1,0:T(8,128)S(1)} %get-tuple-element.56), channel_id=1, source_target_pairs={{0,1},{1,0},{2,3},{3,2},{4,8},{5,9},{6,10},{7,11},{8,4},{9,5},{10,... | collective-permute-start | bytes 712712 | tf_op jit(solution)/shard_map/ppermute | solution.py:432
  12.0 0.0 collective-permute-done.3.halo_src
  12.0 0.0 collective-permute-done.4.halo_rcv
  12.0 1.4 %second_step_far.1 = (f32[4,4,64,128]{3,2,1,0:T(8,128)S(1)}, f32[272,128]{1,0:T(8,128)S(1)}) custom-call(s32[2]{0:T(128)S(1)} %get-tuple-element.34.sy, s32[2]{0:T(128)S(1)} %get-tuple-element.35.sx, s32[2]{0:T(128)S(1)} %get-tuple-element.36.hy, s32[2]{0:T(128)S(1)} %get-tuple-element.37.hx, s32[2]{0:T(128)S(1)} %get-tuple-element.38.depth, ...), custom_call_target="tpu_custom_call" | custom-call | flops 8388608 | bytes 16777216 | tf_op jit(solution)/shard_map/second_step_far/pallas_call | solution.py:515
  13.4 2.5 %collective-permute-start.7 = (f32[272,128]{1,0:T(8,128)S(1)}, f32[272,128]{1,0:T(8,128)S(1)}, u32[]{:S(2)}, u32[]{:S(2)}) collective-permute-start(f32[272,128]{1,0:T(8,128)S(1)} %get-tuple-element.64), channel_id=1, source_target_pairs={{0,3},{1,2},{2,1},{3,0},{4,7},{5,6},{6,5},{7,4},{8,11},{9,10},{10,... | collective-permute-start | bytes 417800 | tf_op jit(solution)/shard_map/ppermute | solution.py:438
  15.9 1.0 %second_step_part.1 = (f32[4,4,64,128]{3,2,1,0:T(8,128)S(1)}, f32[2,4,64,128]{3,2,1,0:T(8,128)S(1)}) custom-call(s32[2]{0:T(128)S(1)} %get-tuple-element.34.sy, s32[2]{0:T(128)S(1)} %get-tuple-element.35.sx, s32[2]{0:T(128)S(1)} %get-tuple-element.38.depth, f32[2,2]{1,0:T(2,128)S(1)} %get-tuple-element.39.wave, ...), custom_call_target="tpu_custom_call" | custom-call | flops 8388608 | bytes 16777216 | tf_op jit(solution)/shard_map/second_step_part/pallas_call | solution.py:528
  16.9 0.0 collective-permute-done.2.halo
  16.9 0.3 %second_step_near.1 = (f32[4,64,128]{2,1,0:T(8,128)S(1)}, f32[4,4,64,128]{3,2,1,0:T(8,128)S(1)}) custom-call(s32[2]{0:T(128)S(1)} %get-tuple-element.34.sy, s32[2]{0:T(128)S(1)} %get-tuple-element.35.sx, s32[2]{0:T(128)S(1)} %get-tuple-element.36.hy, s32[2]{0:T(128)S(1)} %get-tuple-element.37.hx, f32[4,4,64,128]{3,2,1,0:T(8,128)S(1)} %get-tuple-element.54.part, ...), custom_call_target="tpu_custom_call" | custom-call | flops 2097152 | bytes 2097152 | tf_op jit(solution)/shard_map/second_step_near/pallas_call | solution.py:539
  17.3 1.3 %collective-permute-start.5 = (f32[4,64,128]{2,1,0:T(8,128)S(1)}, f32[4,64,128]{2,1,0:T(8,128)S(1)}, u32[]{:S(2)}, u32[]{:S(2)}) collective-permute-start(f32[4,64,128]{2,1,0:T(8,128)S(1)} %get-tuple-element.63), channel_id=1, source_target_pairs={{0,1},{1,0},{2,3},{3,2},{4,5},{5,4},{6,7},{7,6},{8,9},{9,8},{10,11... | collective-permute-start | bytes 393224 | tf_op jit(solution)/shard_map/ppermute | solution.py:438
  18.5 3.2 %collective-permute-done.7 = f32[272,128]{1,0:T(8,128)S(1)} collective-permute-done((f32[272,128]{1,0:T(8,128)S(1)}, f32[272,128]{1,0:T(8,128)S(1)}, u32[]{:S(2)}, u32[]{:S(2)}) %collective-permute-start.7) | collective-permute-done | bytes 139296 | tf_op jit(solution)/shard_map/ppermute | solution.py:438
  21.8 2.4 %collective-permute-start.8 = (f32[272,128]{1,0:T(8,128)S(1)}, f32[272,128]{1,0:T(8,128)S(1)}, u32[]{:S(2)}, u32[]{:S(2)}) collective-permute-start(f32[272,128]{1,0:T(8,128)S(1)} %add.7.far_a), channel_id=1, source_target_pairs={{0,1},{1,0},{2,3},{3,2},{4,5},{5,4},{6,7},{7,6},{8,9},{9,8},{10,11... | collective-permute-start | bytes 417800 | tf_op jit(solution)/shard_map/ppermute | solution.py:438
  24.2 0.0 collective-permute-done.5
  24.2 2.5 %collective-permute-start.6 = (f32[4,64,128]{2,1,0:T(8,128)S(1)}, f32[4,64,128]{2,1,0:T(8,128)S(1)}, u32[]{:S(2)}, u32[]{:S(2)}) collective-permute-start(f32[4,64,128]{2,1,0:T(8,128)S(1)} %add.6.near_a), channel_id=1, source_target_pairs={{0,3},{1,2},{2,1},{3,0},{4,7},{5,6},{6,5},{7,4},{8,11},{9,10},{10,... | collective-permute-start | bytes 393224 | tf_op jit(solution)/shard_map/ppermute | solution.py:438
  26.8 1.0 %write_fields.1 = (f32[2,8,64,128]{3,2,1,0:T(8,128)}, f32[2,8,64,128]{3,2,1,0:T(8,128)}) custom-call(f32[4,4,64,128]{3,2,1,0:T(8,128)S(1)} %get-tuple-element.58.new_near, f32[4,4,64,128]{3,2,1,0:T(8,128)S(1)} %get-tuple-element.60.new_far), custom_call_target="tpu_custom_call" | custom-call | flops 1024 | bytes 4194304 | tf_op jit(solution)/shard_map/write_fields/pallas_call | solution.py:555
  27.8 5.1 %collective-permute-done.6.near_b = f32[4,64,128]{2,1,0:T(8,128)S(1)} collective-permute-done((f32[4,64,128]{2,1,0:T(8,128)S(1)}, f32[4,64,128]{2,1,0:T(8,128)S(1)}, u32[]{:S(2)}, u32[]{:S(2)}) %collective-permute-start.6) | collective-permute-done | bytes 131104 | tf_op jit(solution)/shard_map/ppermute | solution.py:438
  32.9 0.0 collective-permute-done.8.far_b
  32.9 0.7 %image_sum.1 = f32[8,64,128]{2,1,0:T(8,128)} custom-call(f32[4,64,128]{2,1,0:T(8,128)S(1)} %add.6.near_a, f32[4,64,128]{2,1,0:T(8,128)S(1)} %collective-permute-done.6.near_b, f32[272,128]{1,0:T(8,128)S(1)} %add.7.far_a, f32[272,128]{1,0:T(8,128)S(1)} %collective-permute-done.8.far_b), custom_call_target="tpu_custom_call" | custom-call | flops 131072 | bytes 1048576 | tf_op jit(solution)/shard_map/image_sum/pallas_call | solution.py:566
  (2 shorter events, 0.0 us)
Async XLA Ops:
  2.2 3.2 %collective-permute-start = (f32[4,4,64,128]{3,2,1,0:T(8,128)S(1)}, f32[4,4,64,128]{3,2,1,0:T(8,128)S(1)}, u32[]{:S(2)}, u32[]{:S(2)}) collective-permute-start(f32[4,4,64,128]{3,2,1,0:T(8,128)S(1)} %get-tuple-element.43.far_raw), channel_id=1, source_target_pairs={{0,4},{4,0},{8,12},{12,8},{16,20},{20,16},{24,28},{28,24},{1,5},{5... | collective-permute-start | bytes 1572872 | tf_op jit(solution)/shard_map/ppermute | solution.py:422
  2.7 6.7 %collective-permute-start.1 = (f32[464,128]{1,0:T(8,128)S(1)}, f32[464,128]{1,0:T(8,128)S(1)}, u32[]{:S(2)}, u32[]{:S(2)}) collective-permute-start(f32[464,128]{1,0:T(8,128)S(1)} %get-tuple-element.47), channel_id=1, source_target_pairs={{0,1},{1,0},{2,3},{3,2},{4,8},{5,9},{6,10},{7,11},{8,4},{9,5},{10,... | collective-permute-start | bytes 712712 | tf_op jit(solution)/shard_map/ppermute | solution.py:432
  8.4 3.7 %collective-permute-start.3 = (f32[2,4,64,128]{3,2,1,0:T(8,128)S(1)}, f32[2,4,64,128]{3,2,1,0:T(8,128)S(1)}, u32[]{:S(2)}, u32[]{:S(2)}) collective-permute-start(f32[2,4,64,128]{3,2,1,0:T(8,128)S(1)} %get-tuple-element.50.far_src), channel_id=1, source_target_pairs={{0,4},{4,0},{8,12},{12,8},{16,20},{20,16},{24,28},{28,24},{1,5},{5... | collective-permute-start | bytes 786440 | tf_op jit(solution)/shard_map/ppermute | solution.py:422
  8.5 3.6 %collective-permute-start.4 = (f32[2,4,64,128]{3,2,1,0:T(8,128)S(1)}, f32[2,4,64,128]{3,2,1,0:T(8,128)S(1)}, u32[]{:S(2)}, u32[]{:S(2)}) collective-permute-start(f32[2,4,64,128]{3,2,1,0:T(8,128)S(1)} %get-tuple-element.51.far_rcv), channel_id=1, source_target_pairs={{0,4},{4,0},{8,12},{12,8},{16,20},{20,16},{24,28},{28,24},{1,5},{5... | collective-permute-start | bytes 786440 | tf_op jit(solution)/shard_map/ppermute | solution.py:422
  9.9 7.0 %collective-permute-start.2 = (f32[464,128]{1,0:T(8,128)S(1)}, f32[464,128]{1,0:T(8,128)S(1)}, u32[]{:S(2)}, u32[]{:S(2)}) collective-permute-start(f32[464,128]{1,0:T(8,128)S(1)} %get-tuple-element.56), channel_id=1, source_target_pairs={{0,1},{1,0},{2,3},{3,2},{4,8},{5,9},{6,10},{7,11},{8,4},{9,5},{10,... | collective-permute-start | bytes 712712 | tf_op jit(solution)/shard_map/ppermute | solution.py:432
  13.4 8.4 %collective-permute-start.7 = (f32[272,128]{1,0:T(8,128)S(1)}, f32[272,128]{1,0:T(8,128)S(1)}, u32[]{:S(2)}, u32[]{:S(2)}) collective-permute-start(f32[272,128]{1,0:T(8,128)S(1)} %get-tuple-element.64), channel_id=1, source_target_pairs={{0,3},{1,2},{2,1},{3,0},{4,7},{5,6},{6,5},{7,4},{8,11},{9,10},{10,... | collective-permute-start | bytes 417800 | tf_op jit(solution)/shard_map/ppermute | solution.py:438
  17.3 6.9 %collective-permute-start.5 = (f32[4,64,128]{2,1,0:T(8,128)S(1)}, f32[4,64,128]{2,1,0:T(8,128)S(1)}, u32[]{:S(2)}, u32[]{:S(2)}) collective-permute-start(f32[4,64,128]{2,1,0:T(8,128)S(1)} %get-tuple-element.63), channel_id=1, source_target_pairs={{0,1},{1,0},{2,3},{3,2},{4,5},{5,4},{6,7},{7,6},{8,9},{9,8},{10,11... | collective-permute-start | bytes 393224 | tf_op jit(solution)/shard_map/ppermute | solution.py:438
  21.8 11.1 %collective-permute-start.8 = (f32[272,128]{1,0:T(8,128)S(1)}, f32[272,128]{1,0:T(8,128)S(1)}, u32[]{:S(2)}, u32[]{:S(2)}) collective-permute-start(f32[272,128]{1,0:T(8,128)S(1)} %add.7.far_a), channel_id=1, source_target_pairs={{0,1},{1,0},{2,3},{3,2},{4,5},{5,4},{6,7},{7,6},{8,9},{9,8},{10,11... | collective-permute-start | bytes 417800 | tf_op jit(solution)/shard_map/ppermute | solution.py:438
  24.2 8.7 %collective-permute-start.6 = (f32[4,64,128]{2,1,0:T(8,128)S(1)}, f32[4,64,128]{2,1,0:T(8,128)S(1)}, u32[]{:S(2)}, u32[]{:S(2)}) collective-permute-start(f32[4,64,128]{2,1,0:T(8,128)S(1)} %add.6.near_a), channel_id=1, source_target_pairs={{0,3},{1,2},{2,1},{3,0},{4,7},{5,6},{6,5},{7,4},{8,11},{9,10},{10,... | collective-permute-start | bytes 393224 | tf_op jit(solution)/shard_map/ppermute | solution.py:438

commit v5 on v4

--- a/solution.py
+++ b/solution.py
@@ -13,6 +13,7 @@
 HALF_Y, HALF_X = 21, 42
 WIN_Y, WIN_X = 2 * HALF_Y + 1, 2 * HALF_X + 1
 PACK = 29
+TAIL = 8
 REST = WIN_Y - PACK
 SCALE = 5040.0
 MARGIN = 8
@@ -69,6 +70,8 @@
 
 
 def pack_field(planes, f, out, scal, par):
+    if f == 0:
+        out[4 * R * PACK :] = jnp.zeros((TAIL, out.shape[1]), jnp.float32)
     row0 = scal[0][f % 2] - HALF_Y
     col0 = scal[1][f % 2] - HALF_X
     for d in range(R):
@@ -432,18 +435,22 @@
     return lax.ppermute(block, ("slab", "shots"), pairs)
 
 
-def swap_shots(block, turn):
-    flip = 2 ** (turn + 1) - 1
-    count = lax.axis_size("shots")
-    return lax.ppermute(block, "shots", [(i, i ^ flip) for i in range(count)])
-
-
-def shot_rounds(block, turns):
-    other = swap_shots(block, turns[0])
-    turn = turns[1]
+def swap_shots(block, turn, inner):
+    count, groups = lax.axis_size("slab"), lax.axis_size("shots")
+    pairs = []
+    for i in range(count):
+        is_inner = (i % 2 == 1) != (i >= count // 2)
+        flip = 2 ** ((inner if is_inner else turn) + 1) - 1
+        pairs += [(i * groups + g, i * groups + (g ^ flip)) for g in range(groups)]
+    return lax.ppermute(block, ("slab", "shots"), pairs)
+
+
+def shot_rounds(block, turn, inner):
+    other = swap_shots(block, turn, inner)
+    turn = 2
     while 2**turn < lax.axis_size("shots"):
         block = block + other
-        other = swap_shots(block, turn)
+        other = swap_shots(block, turn, turn)
         turn += 1
     return block, other
 
@@ -467,7 +474,7 @@
     half2 = shape((2, R, rows, cols), f32)
     half1 = shape((R, rows, cols), f32)
     far_block = shape((R * rows + SPARE, cols), f32)
-    packed = shape((4 * R * PACK, cols), f32)
+    packed = shape((4 * R * PACK + TAIL, cols), f32)
     dma = lambda n: pltpu.SemaphoreType.DMA((n,))
     planes = (4, R, rows + MARGIN, cols)
     state = pltpu.VMEM((4, layers + 2 * R, rows + 2 * MARGIN, cols), f32)
@@ -522,7 +529,7 @@
         cost_estimate=cost(1 << 23, 1 << 24),
         name="second_step_far",
     )(*scal, before, near_cur, far_src, far_rcv, halo_src, halo_rcv, vel, later, far_image)
-    far_other = swap_shots(far_image, 1)
+    far_other = swap_shots(far_image, 1, 1)
 
 
     near_part, near_twice = pl.pallas_call(
@@ -546,11 +553,11 @@
         cost_estimate=cost(1 << 21, 1 << 21),
         name="second_step_near",
     )(*scal[:4], near_part, near_twice, from_b, near_vel, near_image)
-    near_other = swap_shots(near_image, 0)
+    near_other = swap_shots(near_image, 0, 1)
     near_image = near_image + near_other
     far_image = far_image + far_other
-    near_a, near_b = shot_rounds(near_image, (1, 2))
-    far_a, far_b = shot_rounds(far_image, (0, 2))
+    near_a, near_b = shot_rounds(near_image, 1, 0)
+    far_a, far_b = shot_rounds(far_image, 0, 0)
 
     src_last, rcv_last = pl.pallas_call(
         write_kernel,

time: 33.8 us -> 33.5 us (level)
  waiting for transfers between devices: 8.84 us -> 8.46 us
    ppermute x4, waiting for transfers between devices: 8.34 us -> 7.92 us  [swap_shots(): return lax.ppermute(block, ('slab', 'shots'), pairs)]
  transfers between devices with their start and end apart: 9 -> 9, of which waited for: 3 -> 3; matrix products, arithmetic and copies ran while one was open for 0% -> 0% of each run, Pallas kernels for 21% -> 22%
where the time goes in v5:
time: 33.5 us; the launch traced here: 33.3 us
  starting transfers between devices  14.6 us (44%)
  Pallas kernels  9.46 us (28%)
  waiting for transfers between devices  8.46 us (25%)
  between operations  0.7 us (2%)
    ppermute x4, starting transfers between devices, swap_shots(): return lax.ppermute(block, ('slab', 'shots'), pairs)  8.82 us
    ppermute x4, waiting for transfers between devices, swap_shots(): return lax.ppermute(block, ('slab', 'shots'), pairs)  7.92 us
    ppermute x2, starting transfers between devices, swap_b(): return lax.ppermute(block, ('slab', 'shots'), pairs)  4.73 us
    pallas_call x1, Pallas kernels, per_device(): pl.pallas_call(first_kernel, out_shape=(half2, half2, half1, half4, half2...  3.02 us
    pallas_call x1, Pallas kernels, per_device(): pl.pallas_call(pack_kernel, out_shape=(packed, *(shape(x.shape, x.dtype)...  1.52 us
    pallas_call x1, Pallas kernels, per_device(): pl.pallas_call(second_far_kernel, out_shape=(half4, far_block), in_specs=...  1.36 us
    ppermute x3, starting transfers between devices, swap_a(): return lax.ppermute(block, 'slab', [(i, i ^ 1) for i in range(count)])  1.09 us
    pallas_call x1, Pallas kernels, per_device(): pl.pallas_call(write_kernel, out_shape=(shape(src_cur.shape, f32),) * 2,...  0.99 us
  transfers between devices with their start and end apart: 9, of which 3 were waited for; matrix products, arithmetic and copies ran while one was open for 0% of the time, Pallas kernels for 22%

profile of v5, /device:TPU:0, one launch (start us, length us, event | category | flops | bytes accessed | tf_op | source)
XLA Modules:
  0.0 33.3 jit_solution(3656582715013294066)
XLA Ops:
  0.6 1.5 %pack_halo.1 = (f32[472,128]{1,0:T(8,128)S(1)}, s32[2]{0:T(128)S(1)}, s32[2]{0:T(128)S(1)}, s32[2]{0:T(128)S(1)}, s32[2]{0:T(128)S(1)}, /*index=5*/s32[2]{0:T(12...) custom-call(s32[2]{0:T(128)} %refs_0_.1, ...), custom_call_target="tpu_custom_call" | custom-call | flops 1048576 | bytes 1048576 | tf_op jit(solution)/shard_map/pack_halo/pallas_call | solution.py:484
  2.2 0.5 %collective-permute-start = (f32[4,4,64,128]{3,2,1,0:T(8,128)S(1)}, f32[4,4,64,128]{3,2,1,0:T(8,128)S(1)}, u32[]{:S(2)}, u32[]{:S(2)}) collective-permute-start(f32[4,4,64,128]{3,2,1,0:T(8,128)S(1)} %get-tuple-element.43.far_raw), channel_id=1, source_target_pairs={{0,4},{4,0},{8,12},{12,8},{16,20},{20,16},{24,28},{28,24},{1,5},{5... | collective-permute-start | bytes 1572872 | tf_op jit(solution)/shard_map/ppermute | solution.py:425
  2.7 2.6 %collective-permute-start.1 = (f32[472,128]{1,0:T(8,128)S(1)}, f32[472,128]{1,0:T(8,128)S(1)}, u32[]{:S(2)}, u32[]{:S(2)}) collective-permute-start(f32[472,128]{1,0:T(8,128)S(1)} %get-tuple-element.47), channel_id=1, source_target_pairs={{0,1},{1,0},{2,3},{3,2},{4,8},{5,9},{6,10},{7,11},{8,4},{9,5},{10,... | collective-permute-start | bytes 725000 | tf_op jit(solution)/shard_map/ppermute | solution.py:435
  5.3 0.0 collective-permute-done.halo_raw
  5.3 3.0 %first_step.1 = (f32[2,4,64,128]{3,2,1,0:T(8,128)S(1)}, f32[2,4,64,128]{3,2,1,0:T(8,128)S(1)}, f32[4,64,128]{2,1,0:T(8,128)S(1)}, f32[4,4,64,128]{3,2,1,0:T(8,12...) custom-call(s32[2]{0:T(128)S(1)} %get-tuple-element.34.sy, ...), custom_call_target="tpu_custom_call" | custom-call | flops 16777216 | bytes 33554432 | tf_op jit(solution)/shard_map/first_step/pallas_call | solution.py:498
  8.4 0.1 collective-permute-start.3
  8.5 0.5 %collective-permute-start.4 = (f32[2,4,64,128]{3,2,1,0:T(8,128)S(1)}, f32[2,4,64,128]{3,2,1,0:T(8,128)S(1)}, u32[]{:S(2)}, u32[]{:S(2)}) collective-permute-start(f32[2,4,64,128]{3,2,1,0:T(8,128)S(1)} %get-tuple-element.51.far_rcv), channel_id=1, source_target_pairs={{0,4},{4,0},{8,12},{12,8},{16,20},{20,16},{24,28},{28,24},{1,5},{5... | collective-permute-start | bytes 786440 | tf_op jit(solution)/shard_map/ppermute | solution.py:425
  8.9 0.5 %collective-permute-done.1.halo = f32[472,128]{1,0:T(8,128)S(1)} collective-permute-done((f32[472,128]{1,0:T(8,128)S(1)}, f32[472,128]{1,0:T(8,128)S(1)}, u32[]{:S(2)}, u32[]{:S(2)}) %collective-permute-start.1) | collective-permute-done | bytes 241696 | tf_op jit(solution)/shard_map/ppermute | solution.py:435
  9.5 0.5 %first_step_near.1 = (f32[4,4,72,128]{3,2,1,0:T(8,128)S(1)}, f32[4,64,128]{2,1,0:T(8,128)S(1)}, f32[472,128]{1,0:T(8,128)S(1)}) custom-call(s32[2]{0:T(128)S(1)} %get-tuple-element.34.sy, s32[2]{0:T(128)S(1)} %get-tuple-element.35.sx, s32[2]{0:T(128)S(1)} %get-tuple-element.36.hy, s32[2]{0:T(128)S(1)} %get-tuple-element.37.hx, ...), custom_call_target="tpu_custom_call" | custom-call | flops 2097152 | bytes 67108864 | tf_op jit(solution)/shard_map/first_step_near/pallas_call | solution.py:510
  10.0 2.1 %collective-permute-start.2 = (f32[472,128]{1,0:T(8,128)S(1)}, f32[472,128]{1,0:T(8,128)S(1)}, u32[]{:S(2)}, u32[]{:S(2)}) collective-permute-start(f32[472,128]{1,0:T(8,128)S(1)} %get-tuple-element.56), channel_id=1, source_target_pairs={{0,1},{1,0},{2,3},{3,2},{4,8},{5,9},{6,10},{7,11},{8,4},{9,5},{10,... | collective-permute-start | bytes 725000 | tf_op jit(solution)/shard_map/ppermute | solution.py:435
  12.1 0.0 collective-permute-done.3.halo_src
  12.1 0.0 collective-permute-done.4.halo_rcv
  12.1 1.4 %second_step_far.1 = (f32[4,4,64,128]{3,2,1,0:T(8,128)S(1)}, f32[272,128]{1,0:T(8,128)S(1)}) custom-call(s32[2]{0:T(128)S(1)} %get-tuple-element.34.sy, s32[2]{0:T(128)S(1)} %get-tuple-element.35.sx, s32[2]{0:T(128)S(1)} %get-tuple-element.36.hy, s32[2]{0:T(128)S(1)} %get-tuple-element.37.hx, s32[2]{0:T(128)S(1)} %get-tuple-element.38.depth, ...), custom_call_target="tpu_custom_call" | custom-call | flops 8388608 | bytes 16777216 | tf_op jit(solution)/shard_map/second_step_far/pallas_call | solution.py:522
  13.4 2.5 %collective-permute-start.7 = (f32[272,128]{1,0:T(8,128)S(1)}, f32[272,128]{1,0:T(8,128)S(1)}, u32[]{:S(2)}, u32[]{:S(2)}) collective-permute-start(f32[272,128]{1,0:T(8,128)S(1)} %get-tuple-element.64), channel_id=1, source_target_pairs={{0,3},{1,2},{2,1},{3,0},{4,7},{5,6},{6,5},{7,4},{8,11},{9,10},{10,... | collective-permute-start | bytes 417800 | tf_op jit(solution)/shard_map/ppermute | solution.py:445
  16.0 1.0 %second_step_part.1 = (f32[4,4,64,128]{3,2,1,0:T(8,128)S(1)}, f32[2,4,64,128]{3,2,1,0:T(8,128)S(1)}) custom-call(s32[2]{0:T(128)S(1)} %get-tuple-element.34.sy, s32[2]{0:T(128)S(1)} %get-tuple-element.35.sx, s32[2]{0:T(128)S(1)} %get-tuple-element.38.depth, f32[2,2]{1,0:T(2,128)S(1)} %get-tuple-element.39.wave, ...), custom_call_target="tpu_custom_call" | custom-call | flops 8388608 | bytes 16777216 | tf_op jit(solution)/shard_map/second_step_part/pallas_call | solution.py:535
  17.0 0.0 collective-permute-done.2.halo
  17.0 0.3 %second_step_near.1 = (f32[4,64,128]{2,1,0:T(8,128)S(1)}, f32[4,4,64,128]{3,2,1,0:T(8,128)S(1)}) custom-call(s32[2]{0:T(128)S(1)} %get-tuple-element.34.sy, s32[2]{0:T(128)S(1)} %get-tuple-element.35.sx, s32[2]{0:T(128)S(1)} %get-tuple-element.36.hy, s32[2]{0:T(128)S(1)} %get-tuple-element.37.hx, f32[4,4,64,128]{3,2,1,0:T(8,128)S(1)} %get-tuple-element.54.part, ...), custom_call_target="tpu_custom_call" | custom-call | flops 2097152 | bytes 2097152 | tf_op jit(solution)/shard_map/second_step_near/pallas_call | solution.py:546
  17.3 1.3 %collective-permute-start.5 = (f32[4,64,128]{2,1,0:T(8,128)S(1)}, f32[4,64,128]{2,1,0:T(8,128)S(1)}, u32[]{:S(2)}, u32[]{:S(2)}) collective-permute-start(f32[4,64,128]{2,1,0:T(8,128)S(1)} %get-tuple-element.63), channel_id=1, source_target_pairs={{0,1},{1,0},{2,3},{3,2},{4,7},{5,6},{6,5},{7,4},{8,9},{9,8},{10,11... | collective-permute-start | bytes 393224 | tf_op jit(solution)/shard_map/ppermute | solution.py:445
  18.6 3.2 %collective-permute-done.7 = f32[272,128]{1,0:T(8,128)S(1)} collective-permute-done((f32[272,128]{1,0:T(8,128)S(1)}, f32[272,128]{1,0:T(8,128)S(1)}, u32[]{:S(2)}, u32[]{:S(2)}) %collective-permute-start.7) | collective-permute-done | bytes 139296 | tf_op jit(solution)/shard_map/ppermute | solution.py:445
  21.9 2.3 %collective-permute-start.8 = (f32[272,128]{1,0:T(8,128)S(1)}, f32[272,128]{1,0:T(8,128)S(1)}, u32[]{:S(2)}, u32[]{:S(2)}) collective-permute-start(f32[272,128]{1,0:T(8,128)S(1)} %add.7.far_a), channel_id=1, source_target_pairs={{0,1},{1,0},{2,3},{3,2},{4,5},{5,4},{6,7},{7,6},{8,9},{9,8},{10,11... | collective-permute-start | bytes 417800 | tf_op jit(solution)/shard_map/ppermute | solution.py:445
  24.2 0.0 collective-permute-done.5
  24.2 2.6 %collective-permute-start.6 = (f32[4,64,128]{2,1,0:T(8,128)S(1)}, f32[4,64,128]{2,1,0:T(8,128)S(1)}, u32[]{:S(2)}, u32[]{:S(2)}) collective-permute-start(f32[4,64,128]{2,1,0:T(8,128)S(1)} %add.6.near_a), channel_id=1, source_target_pairs={{0,3},{1,2},{2,1},{3,0},{4,5},{5,4},{6,7},{7,6},{8,11},{9,10},{10,... | collective-permute-start | bytes 393224 | tf_op jit(solution)/shard_map/ppermute | solution.py:445
  26.9 1.0 %write_fields.1 = (f32[2,8,64,128]{3,2,1,0:T(8,128)}, f32[2,8,64,128]{3,2,1,0:T(8,128)}) custom-call(f32[4,4,64,128]{3,2,1,0:T(8,128)S(1)} %get-tuple-element.58.new_near, f32[4,4,64,128]{3,2,1,0:T(8,128)S(1)} %get-tuple-element.60.new_far), custom_call_target="tpu_custom_call" | custom-call | flops 1024 | bytes 4194304 | tf_op jit(solution)/shard_map/write_fields/pallas_call | solution.py:562
  27.9 4.7 %collective-permute-done.6.near_b = f32[4,64,128]{2,1,0:T(8,128)S(1)} collective-permute-done((f32[4,64,128]{2,1,0:T(8,128)S(1)}, f32[4,64,128]{2,1,0:T(8,128)S(1)}, u32[]{:S(2)}, u32[]{:S(2)}) %collective-permute-start.6) | collective-permute-done | bytes 131104 | tf_op jit(solution)/shard_map/ppermute | solution.py:445
  32.6 0.0 collective-permute-done.8.far_b
  32.6 0.7 %image_sum.1 = f32[8,64,128]{2,1,0:T(8,128)} custom-call(f32[4,64,128]{2,1,0:T(8,128)S(1)} %add.6.near_a, f32[4,64,128]{2,1,0:T(8,128)S(1)} %collective-permute-done.6.near_b, f32[272,128]{1,0:T(8,128)S(1)} %add.7.far_a, f32[272,128]{1,0:T(8,128)S(1)} %collective-permute-done.8.far_b), custom_call_target="tpu_custom_call" | custom-call | flops 131072 | bytes 1048576 | tf_op jit(solution)/shard_map/image_sum/pallas_call | solution.py:573
  (2 shorter events, 0.0 us)
Async XLA Ops:
  2.2 3.2 %collective-permute-start = (f32[4,4,64,128]{3,2,1,0:T(8,128)S(1)}, f32[4,4,64,128]{3,2,1,0:T(8,128)S(1)}, u32[]{:S(2)}, u32[]{:S(2)}) collective-permute-start(f32[4,4,64,128]{3,2,1,0:T(8,128)S(1)} %get-tuple-element.43.far_raw), channel_id=1, source_target_pairs={{0,4},{4,0},{8,12},{12,8},{16,20},{20,16},{24,28},{28,24},{1,5},{5... | collective-permute-start | bytes 1572872 | tf_op jit(solution)/shard_map/ppermute | solution.py:425
  2.7 6.8 %collective-permute-start.1 = (f32[472,128]{1,0:T(8,128)S(1)}, f32[472,128]{1,0:T(8,128)S(1)}, u32[]{:S(2)}, u32[]{:S(2)}) collective-permute-start(f32[472,128]{1,0:T(8,128)S(1)} %get-tuple-element.47), channel_id=1, source_target_pairs={{0,1},{1,0},{2,3},{3,2},{4,8},{5,9},{6,10},{7,11},{8,4},{9,5},{10,... | collective-permute-start | bytes 725000 | tf_op jit(solution)/shard_map/ppermute | solution.py:435
  8.4 3.7 %collective-permute-start.3 = (f32[2,4,64,128]{3,2,1,0:T(8,128)S(1)}, f32[2,4,64,128]{3,2,1,0:T(8,128)S(1)}, u32[]{:S(2)}, u32[]{:S(2)}) collective-permute-start(f32[2,4,64,128]{3,2,1,0:T(8,128)S(1)} %get-tuple-element.50.far_src), channel_id=1, source_target_pairs={{0,4},{4,0},{8,12},{12,8},{16,20},{20,16},{24,28},{28,24},{1,5},{5... | collective-permute-start | bytes 786440 | tf_op jit(solution)/shard_map/ppermute | solution.py:425
  8.5 3.6 %collective-permute-start.4 = (f32[2,4,64,128]{3,2,1,0:T(8,128)S(1)}, f32[2,4,64,128]{3,2,1,0:T(8,128)S(1)}, u32[]{:S(2)}, u32[]{:S(2)}) collective-permute-start(f32[2,4,64,128]{3,2,1,0:T(8,128)S(1)} %get-tuple-element.51.far_rcv), channel_id=1, source_target_pairs={{0,4},{4,0},{8,12},{12,8},{16,20},{20,16},{24,28},{28,24},{1,5},{5... | collective-permute-start | bytes 786440 | tf_op jit(solution)/shard_map/ppermute | solution.py:425
  10.0 7.0 %collective-permute-start.2 = (f32[472,128]{1,0:T(8,128)S(1)}, f32[472,128]{1,0:T(8,128)S(1)}, u32[]{:S(2)}, u32[]{:S(2)}) collective-permute-start(f32[472,128]{1,0:T(8,128)S(1)} %get-tuple-element.56), channel_id=1, source_target_pairs={{0,1},{1,0},{2,3},{3,2},{4,8},{5,9},{6,10},{7,11},{8,4},{9,5},{10,... | collective-permute-start | bytes 725000 | tf_op jit(solution)/shard_map/ppermute | solution.py:435
  13.4 8.4 %collective-permute-start.7 = (f32[272,128]{1,0:T(8,128)S(1)}, f32[272,128]{1,0:T(8,128)S(1)}, u32[]{:S(2)}, u32[]{:S(2)}) collective-permute-start(f32[272,128]{1,0:T(8,128)S(1)} %get-tuple-element.64), channel_id=1, source_target_pairs={{0,3},{1,2},{2,1},{3,0},{4,7},{5,6},{6,5},{7,4},{8,11},{9,10},{10,... | collective-permute-start | bytes 417800 | tf_op jit(solution)/shard_map/ppermute | solution.py:445
  17.3 6.9 %collective-permute-start.5 = (f32[4,64,128]{2,1,0:T(8,128)S(1)}, f32[4,64,128]{2,1,0:T(8,128)S(1)}, u32[]{:S(2)}, u32[]{:S(2)}) collective-permute-start(f32[4,64,128]{2,1,0:T(8,128)S(1)} %get-tuple-element.63), channel_id=1, source_target_pairs={{0,1},{1,0},{2,3},{3,2},{4,7},{5,6},{6,5},{7,4},{8,9},{9,8},{10,11... | collective-permute-start | bytes 393224 | tf_op jit(solution)/shard_map/ppermute | solution.py:445
  21.9 10.7 %collective-permute-start.8 = (f32[272,128]{1,0:T(8,128)S(1)}, f32[272,128]{1,0:T(8,128)S(1)}, u32[]{:S(2)}, u32[]{:S(2)}) collective-permute-start(f32[272,128]{1,0:T(8,128)S(1)} %add.7.far_a), channel_id=1, source_target_pairs={{0,1},{1,0},{2,3},{3,2},{4,5},{5,4},{6,7},{7,6},{8,9},{9,8},{10,11... | collective-permute-start | bytes 417800 | tf_op jit(solution)/shard_map/ppermute | solution.py:445
  24.2 8.3 %collective-permute-start.6 = (f32[4,64,128]{2,1,0:T(8,128)S(1)}, f32[4,64,128]{2,1,0:T(8,128)S(1)}, u32[]{:S(2)}, u32[]{:S(2)}) collective-permute-start(f32[4,64,128]{2,1,0:T(8,128)S(1)} %add.6.near_a), channel_id=1, source_target_pairs={{0,3},{1,2},{2,1},{3,0},{4,5},{5,4},{6,7},{7,6},{8,11},{9,10},{10,... | collective-permute-start | bytes 393224 | tf_op jit(solution)/shard_map/ppermute | solution.py:445

commit v6 on v5

--- a/solution.py
+++ b/solution.py
@@ -13,7 +13,8 @@
 HALF_Y, HALF_X = 21, 42
 WIN_Y, WIN_X = 2 * HALF_Y + 1, 2 * HALF_X + 1
 PACK = 29
-TAIL = 8
+LAST = 4 * R - 1
+SHIFT = 3
 REST = WIN_Y - PACK
 SCALE = 5040.0
 MARGIN = 8
@@ -70,13 +71,16 @@
 
 
 def pack_field(planes, f, out, scal, par):
-    if f == 0:
-        out[4 * R * PACK :] = jnp.zeros((TAIL, out.shape[1]), jnp.float32)
     row0 = scal[0][f % 2] - HALF_Y
     col0 = scal[1][f % 2] - HALF_X
-    for d in range(R):
+    for d in reversed(range(R)):
         i = d + par * (R - 1 - 2 * d)
-        out[pl.ds((f * R + d) * PACK, PACK), :] = pack(planes, f, i, row0, col0)[:PACK]
+        n = f * R + d
+        block = pack(planes, f, i, row0, col0)
+        if n == LAST:
+            out[LAST * PACK - SHIFT :] = pltpu.roll(block, SHIFT, 0)
+        else:
+            out[pl.ds(n * PACK, PACK), :] = block[:PACK]
 
 
 def unpack_planes(packed, planes, scal):
@@ -85,10 +89,20 @@
         row0 = scal[0][f % 2] - HALF_Y
         col0 = scal[1][f % 2] - HALF_X
         for e in range(R):
-            n = (f * R + e) * PACK
-            planes[f, e, pl.ds(row0, PACK), :] = packed[pl.ds(n, PACK), :]
-            left = pltpu.roll(packed[pl.ds(n, REST), :], cols - WIN_X, 1)
-            right = pltpu.roll(packed[pl.ds(n + REST, REST), :], cols - HALF_X, 1)
+            n = f * R + e
+            if n == LAST:
+                block = packed[LAST * PACK - SHIFT :]
+                rows = block.shape[0]
+                main = pltpu.roll(block, rows - SHIFT, 0)[:PACK]
+                left = main[:REST]
+                right = pltpu.roll(block, rows - SHIFT - REST, 0)[:REST]
+            else:
+                main = packed[pl.ds(n * PACK, PACK), :]
+                left = packed[pl.ds(n * PACK, REST), :]
+                right = packed[pl.ds(n * PACK + REST, REST), :]
+            planes[f, e, pl.ds(row0, PACK), :] = main
+            left = pltpu.roll(left, cols - WIN_X, 1)
+            right = pltpu.roll(right, cols - HALF_X, 1)
             rest = jnp.where(lanes(left.shape) < col0 + (cols - WIN_X), left, right)
             planes[f, e, pl.ds(row0 + PACK, REST), :] = rest
 
@@ -413,11 +427,18 @@
     ], sems))
 
 
-def image_kernel(near_a, near_b, far_a, far_b, out):
+def image_kernel(near_a, near_b, far_a, far_b, out, sums, sems):
     near, far = halves()
-    out[pl.ds(near, R)] = near_a[...] + near_b[...]
     used = R * out.shape[1]
-    out[pl.ds(far, R)] = (far_a[:used] + far_b[:used]).reshape(R, *out.shape[1:])
+    copies = [
+        pltpu.make_async_copy(sums.at[n], out.at[pl.ds(first, R)], sems.at[n])
+        for n, first in enumerate((far, near))
+    ]
+    sums[0] = (far_a[:used] + far_b[:used]).reshape(R, *out.shape[1:])
+    copies[0].start()
+    sums[1] = near_a[...] + near_b[...]
+    copies[1].start()
+    wait(copies)
 
 
 def swap_a(block):
@@ -474,7 +495,7 @@
     half2 = shape((2, R, rows, cols), f32)
     half1 = shape((R, rows, cols), f32)
     far_block = shape((R * rows + SPARE, cols), f32)
-    packed = shape((4 * R * PACK + TAIL, cols), f32)
+    packed = shape((4 * R * PACK, cols), f32)
     dma = lambda n: pltpu.SemaphoreType.DMA((n,))
     planes = (4, R, rows + MARGIN, cols)
     state = pltpu.VMEM((4, layers + 2 * R, rows + 2 * MARGIN, cols), f32)
@@ -574,7 +595,8 @@
         image_kernel,
         out_shape=shape((layers, rows, cols), f32),
         in_specs=[VMEM] * 4,
-        out_specs=VMEM,
+        out_specs=HBM,
+        scratch_shapes=[pltpu.VMEM((2, R, rows, cols), f32), dma(2)],
         compiler_params=params(),
         cost_estimate=cost(1 << 17, 1 << 20),
         name="image_sum",

time: 33.5 us -> 33.4 us (level)
  no operation moved by 1% of the time
where the time goes in v6:
time: 33.4 us; the launch traced here: 33.2 us
  starting transfers between devices  14.6 us (44%)
  Pallas kernels  9.45 us (28%)
  waiting for transfers between devices  8.39 us (25%)
  between operations  0.71 us (2%)
    ppermute x4, starting transfers between devices, swap_shots(): return lax.ppermute(block, ('slab', 'shots'), pairs)  8.79 us
    ppermute x4, waiting for transfers between devices, swap_shots(): return lax.ppermute(block, ('slab', 'shots'), pairs)  7.9 us
    ppermute x2, starting transfers between devices, swap_b(): return lax.ppermute(block, ('slab', 'shots'), pairs)  4.73 us
    pallas_call x1, Pallas kernels, per_device(): pl.pallas_call(first_kernel, out_shape=(half2, half2, half1, half4, half2...  3.02 us
    pallas_call x1, Pallas kernels, per_device(): pl.pallas_call(pack_kernel, out_shape=(packed, *(shape(x.shape, x.dtype)...  1.52 us
    pallas_call x1, Pallas kernels, per_device(): pl.pallas_call(second_far_kernel, out_shape=(half4, far_block), in_specs=...  1.36 us
    ppermute x3, starting transfers between devices, swap_a(): return lax.ppermute(block, 'slab', [(i, i ^ 1) for i in range(count)])  1.09 us
    pallas_call x1, Pallas kernels, per_device(): pl.pallas_call(write_kernel, out_shape=(shape(src_cur.shape, f32),) * 2,...  0.99 us
  transfers between devices with their start and end apart: 9, of which 3 were waited for; matrix products, arithmetic and copies ran while one was open for 0% of the time, Pallas kernels for 22%

profile of v6, /device:TPU:0, one launch (start us, length us, event | category | flops | bytes accessed | tf_op | source)
XLA Modules:
  0.0 33.2 jit_solution(4326554150386709161)
XLA Ops:
  0.6 1.5 %pack_halo.1 = (f32[464,128]{1,0:T(8,128)S(1)}, s32[2]{0:T(128)S(1)}, s32[2]{0:T(128)S(1)}, s32[2]{0:T(128)S(1)}, s32[2]{0:T(128)S(1)}, /*index=5*/s32[2]{0:T(12...) custom-call(s32[2]{0:T(128)} %refs_0_.1, ...), custom_call_target="tpu_custom_call" | custom-call | flops 1048576 | bytes 1048576 | tf_op jit(solution)/shard_map/pack_halo/pallas_call | solution.py:505
  2.2 0.5 %collective-permute-start = (f32[4,4,64,128]{3,2,1,0:T(8,128)S(1)}, f32[4,4,64,128]{3,2,1,0:T(8,128)S(1)}, u32[]{:S(2)}, u32[]{:S(2)}) collective-permute-start(f32[4,4,64,128]{3,2,1,0:T(8,128)S(1)} %get-tuple-element.43.far_raw), channel_id=1, source_target_pairs={{0,4},{4,0},{8,12},{12,8},{16,20},{20,16},{24,28},{28,24},{1,5},{5... | collective-permute-start | bytes 1572872 | tf_op jit(solution)/shard_map/ppermute | solution.py:446
  2.7 2.6 %collective-permute-start.1 = (f32[464,128]{1,0:T(8,128)S(1)}, f32[464,128]{1,0:T(8,128)S(1)}, u32[]{:S(2)}, u32[]{:S(2)}) collective-permute-start(f32[464,128]{1,0:T(8,128)S(1)} %get-tuple-element.47), channel_id=1, source_target_pairs={{0,1},{1,0},{2,3},{3,2},{4,8},{5,9},{6,10},{7,11},{8,4},{9,5},{10,... | collective-permute-start | bytes 712712 | tf_op jit(solution)/shard_map/ppermute | solution.py:456
  5.3 0.0 collective-permute-done.halo_raw
  5.3 3.0 %first_step.1 = (f32[2,4,64,128]{3,2,1,0:T(8,128)S(1)}, f32[2,4,64,128]{3,2,1,0:T(8,128)S(1)}, f32[4,64,128]{2,1,0:T(8,128)S(1)}, f32[4,4,64,128]{3,2,1,0:T(8,12...) custom-call(s32[2]{0:T(128)S(1)} %get-tuple-element.34.sy, ...), custom_call_target="tpu_custom_call" | custom-call | flops 16777216 | bytes 33554432 | tf_op jit(solution)/shard_map/first_step/pallas_call | solution.py:519
  8.4 0.1 collective-permute-start.3
  8.5 0.5 %collective-permute-start.4 = (f32[2,4,64,128]{3,2,1,0:T(8,128)S(1)}, f32[2,4,64,128]{3,2,1,0:T(8,128)S(1)}, u32[]{:S(2)}, u32[]{:S(2)}) collective-permute-start(f32[2,4,64,128]{3,2,1,0:T(8,128)S(1)} %get-tuple-element.51.far_rcv), channel_id=1, source_target_pairs={{0,4},{4,0},{8,12},{12,8},{16,20},{20,16},{24,28},{28,24},{1,5},{5... | collective-permute-start | bytes 786440 | tf_op jit(solution)/shard_map/ppermute | solution.py:446
  8.9 0.5 %collective-permute-done.1.halo = f32[464,128]{1,0:T(8,128)S(1)} collective-permute-done((f32[464,128]{1,0:T(8,128)S(1)}, f32[464,128]{1,0:T(8,128)S(1)}, u32[]{:S(2)}, u32[]{:S(2)}) %collective-permute-start.1) | collective-permute-done | bytes 237600 | tf_op jit(solution)/shard_map/ppermute | solution.py:456
  9.4 0.5 %first_step_near.1 = (f32[4,4,72,128]{3,2,1,0:T(8,128)S(1)}, f32[4,64,128]{2,1,0:T(8,128)S(1)}, f32[464,128]{1,0:T(8,128)S(1)}) custom-call(s32[2]{0:T(128)S(1)} %get-tuple-element.34.sy, s32[2]{0:T(128)S(1)} %get-tuple-element.35.sx, s32[2]{0:T(128)S(1)} %get-tuple-element.36.hy, s32[2]{0:T(128)S(1)} %get-tuple-element.37.hx, ...), custom_call_target="tpu_custom_call" | custom-call | flops 2097152 | bytes 67108864 | tf_op jit(solution)/shard_map/first_step_near/pallas_call | solution.py:531
  9.9 2.1 %collective-permute-start.2 = (f32[464,128]{1,0:T(8,128)S(1)}, f32[464,128]{1,0:T(8,128)S(1)}, u32[]{:S(2)}, u32[]{:S(2)}) collective-permute-start(f32[464,128]{1,0:T(8,128)S(1)} %get-tuple-element.56), channel_id=1, source_target_pairs={{0,1},{1,0},{2,3},{3,2},{4,8},{5,9},{6,10},{7,11},{8,4},{9,5},{10,... | collective-permute-start | bytes 712712 | tf_op jit(solution)/shard_map/ppermute | solution.py:456
  12.0 0.0 collective-permute-done.3.halo_src
  12.0 0.0 collective-permute-done.4.halo_rcv
  12.0 1.4 %second_step_far.1 = (f32[4,4,64,128]{3,2,1,0:T(8,128)S(1)}, f32[272,128]{1,0:T(8,128)S(1)}) custom-call(s32[2]{0:T(128)S(1)} %get-tuple-element.34.sy, s32[2]{0:T(128)S(1)} %get-tuple-element.35.sx, s32[2]{0:T(128)S(1)} %get-tuple-element.36.hy, s32[2]{0:T(128)S(1)} %get-tuple-element.37.hx, s32[2]{0:T(128)S(1)} %get-tuple-element.38.depth, ...), custom_call_target="tpu_custom_call" | custom-call | flops 8388608 | bytes 16777216 | tf_op jit(solution)/shard_map/second_step_far/pallas_call | solution.py:543
  13.4 2.5 %collective-permute-start.7 = (f32[272,128]{1,0:T(8,128)S(1)}, f32[272,128]{1,0:T(8,128)S(1)}, u32[]{:S(2)}, u32[]{:S(2)}) collective-permute-start(f32[272,128]{1,0:T(8,128)S(1)} %get-tuple-element.64), channel_id=1, source_target_pairs={{0,3},{1,2},{2,1},{3,0},{4,7},{5,6},{6,5},{7,4},{8,11},{9,10},{10,... | collective-permute-start | bytes 417800 | tf_op jit(solution)/shard_map/ppermute | solution.py:466
  15.9 1.0 %second_step_part.1 = (f32[4,4,64,128]{3,2,1,0:T(8,128)S(1)}, f32[2,4,64,128]{3,2,1,0:T(8,128)S(1)}) custom-call(s32[2]{0:T(128)S(1)} %get-tuple-element.34.sy, s32[2]{0:T(128)S(1)} %get-tuple-element.35.sx, s32[2]{0:T(128)S(1)} %get-tuple-element.38.depth, f32[2,2]{1,0:T(2,128)S(1)} %get-tuple-element.39.wave, ...), custom_call_target="tpu_custom_call" | custom-call | flops 8388608 | bytes 16777216 | tf_op jit(solution)/shard_map/second_step_part/pallas_call | solution.py:556
  16.9 0.0 collective-permute-done.2.halo
  16.9 0.3 %second_step_near.1 = (f32[4,64,128]{2,1,0:T(8,128)S(1)}, f32[4,4,64,128]{3,2,1,0:T(8,128)S(1)}) custom-call(s32[2]{0:T(128)S(1)} %get-tuple-element.34.sy, s32[2]{0:T(128)S(1)} %get-tuple-element.35.sx, s32[2]{0:T(128)S(1)} %get-tuple-element.36.hy, s32[2]{0:T(128)S(1)} %get-tuple-element.37.hx, f32[4,4,64,128]{3,2,1,0:T(8,128)S(1)} %get-tuple-element.54.part, ...), custom_call_target="tpu_custom_call" | custom-call | flops 2097152 | bytes 2097152 | tf_op jit(solution)/shard_map/second_step_near/pallas_call | solution.py:567
  17.3 1.3 %collective-permute-start.5 = (f32[4,64,128]{2,1,0:T(8,128)S(1)}, f32[4,64,128]{2,1,0:T(8,128)S(1)}, u32[]{:S(2)}, u32[]{:S(2)}) collective-permute-start(f32[4,64,128]{2,1,0:T(8,128)S(1)} %get-tuple-element.63), channel_id=1, source_target_pairs={{0,1},{1,0},{2,3},{3,2},{4,7},{5,6},{6,5},{7,4},{8,9},{9,8},{10,11... | collective-permute-start | bytes 393224 | tf_op jit(solution)/shard_map/ppermute | solution.py:466
  18.5 3.2 %collective-permute-done.7 = f32[272,128]{1,0:T(8,128)S(1)} collective-permute-done((f32[272,128]{1,0:T(8,128)S(1)}, f32[272,128]{1,0:T(8,128)S(1)}, u32[]{:S(2)}, u32[]{:S(2)}) %collective-permute-start.7) | collective-permute-done | bytes 139296 | tf_op jit(solution)/shard_map/ppermute | solution.py:466
  21.8 2.4 %collective-permute-start.8 = (f32[272,128]{1,0:T(8,128)S(1)}, f32[272,128]{1,0:T(8,128)S(1)}, u32[]{:S(2)}, u32[]{:S(2)}) collective-permute-start(f32[272,128]{1,0:T(8,128)S(1)} %add.7.far_a), channel_id=1, source_target_pairs={{0,1},{1,0},{2,3},{3,2},{4,5},{5,4},{6,7},{7,6},{8,9},{9,8},{10,11... | collective-permute-start | bytes 417800 | tf_op jit(solution)/shard_map/ppermute | solution.py:466
  24.2 0.0 collective-permute-done.5
  24.2 2.6 %collective-permute-start.6 = (f32[4,64,128]{2,1,0:T(8,128)S(1)}, f32[4,64,128]{2,1,0:T(8,128)S(1)}, u32[]{:S(2)}, u32[]{:S(2)}) collective-permute-start(f32[4,64,128]{2,1,0:T(8,128)S(1)} %add.6.near_a), channel_id=1, source_target_pairs={{0,3},{1,2},{2,1},{3,0},{4,5},{5,4},{6,7},{7,6},{8,11},{9,10},{10,... | collective-permute-start | bytes 393224 | tf_op jit(solution)/shard_map/ppermute | solution.py:466
  26.8 1.0 %write_fields.1 = (f32[2,8,64,128]{3,2,1,0:T(8,128)}, f32[2,8,64,128]{3,2,1,0:T(8,128)}) custom-call(f32[4,4,64,128]{3,2,1,0:T(8,128)S(1)} %get-tuple-element.58.new_near, f32[4,4,64,128]{3,2,1,0:T(8,128)S(1)} %get-tuple-element.60.new_far), custom_call_target="tpu_custom_call" | custom-call | flops 1024 | bytes 4194304 | tf_op jit(solution)/shard_map/write_fields/pallas_call | solution.py:583
  27.8 4.7 %collective-permute-done.6.near_b = f32[4,64,128]{2,1,0:T(8,128)S(1)} collective-permute-done((f32[4,64,128]{2,1,0:T(8,128)S(1)}, f32[4,64,128]{2,1,0:T(8,128)S(1)}, u32[]{:S(2)}, u32[]{:S(2)}) %collective-permute-start.6) | collective-permute-done | bytes 131104 | tf_op jit(solution)/shard_map/ppermute | solution.py:466
  32.5 0.0 collective-permute-done.8.far_b
  32.5 0.7 %image_sum.1 = f32[8,64,128]{2,1,0:T(8,128)} custom-call(f32[4,64,128]{2,1,0:T(8,128)S(1)} %add.6.near_a, f32[4,64,128]{2,1,0:T(8,128)S(1)} %collective-permute-done.6.near_b, f32[272,128]{1,0:T(8,128)S(1)} %add.7.far_a, f32[272,128]{1,0:T(8,128)S(1)} %collective-permute-done.8.far_b), custom_call_target="tpu_custom_call" | custom-call | flops 131072 | bytes 1048576 | tf_op jit(solution)/shard_map/image_sum/pallas_call | solution.py:594
  (2 shorter events, 0.0 us)
Async XLA Ops:
  2.2 3.2 %collective-permute-start = (f32[4,4,64,128]{3,2,1,0:T(8,128)S(1)}, f32[4,4,64,128]{3,2,1,0:T(8,128)S(1)}, u32[]{:S(2)}, u32[]{:S(2)}) collective-permute-start(f32[4,4,64,128]{3,2,1,0:T(8,128)S(1)} %get-tuple-element.43.far_raw), channel_id=1, source_target_pairs={{0,4},{4,0},{8,12},{12,8},{16,20},{20,16},{24,28},{28,24},{1,5},{5... | collective-permute-start | bytes 1572872 | tf_op jit(solution)/shard_map/ppermute | solution.py:446
  2.7 6.7 %collective-permute-start.1 = (f32[464,128]{1,0:T(8,128)S(1)}, f32[464,128]{1,0:T(8,128)S(1)}, u32[]{:S(2)}, u32[]{:S(2)}) collective-permute-start(f32[464,128]{1,0:T(8,128)S(1)} %get-tuple-element.47), channel_id=1, source_target_pairs={{0,1},{1,0},{2,3},{3,2},{4,8},{5,9},{6,10},{7,11},{8,4},{9,5},{10,... | collective-permute-start | bytes 712712 | tf_op jit(solution)/shard_map/ppermute | solution.py:456
  8.4 3.7 %collective-permute-start.3 = (f32[2,4,64,128]{3,2,1,0:T(8,128)S(1)}, f32[2,4,64,128]{3,2,1,0:T(8,128)S(1)}, u32[]{:S(2)}, u32[]{:S(2)}) collective-permute-start(f32[2,4,64,128]{3,2,1,0:T(8,128)S(1)} %get-tuple-element.50.far_src), channel_id=1, source_target_pairs={{0,4},{4,0},{8,12},{12,8},{16,20},{20,16},{24,28},{28,24},{1,5},{5... | collective-permute-start | bytes 786440 | tf_op jit(solution)/shard_map/ppermute | solution.py:446
  8.5 3.6 %collective-permute-start.4 = (f32[2,4,64,128]{3,2,1,0:T(8,128)S(1)}, f32[2,4,64,128]{3,2,1,0:T(8,128)S(1)}, u32[]{:S(2)}, u32[]{:S(2)}) collective-permute-start(f32[2,4,64,128]{3,2,1,0:T(8,128)S(1)} %get-tuple-element.51.far_rcv), channel_id=1, source_target_pairs={{0,4},{4,0},{8,12},{12,8},{16,20},{20,16},{24,28},{28,24},{1,5},{5... | collective-permute-start | bytes 786440 | tf_op jit(solution)/shard_map/ppermute | solution.py:446
  9.9 7.0 %collective-permute-start.2 = (f32[464,128]{1,0:T(8,128)S(1)}, f32[464,128]{1,0:T(8,128)S(1)}, u32[]{:S(2)}, u32[]{:S(2)}) collective-permute-start(f32[464,128]{1,0:T(8,128)S(1)} %get-tuple-element.56), channel_id=1, source_target_pairs={{0,1},{1,0},{2,3},{3,2},{4,8},{5,9},{6,10},{7,11},{8,4},{9,5},{10,... | collective-permute-start | bytes 712712 | tf_op jit(solution)/shard_map/ppermute | solution.py:456
  13.4 8.4 %collective-permute-start.7 = (f32[272,128]{1,0:T(8,128)S(1)}, f32[272,128]{1,0:T(8,128)S(1)}, u32[]{:S(2)}, u32[]{:S(2)}) collective-permute-start(f32[272,128]{1,0:T(8,128)S(1)} %get-tuple-element.64), channel_id=1, source_target_pairs={{0,3},{1,2},{2,1},{3,0},{4,7},{5,6},{6,5},{7,4},{8,11},{9,10},{10,... | collective-permute-start | bytes 417800 | tf_op jit(solution)/shard_map/ppermute | solution.py:466
  17.3 6.9 %collective-permute-start.5 = (f32[4,64,128]{2,1,0:T(8,128)S(1)}, f32[4,64,128]{2,1,0:T(8,128)S(1)}, u32[]{:S(2)}, u32[]{:S(2)}) collective-permute-start(f32[4,64,128]{2,1,0:T(8,128)S(1)} %get-tuple-element.63), channel_id=1, source_target_pairs={{0,1},{1,0},{2,3},{3,2},{4,7},{5,6},{6,5},{7,4},{8,9},{9,8},{10,11... | collective-permute-start | bytes 393224 | tf_op jit(solution)/shard_map/ppermute | solution.py:466
  21.8 10.7 %collective-permute-start.8 = (f32[272,128]{1,0:T(8,128)S(1)}, f32[272,128]{1,0:T(8,128)S(1)}, u32[]{:S(2)}, u32[]{:S(2)}) collective-permute-start(f32[272,128]{1,0:T(8,128)S(1)} %add.7.far_a), channel_id=1, source_target_pairs={{0,1},{1,0},{2,3},{3,2},{4,5},{5,4},{6,7},{7,6},{8,9},{9,8},{10,11... | collective-permute-start | bytes 417800 | tf_op jit(solution)/shard_map/ppermute | solution.py:466
  24.2 8.2 %collective-permute-start.6 = (f32[4,64,128]{2,1,0:T(8,128)S(1)}, f32[4,64,128]{2,1,0:T(8,128)S(1)}, u32[]{:S(2)}, u32[]{:S(2)}) collective-permute-start(f32[4,64,128]{2,1,0:T(8,128)S(1)} %add.6.near_a), channel_id=1, source_target_pairs={{0,3},{1,2},{2,1},{3,0},{4,5},{5,4},{6,7},{7,6},{8,11},{9,10},{10,... | collective-permute-start | bytes 393224 | tf_op jit(solution)/shard_map/ppermute | solution.py:466
